TPU v7x, 128 devices: a whole 4x4x4 slice. The times are simulated.
128 devices in a mesh: dp: 32 (over x, z, core), mp: 4 (over y).
Axes of the slice: x: 4, y: 4, z: 4, core: 2. Of those that a mesh axis runs over, the one named last changes fastest.
Arguments:
- hidden_in: bfloat16 [512, 8192], P(None, 'dp'), may hold values from -6 to 6
- gain_attn: float32 [8192], P('dp'), may hold values from 0.1 to 1.9
- w_query: bfloat16 [8192, 8192], P('dp', 'mp'), may hold values from -0.0625 to 0.0625
- w_keyval: bfloat16 [8192, 2, 1024], P('dp', None, 'mp'), may hold values from -0.0625 to 0.0625
- w_out: bfloat16 [8192, 8192], P(None, 'dp'), may hold values from -0.0625 to 0.0625
- key_cache: bfloat16 [512, 8, 192, 128], P('dp', 'mp'), may hold values from -210 to 210
- value_cache: bfloat16 [512, 8, 192, 128], P('dp', 'mp'), may hold values from -6 to 6
- lengths: int32 [512], P('dp'), may hold values from 2 to 192, as said below
- gain_final: float32 [8192], P('dp'), may hold values from 0.1 to 1.9
- w_vocab: bfloat16 [8192, 128256], P(None, ('dp', 'mp')), may hold values from -2.32019413 to 2.32019413
- pair_rows: int32 [512], replicated, may hold values from 0 to 511, each once
- grammar: int32 [256, 8064], P(None, ('dp', 'mp')), may hold values from 0 to 65535, as said below
Outputs:
- logprobs: float32 [256, 128256], P(None, ('dp', 'mp'))
Inputs may be any that keep to these rules, and one draw needn't show every extreme that they name: `lengths`: every draw has a row of exactly 192 cached positions. `grammar`: bits past 1002 in a device's last word are ignored. `pair_rows`: each row appears exactly once.
All inputs are finite; a program needn't handle non-finite values.
Results may differ from a plain program's by a relative error of at most 0.0065.
Values may be sent and summed in bfloat16 or wider, within the bound.
No kernel may reach another device: no remote copies, remote signals or barrier semaphores. Data moves between devices by JAX's collectives and lax.ppermute only.
A program may use at most 128 MiB of HBM per device.

v0:
```python
import jax
import jax.numpy as jnp
from jax import lax
from jax.sharding import PartitionSpec as P

D = 8192
HD = 128


GUIDANCE = 3.0
ROPE_BASE = 500000.0
EPSILON = 1e-05
SENTINEL = -1e30


def combined_all(value, axis, join):
    pieces = jax.tree.map(lambda part: lax.all_gather(part, axis), value)
    head = jax.tree.map(lambda part: part[0], pieces)
    tail = jax.tree.map(lambda part: part[1:], pieces)
    running, _ = lax.scan(lambda running, share: (join(running, share), None), head, tail)
    return running


def rotate(values, positions):
    halves = values.shape[-1] // 2
    frequency = ROPE_BASE ** (-2.0 * jnp.arange(halves, dtype=jnp.float32) / values.shape[-1])
    angles = positions.astype(jnp.float32)[:, None] * frequency[None, :]
    cosine = jnp.cos(angles)[:, None, :]
    sin_part = jnp.sin(angles)[:, None, :]
    leading = values[..., :halves]
    trailing = values[..., halves:]
    return jnp.concatenate(
        [leading * cosine - trailing * sin_part, trailing * cosine + leading * sin_part], -1
    )


def normalize(stream, gain_vec):
    values = stream.astype(jnp.float32)
    squares = lax.psum(jnp.sum(values * values, 1), "dp")
    return (values * lax.rsqrt(squares / D + EPSILON)[:, None] * gain_vec[None, :]).astype(
        jnp.bfloat16
    )


def unpack(packed, offset, count):
    shifts = jnp.arange(16, dtype=jnp.int32)
    bit_value = jnp.right_shift(packed[:, :, None], shifts[None, None, :]) & 1
    flat_bits = bit_value.reshape(packed.shape[0], -1)[:, :count]
    offsets = jnp.arange(count, dtype=jnp.int32)
    return (flat_bits == 1) | (offset + offsets == 0)[None, :]


def attend(queries, new_key, new_value, key_cache, value_cache, lengths):
    rows, groups = (key_cache.shape[0], key_cache.shape[1])
    group_size = queries.shape[1] // groups
    scaling = queries.shape[2] ** (-0.5)
    grouped = queries.reshape(rows, groups, group_size, -1)
    scores = (
        jnp.einsum("rgqd,rgld->rgql", grouped, key_cache, preferred_element_type=jnp.float32)
        * scaling
    )
    fresh = (
        jnp.einsum("rgqd,rgd->rgq", grouped, new_key, preferred_element_type=jnp.float32) * scaling
    )
    usable = jnp.arange(key_cache.shape[2], dtype=jnp.int32)[None, :] < lengths[:, None]
    scores = jnp.where(usable[:, None, None, :], scores, SENTINEL)
    highest = jnp.maximum(jnp.max(scores, -1), fresh)
    weights = jnp.where(usable[:, None, None, :], jnp.exp(scores - highest[..., None]), 0.0)
    fresh_weight = jnp.exp(fresh - highest)
    summed = jnp.sum(weights, -1) + fresh_weight
    probs_cache = (weights / summed[..., None]).astype(jnp.bfloat16)
    probs_fresh = (fresh_weight / summed).astype(jnp.bfloat16)
    mixed = jnp.einsum(
        "rgql,rgld->rgqd", probs_cache, value_cache, preferred_element_type=jnp.float32
    )
    mixed = (
        mixed
        + probs_fresh.astype(jnp.float32)[..., None] * new_value.astype(jnp.float32)[:, :, None, :]
    )
    return mixed.reshape(rows, -1).astype(jnp.bfloat16)


def combine(earlier, later):
    highest = jnp.maximum(earlier[0], later[0])
    summed = earlier[1] * jnp.exp(earlier[0] - highest) + later[1] * jnp.exp(later[0] - highest)
    return (highest, summed)


def local(
    hidden_in,
    gain_attn,
    w_query,
    w_keyval,
    w_out,
    key_cache,
    value_cache,
    lengths,
    gain_final,
    w_vocab,
    pair_rows,
    grammar,
):
    local_rows = lengths.shape[0]
    normed = normalize(hidden_in, gain_attn)
    kv_columns = w_keyval.reshape(w_keyval.shape[0], -1)
    projected = lax.psum_scatter(
        jnp.concatenate(
            [
                jnp.dot(normed, w_query, preferred_element_type=jnp.float32),
                jnp.dot(normed, kv_columns, preferred_element_type=jnp.float32),
            ],
            1,
        ),
        "dp",
        scatter_dimension=0,
        tiled=True,
    )
    query_cols = w_query.shape[1]
    group_count = w_keyval.shape[2] // HD
    queries = rotate(
        projected[:, :query_cols].reshape(local_rows, query_cols // HD, HD), lengths
    ).astype(jnp.bfloat16)
    kv_pairs = projected[:, query_cols:].reshape(local_rows, 2, group_count, HD)
    new_key = rotate(kv_pairs[:, 0], lengths).astype(jnp.bfloat16)
    new_value = kv_pairs[:, 1].astype(jnp.bfloat16)
    attended = attend(queries, new_key, new_value, key_cache, value_cache, lengths)
    everyone = lax.all_gather(attended[None], ("dp", "mp"), axis=0, tiled=True)
    blocks = everyone.reshape(lax.axis_size("dp"), lax.axis_size("mp"), local_rows, query_cols)
    weights = w_out.reshape(lax.axis_size("mp"), query_cols, w_out.shape[1])
    update = jnp.einsum(
        "ijrc,jcd->ird", blocks, weights, preferred_element_type=jnp.float32
    ).reshape(-1, w_out.shape[1])
    residual = (hidden_in.astype(jnp.float32) + update).astype(jnp.bfloat16)
    final_norm = normalize(residual, gain_final)
    vocab_here = w_vocab.shape[1]
    logits = jnp.dot(
        lax.all_gather(final_norm, "dp", axis=1, tiled=True),
        w_vocab,
        preferred_element_type=jnp.float32,
    )
    pair_grid = pair_rows.reshape(-1, 2)
    cond_rows = logits[pair_grid[:, 0]]
    uncond_rows = logits[pair_grid[:, 1]]
    guided = uncond_rows + GUIDANCE * (cond_rows - uncond_rows)
    allowed = unpack(grammar, lax.axis_index(("dp", "mp")) * vocab_here, vocab_here)
    masked = jnp.where(allowed, guided, SENTINEL)
    local_top = jnp.max(masked, 1)
    local_sum = jnp.sum(jnp.where(allowed, jnp.exp(masked - local_top[:, None]), 0.0), 1)
    highest, summed = combined_all((local_top, local_sum), ("dp", "mp"), combine)
    return jnp.where(allowed, guided - highest[:, None] - jnp.log(summed)[:, None], 0.0)


def solution(mesh):
    in_specs = (
        P(None, "dp"),
        P("dp"),
        P("dp", "mp"),
        P("dp", None, "mp"),
        P(None, "dp"),
        P("dp", "mp", None, None),
        P("dp", "mp", None, None),
        P("dp"),
        P("dp"),
        P(None, ("dp", "mp")),
        P(),
        P(None, ("dp", "mp")),
    )
    out_specs = P(None, ("dp", "mp"))
    return jax.shard_map(local, mesh=mesh, in_specs=in_specs, out_specs=out_specs, check_vma=False)
```

profile of v0, /device:TPU:1, one launch (start us, length us, event | category | flops | bytes accessed | tf_op | source)
XLA Modules:
  0.0 518.0 jit_solution(4354605783327506046)
XLA Ops:
  6.5 0.0 copy-start
  6.5 0.0 reduce-scatter.2.cloned.1.call-start
  6.5 1.2 copy.37
  7.8 0.1 fusion.8
  7.8 0.0 copy-start.4
  7.8 64.8 %psum.14 = f32[512]{0:T(512)S(1)} all-reduce(f32[512]{0:T(512)S(1)} %fusion.8), channel_id=1, replica_groups=mesh['dp'=32,'mp'=4] {'dp'}, use_global_device_ids=true, to_apply=%region_1.0 | all-reduce | flops 512 | bytes 4096 | tf_op jit(solution)/shard_map/psum | solution.py:39
  72.7 1.0 copy.53
  73.7 2.1 fusion.21
  75.7 0.0 copy-done.4
  75.7 0.4 fusion.19
  76.1 2.8 pad_maximum_fusion
  78.9 0.0 copy-start.7
  78.9 0.0 copy-start.8
  78.9 0.0 reduce-scatter.2.cloned.1.call-update
  78.9 0.0 all-gather.7.cloned.1.call-start
  79.0 0.6 copy-done.7
  79.6 0.1 iota_compare_fusion
  79.7 0.1 multiply_cosine_fusion
  79.8 83.2 %reduce-scatter.2.cloned.1.call-done = f32[16,2560]{1,0:T(8,128)} async-done(((f32[512,2560]{1,0:T(8,128)}), f32[16,2560]{1,0:T(8,128)}) %reduce-scatter.2.cloned.1.call-update) | async-done | bytes 163856 | tf_op jit(solution)/shard_map/reduce_scatter | solution.py:106
  163.0 0.8 slice.78
  163.8 0.9 slice_bitcast_fusion
  164.8 0.1 subtract_convert_fusion.1
  164.9 0.1 fusion.23
  165.0 0.1 maximum_bitcast_fusion
  165.1 0.2 fusion.25
  165.3 0.0 copy-done
  165.3 1.0 fusion.35
  166.4 0.2 fusion.12
  166.6 0.0 copy-done.8
  166.7 0.6 fusion.4
  167.2 0.7 convert_element_type.70
  167.9 0.0 all-gather.7.cloned.1.call-update
  167.9 0.0 all-gather.9.cloned.1.call-start
  168.0 71.6 %all-gather.7.cloned.1.call-done = bf16[128,16,2048]{2,1,0:T(8,128)(2,1)} async-done(((bf16[1,16,2048]{2,1,0:T(8,128)(2,1)}), bf16[128,16,2048]{2,1,0:T(8,128)(2,1)}) %all-gather.7.cloned.1.call-update) | async-done | bytes 8388624 | tf_op jit(solution)/shard_map/all_gather | solution.py:127
  239.6 8.3 %copy.39 = bf16[32,4,16,2048]{3,2,0,1:T(8,128)(2,1)} copy(bf16[32,4,16,2048]{3,2,1,0:T(8,128)(2,1)} %bitcast.61) | data formatting | bytes 16777216 | tf_op jit(solution)/shard_map/reshape | solution.py:128
  247.8 0.0 copy-start.5
  247.8 7.0 %multiply_reduce_fusion = (f32[512]{0:T(512)S(1)}, f32[512,256]{0,1:T(8,128)S(1)}) fusion(bf16[512,2048,4]{1,0,2:T(8,128)(2,1)} %bitcast.62, bf16[4,2048,256]{2,1,0:T(8,128)(2,1)} %bitcast.78, bf16[512,256]{0,1:T(8,128)(2,1)S(1)} %copy.37), kind=kOutput, calls=%fused_computation.27 | convolution fusion | flops 2148269568 | bytes 13371392 | tf_op jit(solution)/shard_map/ijrc,jcd->ird/dot_general | solution.py:130
  254.8 62.5 %psum.15 = f32[512]{0:T(512)S(1)} all-reduce(f32[512]{0:T(512)S(1)} %get-tuple-element.63), channel_id=1, replica_groups=mesh['dp'=32,'mp'=4] {'dp'}, use_global_device_ids=true, to_apply=%region_6.7 | all-reduce | flops 512 | bytes 4096 | tf_op jit(solution)/shard_map/psum | solution.py:39
  317.3 0.0 copy-done.6
  317.3 0.8 multiply_convert_fusion
  318.1 0.0 all-gather.9.cloned.1.call-update
  318.2 0.0 copy-done.5
  318.2 0.1 reshape.137
  318.3 0.1 shift_right_arithmetic.23
  318.4 0.2 fusion.14
  318.6 50.4 %all-gather.9.cloned.1.call-done = bf16[512,8192]{0,1:T(8,128)(2,1)} async-done(((bf16[512,256]{0,1:T(8,128)(2,1)}), bf16[512,8192]{0,1:T(8,128)(2,1)}) %all-gather.9.cloned.1.call-update) | async-done | bytes 8388624 | tf_op jit(solution)/shard_map/all_gather | solution.py:137
  369.0 14.4 %fusion.36 = f32[512,1002]{1,0:T(8,128)S(1)} fusion(bf16[512,8192]{0,1:T(8,128)(2,1)} %all-gather.9.cloned.1.call-done, bf16[8192,1002]{0,1:T(8,128)(2,1)} %param.23), kind=kOutput, calls=%fused_computation.78 | convolution fusion | flops 8405385216 | bytes 26857472 | tf_op jit(solution)/shard_map/dot_general | solution.py:136
  383.5 2.0 gather_fusion.1
  385.5 1.5 copy.43
  387.1 0.0 copy-start.3
  387.1 2.0 gather_fusion
  389.1 2.5 copy.45
  391.6 0.0 copy-done.3
  391.7 0.0 copy-start.2
  391.7 0.1 shift_right_arithmetic.20
  391.7 0.0 copy-start.1
  391.8 2.0 fusion.11
  393.8 0.0 copy-done.2
  393.8 0.4 select_reduce_fusion
  394.2 53.9 %all-gather.3 = f32[128,1,256]{2,1,0:T(1,128)S(1)} all-gather(f32[1,1,256]{2,1,0:T(1,128)S(1)} %bitcast.77), channel_id=3, replica_groups=mesh['dp'=32,'mp'=4] {'dp','mp'}, dimensions={0}, use_global_device_ids=true | all-gather | bytes 132096 | tf_op jit(solution)/shard_map/all_gather | solution.py:17
  448.1 54.2 %all-gather.2 = f32[128,1,256]{2,1,0:T(1,128)S(1)} all-gather(f32[1,1,256]{2,1,0:T(1,128)S(1)} %bitcast.76), channel_id=2, replica_groups=mesh['dp'=32,'mp'=4] {'dp','mp'}, dimensions={0}, use_global_device_ids=true | all-gather | bytes 132096 | tf_op jit(solution)/shard_map/all_gather | solution.py:17
  502.3 6.7 %while.12 = (s32[]{:T(128)}, f32[256]{0:T(256)S(1)}, f32[256]{0:T(256)S(1)}, f32[127,256]{1,0:T(8,128)S(1)}, f32[127,256]{1,0:T(8,128)S(1)}, /*index=5*/s32[]{:T(128)}) while((s32[]{:T(128)}, f32[256]{0:T(256)S(1)}, f32[256]{0:T(256)S(1)}, f32[127,256]{1,0:T(8,128)S(1)}, f32[127,256]{1,0:T(8,128)S(1)}, /*index=5*/s32[]{:T(128)}) %tuple.45), condition=%wide.region_10.11_spmd, body=%wide.region_9.10_spmd.sunk | while | flops 1538 | bytes 10313 | solution.py:20
  509.0 2.5 subtract_select_fusion
  511.5 0.0 copy-done.1
  (275 shorter events, 4.2 us)
Async XLA Ops:
  6.5 158.8 %copy-start = (bf16[16,2,192,128]{3,2,1,0:T(8,128)(2,1)S(1)}, bf16[16,2,192,128]{3,2,1,0:T(8,128)(2,1)}, u32[]{:S(2)}) copy-start(bf16[16,2,192,128]{3,2,1,0:T(8,128)(2,1)} %param.19) | copy-start | bytes 4718596
  6.5 156.5 %reduce-scatter.2.cloned.1.call-start = ((), (), s32[]{:S(2)}) async-start(), calls=%async_computation.1 | async-start | bytes 5406720 | tf_op jit(solution)/shard_map/reduce_scatter | solution.py:106
  7.8 67.9 %copy-start.4 = (f32[256]{0:T(256)S(1)}, f32[256]{0:T(256)}, u32[]{:S(2)}) copy-start(f32[256]{0:T(256)} %param.15) | copy-start | bytes 3076
  78.9 0.7 copy-start.7
  78.9 87.7 %copy-start.8 = (bf16[16,2,192,128]{3,2,1,0:T(8,128)(2,1)S(1)}, bf16[16,2,192,128]{3,2,1,0:T(8,128)(2,1)}, u32[]{:S(2)}) copy-start(bf16[16,2,192,128]{3,2,1,0:T(8,128)(2,1)} %param.20) | copy-start | bytes 4718596
  78.9 160.6 %all-gather.7.cloned.1.call-start = ((), (), s32[]{:S(2)}) async-start(), calls=%async_computation.2 | async-start | bytes 8454144 | tf_op jit(solution)/shard_map/all_gather | solution.py:127
  167.9 201.1 %all-gather.9.cloned.1.call-start = ((), (), s32[]{:S(2)}) async-start(), calls=%async_computation.3 | async-start | bytes 8650752 | tf_op jit(solution)/shard_map/all_gather | solution.py:137
  247.8 69.5 %copy-start.6 = (f32[256]{0:T(256)S(1)}, f32[256]{0:T(256)}, u32[]{:S(2)}) copy-start(f32[256]{0:T(256)} %param.22) | copy-start | bytes 3076
  247.8 70.3 %copy-start.5 = (s32[512]{0:T(512)S(1)}, s32[512]{0:T(512)}, u32[]{:S(2)}) copy-start(s32[512]{0:T(512)} %param.24) | copy-start | bytes 6148
  387.1 4.6 copy-start.3
  391.7 2.1 copy-start.2
  391.7 119.8 %copy-start.1 = (bf16[16,2,192,128]{3,2,1,0:T(8,128)(2,1)S(1)}, bf16[16,2,192,128]{3,2,1,0:T(8,128)(2,1)}, u32[]{:S(2)}) copy-start(bf16[16,2,192,128]{3,2,1,0:T(8,128)(2,1)} %param.19) | copy-start | bytes 4718596
Sparse Core Ops, SparseCore 0:
  79.1 83.9 reduce-scatter.1
  168.1 71.4 all-gather.6
  318.3 50.7 all-gather.8
where the time goes:
time: 519 us; the launch traced here: 518 us
  blocking collectives  235 us (45%)
  waiting for transfers between devices  205 us (39%)
  matrix products  25.7 us (5%)
  local copies, waits for them, and re-layouts  23.3 us (4%)
  between operations  13.4 us (3%)
  other arithmetic  12.1 us (2%)
    psum x2, blocking collectives, normalize(): squares = lax.psum(jnp.sum(values * values, 1), 'dp')  127 us
    all_gather x2, blocking collectives, combined_all(): pieces = jax.tree.map(lambda part: lax.all_gather(part, axis), value)  108 us
    reduce_scatter x1, waiting for transfers between devices, local(): lax.psum_scatter(jnp.concatenate([jnp.dot(normed, w_query, preferred_elem...  83.2 us
    all_gather x1, waiting for transfers between devices, local(): everyone = lax.all_gather(attended[None], ('dp', 'mp'), axis=0, tiled=True)  71.6 us
    all_gather x1, waiting for transfers between devices, local(): lax.all_gather(final_norm, 'dp', axis=1, tiled=True)  50.4 us
    dot_general x1, matrix products, local(): jnp.dot(lax.all_gather(final_norm, 'dp', axis=1, tiled=True), w_vocab, pr...  14.4 us
  transfers between devices with their start and end apart: 3, of which 3 were waited for; matrix products, arithmetic and copies ran while one was open for 0% of the time, Pallas kernels for 0%

commit v1 on v0

v1 whole, which is shorter than its diff:
```python
import functools

import jax
import jax.numpy as jnp
from jax import lax
from jax.experimental import pallas as pl
from jax.experimental.pallas import tpu as pltpu
from jax.sharding import Mesh
from jax.sharding import PartitionSpec as P

D = 8192
HD = 128
NX, NZ, NC, NY = 4, 4, 2, 4
DP = ("x", "z", "c")
ALL = ("x", "z", "c", "y")

GUIDANCE = 3.0
ROPE_BASE = 500000.0
EPSILON = 1e-05
SENTINEL = -1e30
VOCAB_ROWS = 256
WORD_BITS = 16
SHIFTS = (1, 3, 2)
bf16 = jnp.bfloat16
f32 = jnp.float32


def shift(value, axis, by):
    size = lax.axis_size(axis)
    return lax.ppermute(value, axis, [(i, (i + by) % size) for i in range(size)])


def gather_axis(value, axis):
    got = {by: shift(value, axis, by) for by in SHIFTS}
    return jnp.stack([value, got[1], got[2], got[3]])


def rotate(values, cosine, sin_part):
    halves = values.shape[-1] // 2
    leading = values[..., :halves]
    trailing = values[..., halves:]
    return jnp.concatenate(
        [leading * cosine - trailing * sin_part, trailing * cosine + leading * sin_part], -1
    )


def attend(queries, new_key, new_value, key_cache, value_cache, lengths):
    rows, groups = (key_cache.shape[0], key_cache.shape[1])
    group_size = queries.shape[1] // groups
    scaling = queries.shape[2] ** (-0.5)
    grouped = queries.reshape(rows, groups, group_size, -1)
    scores = (
        jnp.einsum("rgqd,rgld->rgql", grouped, key_cache, preferred_element_type=f32)
        * scaling
    )
    fresh = (
        jnp.einsum("rgqd,rgd->rgq", grouped, new_key, preferred_element_type=f32) * scaling
    )
    usable = jnp.arange(key_cache.shape[2], dtype=jnp.int32)[None, :] < lengths[:, None]
    scores = jnp.where(usable[:, None, None, :], scores, SENTINEL)
    highest = jnp.maximum(jnp.max(scores, -1), fresh)
    weights = jnp.where(usable[:, None, None, :], jnp.exp(scores - highest[..., None]), 0.0)
    fresh_weight = jnp.exp(fresh - highest)
    summed = jnp.sum(weights, -1) + fresh_weight
    probs_cache = (weights / summed[..., None]).astype(bf16)
    probs_fresh = (fresh_weight / summed).astype(bf16)
    mixed = jnp.einsum(
        "rgql,rgld->rgqd", probs_cache, value_cache, preferred_element_type=f32
    )
    mixed = (
        mixed
        + probs_fresh.astype(f32)[..., None] * new_value.astype(f32)[:, :, None, :]
    )
    return mixed.reshape(rows, -1).astype(bf16)


def row_total(values, width):
    return values[..., width : width + 1] + values[..., width + 1 : width + 2]


def load_kernel(w_ref, after_ref, out_ref, arrived):
    copy = pltpu.make_async_copy(w_ref, out_ref, arrived)
    copy.start()
    copy.wait()


def load(weights, after, limit):
    hbm = pl.BlockSpec(memory_space=pl.ANY)
    return pl.pallas_call(
        load_kernel,
        out_shape=pltpu.VMEM(weights.shape, weights.dtype),
        in_specs=[hbm, hbm],
        out_specs=pl.BlockSpec(memory_space=pltpu.VMEM),
        scratch_shapes=[pltpu.SemaphoreType.DMA],
        compiler_params=pltpu.CompilerParams(vmem_limit_bytes=limit),
        cost_estimate=pl.CostEstimate(
            flops=0, bytes_accessed=2 * weights.size * weights.dtype.itemsize, transcendentals=0
        ),
    )(weights, after)


def project_kernel(core_ref, hidden_ref, gain_ref, query_ref, keyval_ref, *refs):
    got_ref = refs[0] if len(refs) == 2 else None
    out_ref = refs[-1]
    blocks, _, local_rows, features = hidden_ref.shape
    rows = blocks * local_rows
    values = hidden_ref[:, core_ref[0]].reshape(rows, features).astype(f32)
    total = jnp.sum(values * values, 1, keepdims=True)
    gained = (values * gain_ref[...]).astype(bf16)
    query_cols = query_ref.shape[1]
    width = query_cols + keyval_ref.shape[1]
    extra = out_ref.shape[1] - width

    def put(part, sums):
        if got_ref is not None:
            sums = sums + got_ref[:, part].astype(f32)
        out_ref[:, part] = sums.astype(bf16)

    put(slice(0, query_cols), jnp.dot(gained, query_ref[...], preferred_element_type=f32))
    put(slice(query_cols, width), jnp.dot(gained, keyval_ref[...], preferred_element_type=f32))
    if got_ref is not None:
        parts = got_ref[:, width:].astype(f32)
        total = total + parts[:, 0:1] + parts[:, 1:2]
    high = total.astype(bf16).astype(f32)
    column = lax.broadcasted_iota(jnp.int32, (rows, extra), 1)
    squares = jnp.where(column == 0, high, jnp.where(column == 1, total - high, 0.0))
    out_ref[:, width:] = squares.astype(bf16)


def project(core, hidden, gain, w_query, kv_columns, got):
    blocks, _, local_rows, features = hidden.shape
    rows = blocks * local_rows
    width = w_query.shape[1] + kv_columns.shape[1] + 128
    operands = [hidden, gain, w_query, kv_columns] + ([] if got is None else [got])
    whole = pl.BlockSpec(memory_space=pltpu.VMEM)
    return pl.pallas_call(
        project_kernel,
        out_shape=jax.ShapeDtypeStruct((rows, width), bf16),
        in_specs=[pl.BlockSpec(memory_space=pltpu.SMEM)] + [whole] * len(operands),
        out_specs=whole,
        compiler_params=pltpu.CompilerParams(vmem_limit_bytes=24 * 2**20),
        cost_estimate=pl.CostEstimate(
            flops=2 * rows * width * features, bytes_accessed=4 * rows * width, transcendentals=0
        ),
    )(core.reshape(1).astype(jnp.int32), *operands)


def guide_kernel(scale_ref, *refs):
    out_ref = refs[-1]
    pairs = out_ref.shape[1]
    kept = GUIDANCE * scale_ref[:pairs, :]
    taken = (GUIDANCE - 1.0) * scale_ref[pairs:, :]
    for place, ref in enumerate(refs[:-1]):
        both = kept * ref[:pairs, :].astype(f32) - taken * ref[pairs:, :].astype(f32)
        out_ref[place] = both.astype(bf16)


def guide_pairs(scale, blocks):
    rows, features = blocks[0].shape
    whole = pl.BlockSpec(memory_space=pltpu.VMEM)
    return pl.pallas_call(
        guide_kernel,
        out_shape=jax.ShapeDtypeStruct((len(blocks), rows // 2, features), bf16),
        in_specs=[whole] * (len(blocks) + 1),
        out_specs=whole,
        compiler_params=pltpu.CompilerParams(vmem_limit_bytes=12 * 2**20),
    )(scale, *blocks)


def vocab_kernel(steps, last, *refs):
    places, offset, w_ref = refs[:3]
    held = refs[3 : 3 + steps]
    refs = refs[3 + steps :]
    if last:
        words_ref, acc_ref, out_ref, share_ref = refs
    elif len(refs) == 1:
        (out_ref,) = refs
        acc_ref = None
    else:
        acc_ref, out_ref = refs
    count, pairs = out_ref.shape
    features = held[0].shape[2]
    top = jnp.full((1, pairs), SENTINEL, f32)
    summed = jnp.zeros((1, pairs), f32)
    for first in range(0, count, VOCAB_ROWS):
        rows = min(VOCAB_ROWS, count - first)
        part = slice(first, first + rows)
        total = None if acc_ref is None else acc_ref[part, :]
        for step in range(steps):
            for dz in range(NZ):
                start = pl.multiple_of(places[step * NZ + dz], features)
                product = lax.dot_general(
                    w_ref[part, pl.ds(start, features)],
                    held[step][dz],
                    (((1,), (1,)), ((), ())),
                    preferred_element_type=f32,
                )
                total = product if total is None else total + product
        if not last:
            out_ref[part, :] = total
            continue
        word_rows = -(-rows // WORD_BITS)
        words = words_ref[first // WORD_BITS : first // WORD_BITS + word_rows, :]
        words = jnp.broadcast_to(words[:, None, :], (word_rows, WORD_BITS, pairs))
        words = words.reshape(word_rows * WORD_BITS, pairs)[:rows]
        row = lax.broadcasted_iota(jnp.int32, total.shape, 0)
        bit = lax.shift_right_logical(words, row & (WORD_BITS - 1)) & 1
        allowed = (bit == 1) | (offset[0] + first + row == 0)
        masked = jnp.where(allowed, total, SENTINEL)
        out_ref[part, :] = masked
        before = top
        top = jnp.maximum(before, jnp.max(masked, 0, keepdims=True))
        summed = summed * jnp.exp(before - top) + jnp.sum(
            jnp.where(allowed, jnp.exp(masked - top), 0.0), 0, keepdims=True
        )
    if last:
        share_ref[...] = jnp.where(
            summed > 0.0, top + jnp.log(jnp.maximum(summed, 1e-30)), SENTINEL
        )


def vocab_step(places, offset, w_rows, held, acc, grammar_rows):
    count = w_rows.shape[0]
    pairs, features = held[0].shape[1:]
    depth = len(held) * NZ * features
    last = grammar_rows is not None
    whole = pl.BlockSpec(memory_space=pltpu.VMEM)
    scalars = pl.BlockSpec(memory_space=pltpu.SMEM)
    operands = [w_rows, *held]
    if last:
        operands.append(grammar_rows)
    aliases = {}
    if acc is not None:
        operands.append(acc)
        aliases = {len(operands) + 1: 0}
    out_shape = jax.ShapeDtypeStruct((count, pairs), f32)
    if last:
        out_shape = (out_shape, jax.ShapeDtypeStruct((1, pairs), f32))
    return pl.pallas_call(
        functools.partial(vocab_kernel, len(held), last),
        out_shape=out_shape,
        in_specs=[scalars, scalars] + [whole] * len(operands),
        out_specs=(whole, whole) if last else whole,
        input_output_aliases=aliases,
        compiler_params=pltpu.CompilerParams(vmem_limit_bytes=12 * 2**20),
        cost_estimate=pl.CostEstimate(
            flops=2 * count * pairs * depth, bytes_accessed=2 * count * depth, transcendentals=0
        ),
    )(places, offset, *operands)


def local(
    hidden_in,
    gain_attn,
    w_query,
    w_keyval,
    w_out,
    key_cache,
    value_cache,
    lengths,
    gain_final,
    w_vocab,
    pair_rows,
    grammar,
):
    local_rows = lengths.shape[0]
    row_count, features = hidden_in.shape
    query_cols = w_query.shape[1]
    group_count = w_keyval.shape[2] // HD
    x, z, c, y = (lax.axis_index(axis) for axis in ALL)
    pair_count = row_count // 2

    hidden_blocks = hidden_in.reshape(NX * NZ, NC, local_rows, features)
    gain_row = gain_attn.reshape(1, features)
    kv_columns = w_keyval.reshape(features, -1)
    width = query_cols + kv_columns.shape[1]
    mine = project(1 - c, hidden_blocks, gain_row, w_query, kv_columns, None)
    mine = project(c, hidden_blocks, gain_row, w_query, kv_columns, shift(mine, "c", 1))
    mine = lax.all_to_all(mine.reshape(NX * NZ, local_rows, -1), ("x", "z"), 0, 0)
    mine = jnp.sum(mine.astype(f32), 0)
    projected = mine * lax.rsqrt(row_total(mine, width) / D + EPSILON)

    halves = HD // 2
    frequency = ROPE_BASE ** (-2.0 * jnp.arange(halves, dtype=f32) / HD)
    angles = lengths.astype(f32)[:, None] * frequency[None, :]
    cosine = jnp.cos(angles)[:, None, :]
    sin_part = jnp.sin(angles)[:, None, :]
    queries = rotate(
        projected[:, :query_cols].reshape(local_rows, query_cols // HD, HD), cosine, sin_part
    ).astype(bf16)
    kv_pairs = projected[:, query_cols:width].reshape(local_rows, 2, group_count, HD)
    new_key = rotate(kv_pairs[:, 0], cosine, sin_part).astype(bf16)
    new_value = kv_pairs[:, 1].astype(bf16)
    attended = attend(queries, new_key, new_value, key_cache, value_cache, lengths)

    share = local_rows // NY
    blocks = jnp.broadcast_to(
        attended.reshape(NY, share, query_cols), (NX * NZ, NY, share, query_cols)
    )
    near = lax.all_to_all(blocks.reshape(-1, share, query_cols), ("x", "z", "y"), 0, 0)
    near, weights = lax.optimization_barrier((near, load(w_out, attended, 48 * 2**20)))
    near = near.reshape(NX * NZ, NY, share, query_cols).transpose(0, 2, 1, 3)
    near = near.reshape(NX * NZ * share, D)
    far = shift(near, "c", 1)
    near = jnp.dot(near, weights, preferred_element_type=f32)
    far = jnp.dot(far, weights, preferred_element_type=f32)
    update = jnp.concatenate([jnp.where(c == 0, near, far), jnp.where(c == 0, far, near)], 0)

    hidden_here = lax.dynamic_index_in_dim(
        hidden_in.reshape(NX * NZ, NC, NY, share, features), y, 2, False
    )
    hidden_here = hidden_here.transpose(1, 0, 2, 3).reshape(-1, features)
    residual = (hidden_here.astype(f32) + update).astype(bf16)
    rounded = residual.astype(f32)
    held = residual.shape[0]
    everyone = gather_axis((rounded * gain_final).astype(bf16), "y").reshape(row_count, features)
    quarters = jnp.arange(NY, dtype=jnp.int32)

    def rows_of(order):
        row = (
            jnp.arange(NX * NZ, dtype=jnp.int32)[None, None, :, None] * NC
            + jnp.arange(NC, dtype=jnp.int32)[None, :, None, None]
        ) * local_rows
        row = row + order[:, None, None, None] * share
        return (row + jnp.arange(share, dtype=jnp.int32)).reshape(-1)

    grid = pair_rows.reshape(pair_count, 2).T.reshape(-1, 1)
    pick = (grid == rows_of((y - quarters + NY) % NY)[None, :]).astype(bf16)
    picked = jnp.dot(pick, everyone, preferred_element_type=f32).astype(bf16)
    picked, squares_out = lax.optimization_barrier((picked, jnp.sum(rounded * rounded, 1)))
    shares = lax.all_to_all(
        jnp.broadcast_to(squares_out, (NX * NZ * NC * NY, held)), ALL, 0, 0
    )
    scale = lax.rsqrt(jnp.sum(shares.reshape(-1, NY * held), 0) / D + EPSILON)
    scale = jnp.sum(jnp.where(grid == rows_of(quarters)[None, :], scale[None, :], 0.0), 1)

    got = {by: shift(picked, "z", by) for by in SHIFTS}
    here = guide_pairs(scale[:, None], [picked, got[1], got[2], got[3]])
    sent = {by: shift(here, "x", by) for by in SHIFTS}
    down = jnp.arange(NZ, dtype=jnp.int32)
    offset = lax.axis_index(ALL) * w_vocab.shape[1]
    w_rows = load(w_vocab.T, here, 36 * 2**20)

    def chips(by):
        return ((x - by + NX) % NX) * NZ + (z - down + NZ) % NZ

    def step(blocks, acc, words):
        places = [(chips(by) * NC + (c + far) % NC) * features for by, far, _ in blocks]
        return vocab_step(
            jnp.concatenate(places).astype(jnp.int32),
            offset.reshape(1).astype(jnp.int32),
            w_rows,
            [block for _, _, block in blocks],
            acc,
            words,
        )

    guided = step([(0, 0, here)], None, None)
    guided, here, *arrived = lax.optimization_barrier((guided, here, *(sent[by] for by in SHIFTS)))
    over = [shift(block, "c", 1) for block in (here, *arrived)]
    guided = step(
        [(0, 1, over[0]), (1, 0, arrived[0]), (3, 0, arrived[1]), (2, 0, arrived[2]), (1, 1, over[1])],
        guided,
        None,
    )
    guided = step([(3, 1, over[2]), (2, 1, over[3])], guided, grammar.T)
    masked, shares = guided
    shares = lax.all_to_all(
        jnp.broadcast_to(shares[0], (NX * NZ * NC * NY, pair_count)), ALL, 0, 0
    )
    highest = jnp.max(shares, 0)
    total = highest + jnp.log(jnp.sum(jnp.exp(shares - highest), 0))
    return jnp.where(masked > 0.5 * SENTINEL, masked - total[None, :], 0.0).T


def solution(mesh):
    split = Mesh(mesh.devices.reshape(NX, NZ, NC, NY), ALL)
    in_specs = (
        P(None, DP),
        P(DP),
        P(DP, "y"),
        P(DP, None, "y"),
        P(None, DP),
        P(DP, "y", None, None),
        P(DP, "y", None, None),
        P(DP),
        P(DP),
        P(None, ALL),
        P(),
        P(None, ALL),
    )
    out_specs = P(None, ALL)
    return jax.shard_map(local, mesh=split, in_specs=in_specs, out_specs=out_specs, check_vma=False)
```

time: 519 us -> 173 us (0.33)
  blocking collectives: 235 us -> 18.2 us
  waiting for transfers between devices: 205 us -> 56.8 us
  starting transfers between devices: 0.09 us -> 41.9 us
  matrix products: 25.7 us -> 6.11 us
  Pallas kernels: 0 us -> 19 us
  between operations: 13.4 us -> 0.55 us
  other arithmetic: 12.1 us -> 4.23 us
    psum x2 -> x0, blocking collectives: 127 us -> none  [normalize(): squares = lax.psum(jnp.sum(values * values, 1), 'dp')]
    all_gather x2 -> x0, waiting for transfers between devices: 122 us -> none  [the longest x1 71.6 us: local(): everyone = lax.all_gather(attended[None], ('dp', 'mp'), axis=0, tiled=True)]
    all_gather x2 -> x0, blocking collectives: 108 us -> none  [combined_all(): pieces = jax.tree.map(lambda part: lax.all_gather(part, axis), value)]
    reduce_scatter x1 -> x0, waiting for transfers between devices: 83.2 us -> none  [local(): lax.psum_scatter(jnp.concatenate([jnp.dot(normed, w_query, preferred_elem...]
    all_to_all x0 -> x3, waiting for transfers between devices: none -> 35.1 us  [the longest x1 18.9 us: local(): lax.all_to_all(mine.reshape(NX * NZ, local_rows, -1), ('x', 'z'), 0, 0)]
    all_to_all x0 -> x3, starting transfers between devices: none -> 22 us  [the longest x1 8.41 us: local(): lax.all_to_all(blocks.reshape(-1, share, query_cols), ('x', 'z', 'y'), 0, 0)]
    ppermute x0 -> x15, waiting for transfers between devices: none -> 21.7 us  [shift(): lax.ppermute(value, axis, [(i, (i + by) % size) for i in range(size)])]
    ppermute x0 -> x15, starting transfers between devices: none -> 19.9 us  [shift(): lax.ppermute(value, axis, [(i, (i + by) % size) for i in range(size)])]
  transfers between devices with their start and end apart: 3 -> 18, of which waited for: 3 -> 9; matrix products, arithmetic and copies ran while one was open for 0% -> 4% of each run, Pallas kernels for 0% -> 8%
where the time goes in v1:
time: 173 us; the launch traced here: 172 us
  waiting for transfers between devices  56.8 us (33%)
  starting transfers between devices  41.9 us (24%)
  local copies, waits for them, and re-layouts  25.3 us (15%)
  Pallas kernels  19 us (11%)
  blocking collectives  18.2 us (11%)
  matrix products  6.11 us (4%)
  other arithmetic  4.23 us (2%)
    ppermute x15, waiting for transfers between devices, shift(): lax.ppermute(value, axis, [(i, (i + by) % size) for i in range(size)])  21.7 us
    unnamed x49, local copies, waits for them, and re-layouts  20.6 us
    ppermute x15, starting transfers between devices, shift(): lax.ppermute(value, axis, [(i, (i + by) % size) for i in range(size)])  19.9 us
    all_to_all x1, waiting for transfers between devices, local(): lax.all_to_all(mine.reshape(NX * NZ, local_rows, -1), ('x', 'z'), 0, 0)  18.9 us
    all_to_all x1, blocking collectives, local(): lax.all_to_all(jnp.broadcast_to(shares[0], (NX * NZ * NC * NY, pair_count...  18.2 us
    all_to_all x1, waiting for transfers between devices, local(): lax.all_to_all(blocks.reshape(-1, share, query_cols), ('x', 'z', 'y'), 0, 0)  12.1 us
    pallas_call x3, Pallas kernels, vocab_step(): pl.pallas_call(functools.partial(vocab_kernel, len(held), last), out_shap...  8.68 us
    all_to_all x1, starting transfers between devices, local(): lax.all_to_all(blocks.reshape(-1, share, query_cols), ('x', 'z', 'y'), 0, 0)  8.41 us
  transfers between devices with their start and end apart: 18, of which 9 were waited for; matrix products, arithmetic and copies ran while one was open for 4% of the time, Pallas kernels for 8%

profile of v1, /device:TPU:1, one launch (start us, length us, event | category | flops | bytes accessed | tf_op | source)
XLA Modules:
  0.0 172.2 jit_solution(10305325685835659358)
XLA Ops:
  0.0 1.1 copy.70
  1.2 1.2 copy-done.6
  2.4 0.9 copy-done.8
  3.3 0.7 copy-done.15
  4.0 0.5 shard_map.118
  4.5 1.5 collective-permute-start
  6.0 2.8 %collective-permute-done.refs_0_ = bf16[256,2688]{1,0:T(8,128)(2,1)S(1)} collective-permute-done((bf16[256,2688]{1,0:T(8,128)(2,1)S(1)}, bf16[256,2688]{1,0:T(8,128)(2,1)S(1)}, u32[]{:S(2)}, u32[]{:S(2)}) %collective-permute-start) | collective-permute-done | bytes 1376288 | tf_op jit(solution)/shard_map/ppermute | solution.py:30
  8.8 1.6 shard_map.119
  10.4 7.8 %all-to-all-start = ((bf16[16,16,2688]{2,1,0:T(8,128)(2,1)}), bf16[16,16,2688]{2,1,0:T(8,128)(2,1)S(1)}, u32[]{:S(2)}, u32[]{:S(2)}) async-start(bf16[16,16,2688]{2,1,0:T(8,128)(2,1)} %bitcast.9), calls=%async_computation | async-start | bytes 2752512 | tf_op jit(solution)/shard_map/all_to_all | solution.py:279
  18.5 18.9 %all-to-all-done = bf16[16,16,2688]{2,1,0:T(8,128)(2,1)S(1)} async-done(((bf16[16,16,2688]{2,1,0:T(8,128)(2,1)}), bf16[16,16,2688]{2,1,0:T(8,128)(2,1)S(1)}, u32[]{:S(2)}, u32[]{:S(2)}) %all-to-all-start) | async-done | bytes 1376288 | tf_op jit(solution)/shard_map/all_to_all | solution.py:279
  37.3 0.2 convert_reduce_fusion
  37.5 0.2 fusion.22
  38.2 0.2 fusion.15
  38.5 1.0 fusion.31
  39.5 0.2 fusion.5
  39.8 0.6 fusion.1
  40.4 1.5 broadcast_in_dim.44
  41.9 8.4 %all-to-all-start.1 = ((bf16[64,4,2048]{2,1,0:T(4,128)(2,1)}), bf16[64,4,2048]{2,1,0:T(4,128)(2,1)S(1)}, u32[]{:S(2)}, u32[]{:S(2)}) async-start(bf16[64,4,2048]{2,1,0:T(4,128)(2,1)} %bitcast.17), calls=%async_computation.1 | async-start | bytes 2097152 | tf_op jit(solution)/shard_map/all_to_all | solution.py:300
  50.5 2.2 %shard_map.120 = bf16[8192,256]{1,0:T(8,128)(2,1)S(1)} custom-call(bf16[8192,256]{1,0:T(8,128)(2,1)} %w_ref.1, bf16[16,2048]{1,0:T(8,128)(2,1)S(1)} %bitcast.88), custom_call_target="tpu_custom_call" | custom-call | bytes 8388608 | tf_op jit(solution)/shard_map/pallas_call | solution.py:89
  52.7 1.9 %copy-done.4 = bf16[8192,256]{1,0:T(8,128)(2,1)} copy-done((bf16[8192,256]{1,0:T(8,128)(2,1)}, bf16[8192,256]{1,0:T(8,128)(2,1)S(1)}, u32[]{:S(2)}) %copy-start.4) | copy-done | bytes 4194328
  54.6 12.1 %all-to-all-done.1 = bf16[64,4,2048]{2,1,0:T(4,128)(2,1)S(1)} async-done(((bf16[64,4,2048]{2,1,0:T(4,128)(2,1)}), bf16[64,4,2048]{2,1,0:T(4,128)(2,1)S(1)}, u32[]{:S(2)}, u32[]{:S(2)}) %all-to-all-start.1) | async-done | bytes 1048608 | tf_op jit(solution)/shard_map/all_to_all | solution.py:300
  66.7 0.9 copy.60
  67.6 0.6 copy.74
  68.2 3.2 %collective-permute-start.1 = (bf16[64,8192]{1,0:T(8,128)(2,1)S(1)}, bf16[64,8192]{1,0:T(8,128)(2,1)S(1)}, u32[]{:S(2)}, u32[]{:S(2)}) collective-permute-start(bf16[64,8192]{1,0:T(8,128)(2,1)S(1)} %bitcast.96), channel_id=1, source_target_pairs={{0,4},{4,0},{1,5},{5,1},{2,6},{6,2},{3,7},{7,3},{8,12},{12,8},{9,1... | collective-permute-start | bytes 3145736 | tf_op jit(solution)/shard_map/ppermute | solution.py:30
  72.1 3.1 %fusion.32 = f32[64,256]{1,0:T(8,128)S(1)} fusion(bf16[64,8192]{1,0:T(8,128)(2,1)S(1)} %bitcast.97, bf16[8192,256]{1,0:T(8,128)(2,1)} %copy-done.4), kind=kOutput, calls=%fused_computation.101 | convolution fusion | flops 268435456 | bytes 5308416 | tf_op jit(solution)/shard_map/dot_general | solution.py:305
  75.2 0.3 copy-done.5
  75.5 0.8 broadcast_select_fusion.1
  76.4 0.6 collective-permute-start.2
  77.0 1.2 collective-permute-start.3
  78.2 1.4 collective-permute-start.4
  80.0 2.8 %collective-permute-done.2 = bf16[128,256]{1,0:T(8,128)(2,1)S(1)} collective-permute-done((bf16[128,256]{1,0:T(8,128)(2,1)S(1)}, bf16[128,256]{1,0:T(8,128)(2,1)S(1)}, u32[]{:S(2)}, u32[]{:S(2)}) %collective-permute-start.2) | collective-permute-done | bytes 65568 | tf_op jit(solution)/shard_map/ppermute | solution.py:30
  82.8 0.3 collective-permute-done.4
  83.0 0.4 convolution_convert_fusion.refs_0_
  83.4 0.7 broadcast_in_dim.74
  84.1 5.8 %all-to-all-start.2 = ((f32[128,1,128]{2,1,0:T(1,128)}), f32[128,1,128]{2,1,0:T(1,128)S(1)}, u32[]{:S(2)}, u32[]{:S(2)}) async-start(f32[128,1,128]{2,1,0:T(1,128)} %broadcast_in_dim.74), calls=%async_computation.2 | async-start | bytes 131072 | tf_op jit(solution)/shard_map/all_to_all | solution.py:331
  90.1 1.6 collective-permute-start.5
  91.6 2.9 %collective-permute-start.6 = (bf16[512,256]{1,0:T(8,128)(2,1)S(1)}, bf16[512,256]{1,0:T(8,128)(2,1)S(1)}, u32[]{:S(2)}, u32[]{:S(2)}) collective-permute-start(bf16[512,256]{1,0:T(8,128)(2,1)S(1)} %convolution_convert_fusion.refs_0_), channel_id=1, source_target_pairs={{0,16},{8,24},{16,0},{24,8},{1,17},{9,25},{17,1},{25,9},{2,18},{10... | collective-permute-start | bytes 786440 | tf_op jit(solution)/shard_map/ppermute | solution.py:30
  94.6 0.9 collective-permute-start.7
  95.5 4.2 %all-to-all-done.2 = f32[128,1,128]{2,1,0:T(1,128)S(1)} async-done(((f32[128,1,128]{2,1,0:T(1,128)}), f32[128,1,128]{2,1,0:T(1,128)S(1)}, u32[]{:S(2)}, u32[]{:S(2)}) %all-to-all-start.2) | async-done | bytes 65568 | tf_op jit(solution)/shard_map/all_to_all | solution.py:331
  99.7 0.5 broadcast.329
  100.2 0.8 reduce.7
  101.1 0.3 select_reduce_fusion
  101.5 5.5 %collective-permute-done.6.refs_2_ = bf16[512,256]{1,0:T(8,128)(2,1)S(1)} collective-permute-done((bf16[512,256]{1,0:T(8,128)(2,1)S(1)}, bf16[512,256]{1,0:T(8,128)(2,1)S(1)}, u32[]{:S(2)}, u32[]{:S(2)}) %collective-permute-start.6) | collective-permute-done | bytes 262176 | tf_op jit(solution)/shard_map/ppermute | solution.py:30
  107.0 0.3 shard_map.121.after_ref.refs_3_
  107.3 2.6 %collective-permute-start.10 = (bf16[4,256,256]{2,1,0:T(8,128)(2,1)S(1)}, bf16[4,256,256]{2,1,0:T(8,128)(2,1)S(1)}, u32[]{:S(2)}, u32[]{:S(2)}) collective-permute-start(bf16[4,256,256]{2,1,0:T(8,128)(2,1)S(1)} %shard_map.121.after_ref.refs_3_), channel_id=1, source_target_pairs={{0,64},{32,96},{64,0},{96,32},{1,65},{33,97},{65,1},{97,33},{2,66}... | collective-permute-start | bytes 1572872 | tf_op jit(solution)/shard_map/ppermute | solution.py:30
  109.9 0.3 collective-permute-start.8
  110.2 2.4 %collective-permute-start.9 = (bf16[4,256,256]{2,1,0:T(8,128)(2,1)S(1)}, bf16[4,256,256]{2,1,0:T(8,128)(2,1)}, u32[]{:S(2)}, u32[]{:S(2)}) collective-permute-start(bf16[4,256,256]{2,1,0:T(8,128)(2,1)S(1)} %shard_map.121.after_ref.refs_3_), channel_id=1, source_target_pairs={{0,96},{32,0},{64,32},{96,64},{1,97},{33,1},{65,33},{97,65},{2,98}... | collective-permute-start | bytes 1572872 | tf_op jit(solution)/shard_map/ppermute | solution.py:30
  112.6 5.7 %shard_map.122.refs_2_ = bf16[1002,8192]{1,0:T(8,128)(2,1)S(1)} custom-call(bf16[1002,8192]{1,0:T(8,128)(2,1)} %bitcast.93, bf16[4,256,256]{2,1,0:T(8,128)(2,1)S(1)} %shard_map.121.after_ref.refs_3_), custom_call_target="tpu_custom_call" | custom-call | bytes 32833536 | tf_op jit(solution)/shard_map/pallas_call | solution.py:89
  118.3 1.3 shard_map.123.refs_8_
  119.6 4.4 %copy-done.2 = bf16[1002,8192]{1,0:T(8,128)(2,1)} copy-done((bf16[1002,8192]{1,0:T(8,128)(2,1)}, bf16[1002,8192]{1,0:T(8,128)(2,1)S(1)}, u32[]{:S(2)}) %copy-start.2) | copy-done | bytes 16416792
  124.0 10.0 %collective-permute-done.8.refs_4_ = bf16[4,256,256]{2,1,0:T(8,128)(2,1)S(1)} collective-permute-done((bf16[4,256,256]{2,1,0:T(8,128)(2,1)S(1)}, bf16[4,256,256]{2,1,0:T(8,128)(2,1)S(1)}, u32[]{:S(2)}, u32[]{:S(2)}) %collective-permute-start.8) | collective-permute-done | bytes 524320 | tf_op jit(solution)/shard_map/ppermute | solution.py:30
  133.9 0.5 collective-permute-start.13
  134.4 0.8 copy-done.10
  135.3 0.6 collective-permute-start.11
  136.1 0.4 collective-permute-done.13.refs_3_
  136.6 0.8 copy-done.12
  137.4 5.7 %copy-done.3 = bf16[1002,8192]{1,0:T(8,128)(2,1)S(1)} copy-done((bf16[1002,8192]{1,0:T(8,128)(2,1)S(1)}, bf16[1002,8192]{1,0:T(8,128)(2,1)}, u32[]{:S(2)}) %copy-start.3) | copy-done | bytes 16416792
  143.1 1.0 copy-done.11
  144.1 1.0 copy-done.13
  145.2 4.2 %shard_map.124.refs_6_ = f32[1002,256]{1,0:T(8,128)S(1)} custom-call(s32[20]{0:T(128)S(1)} %concatenate.47.refs_0_, s32[1]{0:T(128)} %bitcast.refs_1_, bf16[1002,8192]{1,0:T(8,128)(2,1)S(1)} %copy-done.3, bf16[4,256,256]{2,1,0:T(8,128)(2,1)S(1)} %copy-done.13, bf16[4,256,256]{2,1,0:T(8,128)(2,1)S(1)} %copy-done.11, ...), custom_call_target="tpu_custom_call", output_to_operand_aliasing={{}: (8, {})} | custom-call | flops 2626682880 | bytes 10260480 | tf_op jit(solution)/shard_map/pallas_call | solution.py:239
  149.4 3.2 %shard_map.125 = (f32[1002,256]{1,0:T(8,128)S(1)}, f32[1,256]{1,0:T(1,128)S(1)}) custom-call(s32[8]{0:T(128)S(1)} %pad_add_fusion.refs_0_, s32[1]{0:T(128)} %bitcast.refs_1_, bf16[1002,8192]{1,0:T(8,128)(2,1)S(1)} %copy-done.3, bf16[4,256,256]{2,1,0:T(8,128)(2,1)} %collective-permute-done.11.refs_3_, ...), custom_call_target="tpu_custom_call", output_to_operand_aliasing={{0}: (6, {})} | custom-call | flops 1050673152 | bytes 4104192 | tf_op jit(solution)/shard_map/pallas_call | solution.py:239
  152.7 18.2 %all_to_all.25 = f32[128,1,256]{2,1,0:T(1,128)S(1)} all-to-all(f32[128,1,256]{2,1,0:T(1,128)S(1)} %broadcast_in_dim.78), channel_id=1, replica_groups=mesh['x'=4,'z'=4,'c'=2,'y'=4] {'x','z','c','y'}, dimensions={0} | all-to-all | bytes 262144 | tf_op jit(solution)/shard_map/all_to_all | solution.py:368
  170.9 0.2 reduce_max.19
  171.1 1.1 select_bitcast_fusion
  (96 shorter events, 2.7 us)
Async XLA Ops:
  0.0 38.5 %copy-start = (bf16[16,2,192,128]{3,2,1,0:T(8,128)(2,1)S(1)}, bf16[16,2,192,128]{3,2,1,0:T(8,128)(2,1)}, u32[]{:S(2)}) copy-start(bf16[16,2,192,128]{3,2,1,0:T(8,128)(2,1)} %param.17) | copy-start | bytes 4718596
  0.0 8.8 %copy-start.9 = (bf16[512,256]{1,0:T(8,128)(2,1)S(1)}, bf16[512,256]{1,0:T(8,128)(2,1)}, u32[]{:S(2)}) copy-start(bf16[512,256]{1,0:T(8,128)(2,1)} %param.12) | copy-start | bytes 786436
  1.1 7.7 %copy-start.16 = (f32[256]{0:T(256)S(1)}, f32[256]{0:T(256)}, u32[]{:S(2)}) copy-start(f32[256]{0:T(256)} %param.13) | copy-start | bytes 3076
  1.1 1.2 copy-start.6
  2.4 0.9 copy-start.8
  3.3 0.7 copy-start.15
  4.0 4.8 %copy-start.7 = (bf16[256,2048]{1,0:T(8,128)(2,1)S(1)}, bf16[256,2048]{1,0:T(8,128)(2,1)}, u32[]{:S(2)}) copy-start(bf16[256,2048]{1,0:T(8,128)(2,1)} %query_ref.3) | copy-start | bytes 3145732
  4.5 4.3 %collective-permute-start = (bf16[256,2688]{1,0:T(8,128)(2,1)S(1)}, bf16[256,2688]{1,0:T(8,128)(2,1)S(1)}, u32[]{:S(2)}, u32[]{:S(2)}) collective-permute-start(bf16[256,2688]{1,0:T(8,128)(2,1)S(1)} %shard_map.118), channel_id=1, source_target_pairs={{0,4},{4,0},{1,5},{5,1},{2,6},{6,2},{3,7},{7,3},{8,12},{12,8},{9,1... | collective-permute-start | bytes 4128776 | tf_op jit(solution)/shard_map/ppermute | solution.py:30
  10.4 7.8 %copy-start.19 = (s32[16]{0:T(128)S(1)}, s32[16]{0:T(128)}, u32[]{:S(2)}) copy-start(s32[16]{0:T(128)} %param.19) | copy-start | bytes 196
  10.4 26.9 %all-to-all-start = ((bf16[16,16,2688]{2,1,0:T(8,128)(2,1)}), bf16[16,16,2688]{2,1,0:T(8,128)(2,1)S(1)}, u32[]{:S(2)}, u32[]{:S(2)}) async-start(bf16[16,16,2688]{2,1,0:T(8,128)(2,1)} %bitcast.9), calls=%async_computation | async-start | bytes 2752512 | tf_op jit(solution)/shard_map/all_to_all | solution.py:279
  37.9 1.8 %copy-start.20 = (bf16[16,2,192,128]{3,2,1,0:T(8,128)(2,1)S(1)}, bf16[16,2,192,128]{3,2,1,0:T(8,128)(2,1)}, u32[]{:S(2)}) copy-start(bf16[16,2,192,128]{3,2,1,0:T(8,128)(2,1)} %param.18) | copy-start | bytes 4718596
  41.9 24.8 %all-to-all-start.1 = ((bf16[64,4,2048]{2,1,0:T(4,128)(2,1)}), bf16[64,4,2048]{2,1,0:T(4,128)(2,1)S(1)}, u32[]{:S(2)}, u32[]{:S(2)}) async-start(bf16[64,4,2048]{2,1,0:T(4,128)(2,1)} %bitcast.17), calls=%async_computation.1 | async-start | bytes 2097152 | tf_op jit(solution)/shard_map/all_to_all | solution.py:300
  52.7 1.9 %copy-start.4 = (bf16[8192,256]{1,0:T(8,128)(2,1)}, bf16[8192,256]{1,0:T(8,128)(2,1)S(1)}, u32[]{:S(2)}) copy-start(bf16[8192,256]{1,0:T(8,128)(2,1)S(1)} %shard_map.120) | copy-start | bytes 12582916
  67.6 4.2 %copy-start.18 = (s32[512]{0:T(512)S(1)}, s32[512]{0:T(512)}, u32[]{:S(2)}) copy-start(s32[512]{0:T(512)} %param.22) | copy-start | bytes 6148
  68.2 7.0 %collective-permute-start.1 = (bf16[64,8192]{1,0:T(8,128)(2,1)S(1)}, bf16[64,8192]{1,0:T(8,128)(2,1)S(1)}, u32[]{:S(2)}, u32[]{:S(2)}) collective-permute-start(bf16[64,8192]{1,0:T(8,128)(2,1)S(1)} %bitcast.96), channel_id=1, source_target_pairs={{0,4},{4,0},{1,5},{5,1},{2,6},{6,2},{3,7},{7,3},{8,12},{12,8},{9,1... | collective-permute-start | bytes 3145736 | tf_op jit(solution)/shard_map/ppermute | solution.py:30
  72.1 3.5 %copy-start.5 = (bf16[8192,256]{1,0:T(8,128)(2,1)S(1)}, bf16[8192,256]{1,0:T(8,128)(2,1)}, u32[]{:S(2)}) copy-start(bf16[8192,256]{1,0:T(8,128)(2,1)} %copy-done.4) | copy-start | bytes 12582916
  75.2 1.1 copy-start.17
  76.4 6.4 %collective-permute-start.2 = (bf16[128,256]{1,0:T(8,128)(2,1)S(1)}, bf16[128,256]{1,0:T(8,128)(2,1)S(1)}, u32[]{:S(2)}, u32[]{:S(2)}) collective-permute-start(bf16[128,256]{1,0:T(8,128)(2,1)S(1)} %get-tuple-element.30), channel_id=1, source_target_pairs={{0,1},{1,2},{2,3},{3,0},{4,5},{5,6},{6,7},{7,4},{8,9},{9,10},{10,1... | collective-permute-start | bytes 196616 | tf_op jit(solution)/shard_map/ppermute | solution.py:30
  77.0 5.8 %collective-permute-start.3 = (bf16[128,256]{1,0:T(8,128)(2,1)S(1)}, bf16[128,256]{1,0:T(8,128)(2,1)S(1)}, u32[]{:S(2)}, u32[]{:S(2)}) collective-permute-start(bf16[128,256]{1,0:T(8,128)(2,1)S(1)} %get-tuple-element.30), channel_id=1, source_target_pairs={{0,2},{1,3},{2,0},{3,1},{4,6},{5,7},{6,4},{7,5},{8,10},{9,11},{10,... | collective-permute-start | bytes 196616 | tf_op jit(solution)/shard_map/ppermute | solution.py:30
  78.2 4.8 %collective-permute-start.4 = (bf16[128,256]{1,0:T(8,128)(2,1)S(1)}, bf16[128,256]{1,0:T(8,128)(2,1)S(1)}, u32[]{:S(2)}, u32[]{:S(2)}) collective-permute-start(bf16[128,256]{1,0:T(8,128)(2,1)S(1)} %get-tuple-element.30), channel_id=1, source_target_pairs={{0,3},{1,0},{2,1},{3,2},{4,7},{5,4},{6,5},{7,6},{8,11},{9,8},{10,9... | collective-permute-start | bytes 196616 | tf_op jit(solution)/shard_map/ppermute | solution.py:30
  84.1 15.6 %all-to-all-start.2 = ((f32[128,1,128]{2,1,0:T(1,128)}), f32[128,1,128]{2,1,0:T(1,128)S(1)}, u32[]{:S(2)}, u32[]{:S(2)}) async-start(f32[128,1,128]{2,1,0:T(1,128)} %broadcast_in_dim.74), calls=%async_computation.2 | async-start | bytes 131072 | tf_op jit(solution)/shard_map/all_to_all | solution.py:331
  90.1 11.4 %collective-permute-start.5 = (bf16[512,256]{1,0:T(8,128)(2,1)S(1)}, bf16[512,256]{1,0:T(8,128)(2,1)S(1)}, u32[]{:S(2)}, u32[]{:S(2)}) collective-permute-start(bf16[512,256]{1,0:T(8,128)(2,1)S(1)} %convolution_convert_fusion.refs_0_), channel_id=1, source_target_pairs={{0,8},{8,16},{16,24},{24,0},{1,9},{9,17},{17,25},{25,1},{2,10},{10... | collective-permute-start | bytes 786440 | tf_op jit(solution)/shard_map/ppermute | solution.py:30
  91.6 15.3 %collective-permute-start.6 = (bf16[512,256]{1,0:T(8,128)(2,1)S(1)}, bf16[512,256]{1,0:T(8,128)(2,1)S(1)}, u32[]{:S(2)}, u32[]{:S(2)}) collective-permute-start(bf16[512,256]{1,0:T(8,128)(2,1)S(1)} %convolution_convert_fusion.refs_0_), channel_id=1, source_target_pairs={{0,16},{8,24},{16,0},{24,8},{1,17},{9,25},{17,1},{25,9},{2,18},{10... | collective-permute-start | bytes 786440 | tf_op jit(solution)/shard_map/ppermute | solution.py:30
  94.6 12.4 %collective-permute-start.7 = (bf16[512,256]{1,0:T(8,128)(2,1)S(1)}, bf16[512,256]{1,0:T(8,128)(2,1)S(1)}, u32[]{:S(2)}, u32[]{:S(2)}) collective-permute-start(bf16[512,256]{1,0:T(8,128)(2,1)S(1)} %convolution_convert_fusion.refs_0_), channel_id=1, source_target_pairs={{0,24},{8,0},{16,8},{24,16},{1,25},{9,1},{17,9},{25,17},{2,26},{10... | collective-permute-start | bytes 786440 | tf_op jit(solution)/shard_map/ppermute | solution.py:30
  107.3 16.7 %collective-permute-start.10 = (bf16[4,256,256]{2,1,0:T(8,128)(2,1)S(1)}, bf16[4,256,256]{2,1,0:T(8,128)(2,1)S(1)}, u32[]{:S(2)}, u32[]{:S(2)}) collective-permute-start(bf16[4,256,256]{2,1,0:T(8,128)(2,1)S(1)} %shard_map.121.after_ref.refs_3_), channel_id=1, source_target_pairs={{0,64},{32,96},{64,0},{96,32},{1,65},{33,97},{65,1},{97,33},{2,66}... | collective-permute-start | bytes 1572872 | tf_op jit(solution)/shard_map/ppermute | solution.py:30
  109.9 24.0 %collective-permute-start.8 = (bf16[4,256,256]{2,1,0:T(8,128)(2,1)S(1)}, bf16[4,256,256]{2,1,0:T(8,128)(2,1)S(1)}, u32[]{:S(2)}, u32[]{:S(2)}) collective-permute-start(bf16[4,256,256]{2,1,0:T(8,128)(2,1)S(1)} %shard_map.121.after_ref.refs_3_), channel_id=1, source_target_pairs={{0,32},{32,64},{64,96},{96,0},{1,33},{33,65},{65,97},{97,1},{2,34}... | collective-permute-start | bytes 1572872 | tf_op jit(solution)/shard_map/ppermute | solution.py:30
  110.2 23.8 %collective-permute-start.9 = (bf16[4,256,256]{2,1,0:T(8,128)(2,1)S(1)}, bf16[4,256,256]{2,1,0:T(8,128)(2,1)}, u32[]{:S(2)}, u32[]{:S(2)}) collective-permute-start(bf16[4,256,256]{2,1,0:T(8,128)(2,1)S(1)} %shard_map.121.after_ref.refs_3_), channel_id=1, source_target_pairs={{0,96},{32,0},{64,32},{96,64},{1,97},{33,1},{65,33},{97,65},{2,98}... | collective-permute-start | bytes 1572872 | tf_op jit(solution)/shard_map/ppermute | solution.py:30
  118.3 5.7 %copy-start.2 = (bf16[1002,8192]{1,0:T(8,128)(2,1)}, bf16[1002,8192]{1,0:T(8,128)(2,1)S(1)}, u32[]{:S(2)}) copy-start(bf16[1002,8192]{1,0:T(8,128)(2,1)S(1)} %shard_map.122.refs_2_) | copy-start | bytes 49250308
  133.9 2.6 %collective-permute-start.13 = (bf16[4,256,256]{2,1,0:T(8,128)(2,1)S(1)}, bf16[4,256,256]{2,1,0:T(8,128)(2,1)S(1)}, u32[]{:S(2)}, u32[]{:S(2)}) collective-permute-start(bf16[4,256,256]{2,1,0:T(8,128)(2,1)S(1)} %shard_map.121.after_ref.refs_3_), channel_id=1, source_target_pairs={{0,4},{4,0},{1,5},{5,1},{2,6},{6,2},{3,7},{7,3},{8,12},{12,8},{9,1... | collective-permute-start | bytes 1572872 | tf_op jit(solution)/shard_map/ppermute | solution.py:30
  134.4 2.9 %collective-permute-start.14 = (bf16[4,256,256]{2,1,0:T(8,128)(2,1)S(1)}, bf16[4,256,256]{2,1,0:T(8,128)(2,1)}, u32[]{:S(2)}, u32[]{:S(2)}) collective-permute-start(bf16[4,256,256]{2,1,0:T(8,128)(2,1)S(1)} %collective-permute-done.8.refs_4_), channel_id=1, source_target_pairs={{0,4},{4,0},{1,5},{5,1},{2,6},{6,2},{3,7},{7,3},{8,12},{12,8},{9,1... | collective-permute-start | bytes 1572872 | tf_op jit(solution)/shard_map/ppermute | solution.py:30
  134.4 0.8 copy-start.10
  135.3 14.1 %collective-permute-start.11 = (bf16[4,256,256]{2,1,0:T(8,128)(2,1)}, bf16[4,256,256]{2,1,0:T(8,128)(2,1)}, u32[]{:S(2)}, u32[]{:S(2)}) collective-permute-start(bf16[4,256,256]{2,1,0:T(8,128)(2,1)} %collective-permute-done.9.refs_5_), channel_id=1, source_target_pairs={{0,4},{4,0},{1,5},{5,1},{2,6},{6,2},{3,7},{7,3},{8,12},{12,8},{9,1... | collective-permute-start | bytes 1572872 | tf_op jit(solution)/shard_map/ppermute | solution.py:30
  135.9 13.5 %collective-permute-start.12 = (bf16[4,256,256]{2,1,0:T(8,128)(2,1)S(1)}, bf16[4,256,256]{2,1,0:T(8,128)(2,1)}, u32[]{:S(2)}, u32[]{:S(2)}) collective-permute-start(bf16[4,256,256]{2,1,0:T(8,128)(2,1)S(1)} %collective-permute-done.10.refs_6_), channel_id=1, source_target_pairs={{0,4},{4,0},{1,5},{5,1},{2,6},{6,2},{3,7},{7,3},{8,12},{12,8},{9,1... | collective-permute-start | bytes 1572872 | tf_op jit(solution)/shard_map/ppermute | solution.py:30
  136.6 0.8 copy-start.12
  137.4 5.7 %copy-start.3 = (bf16[1002,8192]{1,0:T(8,128)(2,1)S(1)}, bf16[1002,8192]{1,0:T(8,128)(2,1)}, u32[]{:S(2)}) copy-start(bf16[1002,8192]{1,0:T(8,128)(2,1)} %copy-done.2) | copy-start | bytes 49250308
  143.1 1.0 copy-start.11
  144.1 1.0 copy-start.13
  145.2 4.2 %copy-start.14 = (s32[256,63]{0,1:T(8,128)S(1)}, s32[256,63]{0,1:T(8,128)}, u32[]{:S(2)}) copy-start(s32[256,63]{0,1:T(8,128)} %param.23) | copy-start | bytes 193540
  149.4 22.9 %copy-start.1 = (bf16[16,2,192,128]{3,2,1,0:T(8,128)(2,1)S(1)}, bf16[16,2,192,128]{3,2,1,0:T(8,128)(2,1)}, u32[]{:S(2)}) copy-start(bf16[16,2,192,128]{3,2,1,0:T(8,128)(2,1)} %param.17) | copy-start | bytes 4718596

commit v2 on v1

v2 whole, which is shorter than its diff:
```python
import functools

import jax
import jax.numpy as jnp
from jax import lax
from jax.experimental import pallas as pl
from jax.experimental.pallas import tpu as pltpu
from jax.sharding import Mesh
from jax.sharding import PartitionSpec as P

D = 8192
HD = 128
NX, NZ, NC, NY = 4, 4, 2, 4
DP = ("x", "z", "c")
ALL = ("x", "z", "c", "y")

GUIDANCE = 3.0
ROPE_BASE = 500000.0
EPSILON = 1e-05
SENTINEL = -1e30
VOCAB_ROWS = 256
WORD_BITS = 16
SHIFTS = (1, 3, 2)
SWAPS = (("x", 1), ("x", 3), ("z", 1), ("z", 3))
PARTS = len(SWAPS)
bf16 = jnp.bfloat16
f32 = jnp.float32


def shift(value, axis, by):
    size = lax.axis_size(axis)
    return lax.ppermute(value, axis, [(i, (i + by) % size) for i in range(size)])


def swap(value, part, step):
    axis, by = SWAPS[(part + step) % PARTS]
    return lax.ppermute(value, axis, [(i, i ^ by) for i in range(lax.axis_size(axis))])


def slot_of(part, distance):
    return sum((distance >> (part + step) % PARTS & 1) << step for step in range(PARTS))


def rotate(values, cosine, sin_part):
    halves = values.shape[-1] // 2
    leading = values[..., :halves]
    trailing = values[..., halves:]
    return jnp.concatenate(
        [leading * cosine - trailing * sin_part, trailing * cosine + leading * sin_part], -1
    )


def attend(queries, new_key, new_value, key_cache, value_cache, lengths):
    rows, groups = (key_cache.shape[0], key_cache.shape[1])
    group_size = queries.shape[1] // groups
    scaling = queries.shape[2] ** (-0.5)
    grouped = queries.reshape(rows, groups, group_size, -1)
    scores = (
        jnp.einsum("rgqd,rgld->rgql", grouped, key_cache, preferred_element_type=f32)
        * scaling
    )
    fresh = (
        jnp.einsum("rgqd,rgd->rgq", grouped, new_key, preferred_element_type=f32) * scaling
    )
    usable = jnp.arange(key_cache.shape[2], dtype=jnp.int32)[None, :] < lengths[:, None]
    scores = jnp.where(usable[:, None, None, :], scores, SENTINEL)
    highest = jnp.maximum(jnp.max(scores, -1), fresh)
    weights = jnp.where(usable[:, None, None, :], jnp.exp(scores - highest[..., None]), 0.0)
    fresh_weight = jnp.exp(fresh - highest)
    summed = jnp.sum(weights, -1) + fresh_weight
    probs_cache = (weights / summed[..., None]).astype(bf16)
    probs_fresh = (fresh_weight / summed).astype(bf16)
    mixed = jnp.einsum(
        "rgql,rgld->rgqd", probs_cache, value_cache, preferred_element_type=f32
    )
    mixed = (
        mixed
        + probs_fresh.astype(f32)[..., None] * new_value.astype(f32)[:, :, None, :]
    )
    return mixed.reshape(rows, -1).astype(bf16)


def row_total(values, width):
    return values[..., width : width + 1] + values[..., width + 1 : width + 2]


def small_cost(flops, moved):
    return pl.CostEstimate(flops=flops, bytes_accessed=moved, transcendentals=0)


def load_kernel(w_ref, after_ref, out_ref, arrived):
    copy = pltpu.make_async_copy(w_ref, out_ref, arrived)
    copy.start()
    copy.wait()


def load(weights, after, limit):
    hbm = pl.BlockSpec(memory_space=pl.ANY)
    return pl.pallas_call(
        load_kernel,
        out_shape=pltpu.VMEM(weights.shape, weights.dtype),
        in_specs=[hbm, hbm],
        out_specs=pl.BlockSpec(memory_space=pltpu.VMEM),
        scratch_shapes=[pltpu.SemaphoreType.DMA],
        compiler_params=pltpu.CompilerParams(vmem_limit_bytes=limit),
        cost_estimate=pl.CostEstimate(
            flops=0, bytes_accessed=2 * weights.size * weights.dtype.itemsize, transcendentals=0
        ),
    )(weights, after)


def repeat_kernel(block_ref, out_ref):
    for copy in range(out_ref.shape[0]):
        out_ref[copy] = block_ref[...]


def repeat(block, copies):
    whole = pl.BlockSpec(memory_space=pltpu.VMEM)
    return pl.pallas_call(
        repeat_kernel,
        out_shape=jax.ShapeDtypeStruct((copies,) + block.shape, block.dtype),
        in_specs=[whole],
        out_specs=whole,
        compiler_params=pltpu.CompilerParams(vmem_limit_bytes=12 * 2**20),
        cost_estimate=small_cost(0, 2 * (copies + 1) * block.size),
    )(block)


def project_kernel(core_ref, hidden_ref, gain_ref, query_ref, keyval_ref, *refs):
    got_ref = refs[0] if len(refs) == 2 else None
    out_ref = refs[-1]
    blocks, _, local_rows, features = hidden_ref.shape
    rows = blocks * local_rows
    values = hidden_ref[:, core_ref[0]].reshape(rows, features).astype(f32)
    total = jnp.sum(values * values, 1, keepdims=True)
    gained = (values * gain_ref[...]).astype(bf16)
    query_cols = query_ref.shape[1]
    key_cols = keyval_ref.shape[2]
    width = query_cols + 2 * key_cols
    extra = out_ref.shape[1] - width

    def put(part, sums):
        if got_ref is not None:
            sums = sums + got_ref[:, part].astype(f32)
        out_ref[:, part] = sums.astype(bf16)

    put(slice(0, query_cols), jnp.dot(gained, query_ref[...], preferred_element_type=f32))
    for half in range(2):
        start = query_cols + half * key_cols
        sums = jnp.dot(gained, keyval_ref[:, half, :], preferred_element_type=f32)
        put(slice(start, start + key_cols), sums)
    if got_ref is not None:
        parts = got_ref[:, width:].astype(f32)
        total = total + parts[:, 0:1] + parts[:, 1:2]
    high = total.astype(bf16).astype(f32)
    column = lax.broadcasted_iota(jnp.int32, (rows, extra), 1)
    squares = jnp.where(column == 0, high, jnp.where(column == 1, total - high, 0.0))
    out_ref[:, width:] = squares.astype(bf16)


def project(core, hidden, gain, w_query, w_keyval, got, limit):
    blocks, _, local_rows, features = hidden.shape
    rows = blocks * local_rows
    width = w_query.shape[1] + w_keyval.shape[1] * w_keyval.shape[2] + 128
    operands = [hidden, gain, w_query, w_keyval] + ([] if got is None else [got])
    whole = pl.BlockSpec(memory_space=pltpu.VMEM)
    return pl.pallas_call(
        project_kernel,
        out_shape=jax.ShapeDtypeStruct((rows, width), bf16),
        in_specs=[pl.BlockSpec(memory_space=pltpu.SMEM)] + [whole] * len(operands),
        out_specs=whole,
        compiler_params=pltpu.CompilerParams(vmem_limit_bytes=limit * 2**20),
        cost_estimate=pl.CostEstimate(
            flops=2 * rows * width * features, bytes_accessed=4 * rows * width, transcendentals=0
        ),
    )(core.reshape(1).astype(jnp.int32), *operands)


def pick_kernel(pick_ref, *refs):
    blocks, outs = refs[:NY], refs[NY:]
    held = blocks[0].shape[0]
    rows = outs[0].shape[1]
    for part, out_ref in enumerate(outs):
        lines = slice(part * rows, (part + 1) * rows)
        total = None
        for quarter, block in enumerate(blocks):
            chosen = pick_ref[lines, quarter * held : (quarter + 1) * held]
            product = jnp.dot(chosen, block[...], preferred_element_type=f32)
            total = product if total is None else total + product
        out_ref[0] = total.astype(bf16)


def pick_rows(pick, blocks):
    whole = pl.BlockSpec(memory_space=pltpu.VMEM)
    shape = (1, pick.shape[0] // PARTS, blocks[0].shape[1])
    return pl.pallas_call(
        pick_kernel,
        out_shape=[jax.ShapeDtypeStruct(shape, bf16)] * PARTS,
        in_specs=[whole] * (1 + len(blocks)),
        out_specs=[whole] * PARTS,
        compiler_params=pltpu.CompilerParams(vmem_limit_bytes=12 * 2**20),
        cost_estimate=small_cost(2 * pick.size * blocks[0].shape[1], pick.size * 4),
    )(pick, *blocks)


def join_kernel(*refs):
    ins, outs = refs[: 2 * PARTS], refs[2 * PARTS :]
    count = ins[0].shape[0]
    for part in range(PARTS):
        for half in range(2):
            value = ins[2 * part + half][...]
            lines = slice(half * count, (half + 1) * count)
            outs[part][lines] = value
            if len(outs) > PARTS:
                outs[PARTS][part, lines] = value


def join(pairs, together):
    whole = pl.BlockSpec(memory_space=pltpu.VMEM)
    count, *rest = pairs[0][0].shape
    shapes = [jax.ShapeDtypeStruct((2 * count, *rest), bf16)] * PARTS
    if together:
        shapes.append(jax.ShapeDtypeStruct((PARTS, 2 * count, *rest), bf16))
    return pl.pallas_call(
        join_kernel,
        out_shape=shapes,
        in_specs=[whole] * (2 * PARTS),
        out_specs=[whole] * len(shapes),
        compiler_params=pltpu.CompilerParams(vmem_limit_bytes=12 * 2**20),
        cost_estimate=small_cost(0, 16 * PARTS * pairs[0][0].size),
    )(*(half for pair in pairs for half in pair))


def guide_kernel(shares_ref, place_ref, *refs):
    ins, outs = refs[: 2 * PARTS], refs[2 * PARTS :]
    devices, held = shares_ref.shape
    total = jnp.sum(shares_ref[...].reshape(devices // NY, NY, held), 0)
    scale = lax.rsqrt(total / D + EPSILON)
    place = place_ref[...]
    lane = lax.broadcasted_iota(jnp.int32, (place.shape[0], held), 1)
    chosen = jnp.zeros((place.shape[0], held), f32)
    for quarter in range(NY):
        here = lane + quarter * held == place
        chosen = chosen + jnp.where(here, scale[quarter : quarter + 1, :], 0.0)
    chosen = jnp.sum(chosen, 1, keepdims=True)
    rows = ins[0].shape[1]
    half = rows // 2
    for part in range(PARTS):
        kept = GUIDANCE * chosen[part * rows : part * rows + half]
        taken = (GUIDANCE - 1.0) * chosen[part * rows + half : (part + 1) * rows]
        for slot in range(outs[part].shape[0]):
            ref = ins[2 * part + slot // 2]
            both = kept * ref[slot % 2, :half, :].astype(f32)
            both = both - taken * ref[slot % 2, half:, :].astype(f32)
            outs[part][slot] = both.astype(bf16)


def guide_pairs(shares, place, pairs):
    _, rows, features = pairs[0][0].shape
    whole = pl.BlockSpec(memory_space=pltpu.VMEM)
    return pl.pallas_call(
        guide_kernel,
        out_shape=[jax.ShapeDtypeStruct((4, rows // 2, features), bf16)] * PARTS,
        in_specs=[whole] * (2 + 2 * PARTS),
        out_specs=[whole] * PARTS,
        compiler_params=pltpu.CompilerParams(vmem_limit_bytes=12 * 2**20),
        cost_estimate=small_cost(0, 16 * PARTS * pairs[0][0].size),
    )(shares, place, *(half for pair in pairs for half in pair))


def vocab_kernel(count, places, w_ref, *refs):
    near, far, near_later, far_later = (
        refs[:PARTS],
        refs[PARTS],
        refs[PARTS + 1 : 2 * PARTS + 1],
        refs[2 * PARTS + 1 : 3 * PARTS + 1],
    )
    words_ref, out_ref, share_ref, top_ref, sum_ref = refs[3 * PARTS + 1 :]
    features = near[0].shape[2]
    early = near[0].shape[0]

    def piece(core, part, slot):
        if slot >= early:
            return (far_later if core else near_later)[part][slot - early]
        return far[part, slot] if core else near[part][slot]

    total = None
    for core in range(NC):
        for distance in range(NX * NZ):
            start = pl.multiple_of(places[1 + core * NX * NZ + distance], features)
            held = [piece(core, part, slot_of(part, distance)) for part in range(PARTS)]
            product = lax.dot_general(
                w_ref[:, pl.ds(start, features)],
                jnp.concatenate(held, 0),
                (((1,), (1,)), ((), ())),
                preferred_element_type=f32,
            )
            total = product if total is None else total + product
    step = pl.program_id(0)
    rows, pairs = total.shape
    words = words_ref[...]
    words = jnp.broadcast_to(words[:, None, :], (words.shape[0], WORD_BITS, pairs))
    words = words.reshape(rows, pairs)
    row = lax.broadcasted_iota(jnp.int32, total.shape, 0)
    place = step * rows + row
    bit = lax.shift_right_logical(words, row & (WORD_BITS - 1)) & 1
    allowed = ((bit == 1) | (places[0] + place == 0)) & (place < count)
    masked = jnp.where(allowed, total, SENTINEL)
    out_ref[...] = masked

    @pl.when(step == 0)
    def _():
        top_ref[...] = jnp.full_like(top_ref, SENTINEL)
        sum_ref[...] = jnp.zeros_like(sum_ref)

    before = top_ref[...]
    top = jnp.maximum(before, jnp.max(masked, 0, keepdims=True))
    summed = sum_ref[...] * jnp.exp(before - top) + jnp.sum(
        jnp.where(allowed, jnp.exp(masked - top), 0.0), 0, keepdims=True
    )
    top_ref[...] = top
    sum_ref[...] = summed

    @pl.when(step == pl.num_programs(0) - 1)
    def _():
        share_ref[...] = jnp.where(
            summed > 0.0, top + jnp.log(jnp.maximum(summed, 1e-30)), SENTINEL
        )


def vocab_logits(places, w_rows, near, far, near_later, far_later, grammar_rows):
    count, depth = w_rows.shape
    pairs = PARTS * near[0].shape[1]
    blocks = [*near, far, *near_later, *far_later]

    def whole(block):
        return pl.BlockSpec(
            block.shape, lambda i, s: (0,) * block.ndim, pipeline_mode=pl.Buffered(1)
        )

    part = pl.BlockSpec((VOCAB_ROWS, pairs), lambda i, s: (i, 0))
    return pl.pallas_call(
        functools.partial(vocab_kernel, count),
        out_shape=(
            jax.ShapeDtypeStruct((count, pairs), f32),
            jax.ShapeDtypeStruct((1, pairs), f32),
        ),
        grid_spec=pltpu.PrefetchScalarGridSpec(
            num_scalar_prefetch=1,
            grid=(pl.cdiv(count, VOCAB_ROWS),),
            in_specs=[
                pl.BlockSpec((VOCAB_ROWS, depth), lambda i, s: (i, 0)),
                *(whole(block) for block in blocks),
                pl.BlockSpec((VOCAB_ROWS // WORD_BITS, pairs), lambda i, s: (i, 0)),
            ],
            out_specs=(part, pl.BlockSpec((1, pairs), lambda i, s: (0, 0))),
            scratch_shapes=[pltpu.VMEM((1, pairs), f32), pltpu.VMEM((1, pairs), f32)],
        ),
        compiler_params=pltpu.CompilerParams(vmem_limit_bytes=48 * 2**20),
        cost_estimate=pl.CostEstimate(
            flops=2 * count * pairs * depth, bytes_accessed=2 * count * depth, transcendentals=0
        ),
    )(places, w_rows, *blocks, grammar_rows)


def local(
    hidden_in,
    gain_attn,
    w_query,
    w_keyval,
    w_out,
    key_cache,
    value_cache,
    lengths,
    gain_final,
    w_vocab,
    pair_rows,
    grammar,
):
    local_rows = lengths.shape[0]
    row_count, features = hidden_in.shape
    query_cols = w_query.shape[1]
    group_count = w_keyval.shape[2] // HD
    x, z, c, y = (lax.axis_index(axis) for axis in ALL)
    pair_count = row_count // 2

    hidden_blocks = hidden_in.reshape(NX * NZ, NC, local_rows, features)
    gain_row = gain_attn.reshape(1, features)
    width = query_cols + w_keyval.shape[1] * w_keyval.shape[2]
    mine = project(1 - c, hidden_blocks, gain_row, w_query, w_keyval, None, 56)
    mine = project(c, hidden_blocks, gain_row, w_query, w_keyval, shift(mine, "c", 1), 24)
    mine = lax.all_to_all(mine.reshape(NX * NZ, local_rows, -1), ("x", "z"), 0, 0)
    mine = jnp.sum(mine.astype(f32), 0)
    projected = mine * lax.rsqrt(row_total(mine, width) / D + EPSILON)

    halves = HD // 2
    frequency = ROPE_BASE ** (-2.0 * jnp.arange(halves, dtype=f32) / HD)
    angles = lengths.astype(f32)[:, None] * frequency[None, :]
    cosine = jnp.cos(angles)[:, None, :]
    sin_part = jnp.sin(angles)[:, None, :]
    queries = rotate(
        projected[:, :query_cols].reshape(local_rows, query_cols // HD, HD), cosine, sin_part
    ).astype(bf16)
    kv_pairs = projected[:, query_cols:width].reshape(local_rows, 2, group_count, HD)
    new_key = rotate(kv_pairs[:, 0], cosine, sin_part).astype(bf16)
    new_value = kv_pairs[:, 1].astype(bf16)
    attended = attend(queries, new_key, new_value, key_cache, value_cache, lengths)

    share = local_rows // NY
    blocks = repeat(attended.reshape(NY, share, query_cols), NX * NZ)
    near = lax.all_to_all(blocks.reshape(-1, share, query_cols), ("x", "z", "y"), 0, 0)
    near, weights = lax.optimization_barrier((near, load(w_out, attended, 48 * 2**20)))
    near = near.reshape(NX * NZ, NY, share, query_cols).transpose(0, 2, 1, 3)
    near = near.reshape(NX * NZ * share, D)
    far = shift(near, "c", 1)
    near = jnp.dot(near, weights, preferred_element_type=f32)
    far = jnp.dot(far, weights, preferred_element_type=f32)
    update = jnp.concatenate([jnp.where(c == 0, near, far), jnp.where(c == 0, far, near)], 0)

    hidden_here = lax.dynamic_index_in_dim(
        hidden_in.reshape(NX * NZ, NC, NY, share, features), y, 2, False
    )
    hidden_here = hidden_here.transpose(1, 0, 2, 3).reshape(-1, features)
    residual = (hidden_here.astype(f32) + update).astype(bf16)
    rounded = residual.astype(f32)
    held = residual.shape[0]
    scaled = (rounded * gain_final).astype(bf16)
    got = {by: shift(scaled, "y", by) for by in SHIFTS}
    quarters = jnp.arange(NY, dtype=jnp.int32)

    def rows_of(order):
        row = (
            jnp.arange(NX * NZ, dtype=jnp.int32)[None, None, :, None] * NC
            + jnp.arange(NC, dtype=jnp.int32)[None, :, None, None]
        ) * local_rows
        row = row + order[:, None, None, None] * share
        return (row + jnp.arange(share, dtype=jnp.int32)).reshape(-1)

    grid = pair_rows.reshape(PARTS, pair_count // PARTS, 2).transpose(0, 2, 1).reshape(-1, 1)
    pick = (grid == rows_of((y - quarters + NY) % NY)[None, :]).astype(bf16)
    order = jnp.arange(row_count, dtype=jnp.int32)
    place = jnp.sum(jnp.where(grid == rows_of(quarters)[None, :], order[None, :], 0), 1)

    parts = pick_rows(pick, [scaled, got[1], got[2], got[3]])
    shares = lax.all_to_all(
        jnp.broadcast_to(jnp.sum(rounded * rounded, 1), (NX * NZ * NC * NY, held)), ALL, 0, 0
    )
    parts = join([(part, swap(part, i, 0)) for i, part in enumerate(parts)], False)
    parts = [(part, swap(part, i, 1)) for i, part in enumerate(parts)]
    shares, first = lax.optimization_barrier((shares, parts[0][1]))
    parts[0] = (parts[0][0], first)
    parts = guide_pairs(shares, place[:, None], parts)
    *near, together = join([(part, swap(part, i, 2)) for i, part in enumerate(parts)], True)
    far = shift(together, "c", 1)
    near_later = [swap(part, i, 3) for i, part in enumerate(near)]
    far_later = [shift(part, "c", 1) for part in near_later]

    columns = []
    for core in range(NC):
        for distance in range(NX * NZ):
            where = {"x": x, "z": z}
            for bit, (axis, by) in enumerate(SWAPS):
                if distance >> bit & 1:
                    where[axis] = where[axis] ^ by
            columns.append(((where["x"] * NZ + where["z"]) * NC + (c + core) % NC) * features)
    offset = lax.axis_index(ALL) * w_vocab.shape[1]
    guided = vocab_logits(
        jnp.stack([offset, *columns]).astype(jnp.int32),
        w_vocab.T,
        near,
        far,
        near_later,
        far_later,
        grammar.T,
    )
    masked, shares = guided
    shares = lax.all_to_all(
        jnp.broadcast_to(shares[0], (NX * NZ * NC * NY, pair_count)), ALL, 0, 0
    )
    highest = jnp.max(shares, 0)
    total = highest + jnp.log(jnp.sum(jnp.exp(shares - highest), 0))
    return jnp.where(masked > 0.5 * SENTINEL, masked - total[None, :], 0.0).T


def solution(mesh):
    split = Mesh(mesh.devices.reshape(NX, NZ, NC, NY), ALL)
    in_specs = (
        P(None, DP),
        P(DP),
        P(DP, "y"),
        P(DP, None, "y"),
        P(None, DP),
        P(DP, "y", None, None),
        P(DP, "y", None, None),
        P(DP),
        P(DP),
        P(None, ALL),
        P(),
        P(None, ALL),
    )
    out_specs = P(None, ALL)
    return jax.shard_map(local, mesh=split, in_specs=in_specs, out_specs=out_specs, check_vma=False)
```

time: 173 us -> 166 us (0.960)
  local copies, waits for them, and re-layouts: 25.3 us -> 8.31 us
  starting transfers between devices: 41.9 us -> 54.2 us
  waiting for transfers between devices: 56.8 us -> 52.3 us
  blocking collectives: 18.2 us -> 15.6 us
  Pallas kernels: 19 us -> 21.2 us
    unnamed x49 -> x35, local copies, waits for them, and re-layouts: 20.6 us -> 5.59 us
    ppermute x15 -> x10, waiting for transfers between devices: 21.7 us -> 7.73 us  [shift(): lax.ppermute(value, axis, [(i, (i + by) % size) for i in range(size)])]
    ppermute x0 -> x16, starting transfers between devices: none -> 13.7 us  [swap(): lax.ppermute(value, axis, [(i, i ^ by) for i in range(lax.axis_size(axis))])]
    ppermute x0 -> x16, waiting for transfers between devices: none -> 10.1 us  [swap(): lax.ppermute(value, axis, [(i, i ^ by) for i in range(lax.axis_size(axis))])]
    pallas_call x2 -> x1, Pallas kernels: 7.9 us -> 2.2 us  [load(): pl.pallas_call(load_kernel, out_shape=pltpu.VMEM(weights.shape, weights.d...]
    ppermute x15 -> x10, starting transfers between devices: 19.9 us -> 14.8 us  [shift(): lax.ppermute(value, axis, [(i, (i + by) % size) for i in range(size)])]
    pallas_call x4 -> x6, Pallas kernels: 8.96 us -> 13.3 us  [the longest x1 10.2 us: vocab_logits(): pl.pallas_call(functools.partial(vocab_kernel, count), out_shape=(jax.Sha...]
    all_to_all x1, starting transfers between devices: 5.79 us -> 9.61 us  [local(): lax.all_to_all(jnp.broadcast_to(jnp.sum(rounded * rounded, 1), (NX * NZ *...]
  transfers between devices with their start and end apart: 18 -> 29, of which waited for: 9 -> 14; matrix products, arithmetic and copies ran while one was open for 4% -> 4% of each run, Pallas kernels for 8% -> 1%
where the time goes in v2:
time: 166 us; the launch traced here: 165 us
  starting transfers between devices  54.2 us (33%)
  waiting for transfers between devices  52.3 us (32%)
  Pallas kernels  21.2 us (13%)
  blocking collectives  15.6 us (9%)
  local copies, waits for them, and re-layouts  8.31 us (5%)
  matrix products  6.99 us (4%)
  other arithmetic  5.84 us (4%)
    all_to_all x1, waiting for transfers between devices, local(): lax.all_to_all(mine.reshape(NX * NZ, local_rows, -1), ('x', 'z'), 0, 0)  19.1 us
    all_to_all x1, blocking collectives, local(): lax.all_to_all(jnp.broadcast_to(shares[0], (NX * NZ * NC * NY, pair_count...  15.6 us
    ppermute x10, starting transfers between devices, shift(): lax.ppermute(value, axis, [(i, (i + by) % size) for i in range(size)])  14.8 us
    ppermute x16, starting transfers between devices, swap(): lax.ppermute(value, axis, [(i, i ^ by) for i in range(lax.axis_size(axis))])  13.7 us
    all_to_all x1, waiting for transfers between devices, local(): lax.all_to_all(blocks.reshape(-1, share, query_cols), ('x', 'z', 'y'), 0, 0)  12.1 us
    pallas_call x1, Pallas kernels, vocab_logits(): pl.pallas_call(functools.partial(vocab_kernel, count), out_shape=(jax.Sha...  10.2 us
    ppermute x16, waiting for transfers between devices, swap(): lax.ppermute(value, axis, [(i, i ^ by) for i in range(lax.axis_size(axis))])  10.1 us
    all_to_all x1, starting transfers between devices, local(): lax.all_to_all(jnp.broadcast_to(jnp.sum(rounded * rounded, 1), (NX * NZ *...  9.61 us
  transfers between devices with their start and end apart: 29, of which 14 were waited for; matrix products, arithmetic and copies ran while one was open for 4% of the time, Pallas kernels for 1%

profile of v2, /device:TPU:1, one launch (start us, length us, event | category | flops | bytes accessed | tf_op | source)
XLA Modules:
  0.0 165.0 jit_solution(18376773315518336427)
XLA Ops:
  0.0 3.6 %shard_map.118 = bf16[256,2688]{1,0:T(8,128)(2,1)} custom-call(s32[1]{0:T(128)} %bitcast.39.core_ref, bf16[16,2,16,256]{3,2,1,0:T(8,128)(2,1)} %bitcast.106, f32[1,256]{1,0:T(1,128)} %bitcast.111, bf16[256,2048]{1,0:T(8,128)(2,1)} %query_ref.3, bf16[256,2,256]{2,1,0:T(2,128)(2,1)} %keyval_ref.3), custom_call_target="tpu_custom_call" | custom-call | flops 352321536 | bytes 2752512 | tf_op jit(solution)/shard_map/pallas_call | solution.py:167
  3.6 1.4 collective-permute-start
  5.1 3.0 %collective-permute-done.refs_0_ = bf16[256,2688]{1,0:T(8,128)(2,1)S(1)} collective-permute-done((bf16[256,2688]{1,0:T(8,128)(2,1)}, bf16[256,2688]{1,0:T(8,128)(2,1)S(1)}, u32[]{:S(2)}, u32[]{:S(2)}) %collective-permute-start) | collective-permute-done | bytes 1376288 | tf_op jit(solution)/shard_map/ppermute | solution.py:32
  8.0 2.2 %shard_map.119 = bf16[256,2688]{1,0:T(8,128)(2,1)} custom-call(s32[1]{0:T(128)} %bitcast.36.core_ref, bf16[16,2,16,256]{3,2,1,0:T(8,128)(2,1)S(1)} %bitcast.107, f32[1,256]{1,0:T(1,128)S(1)} %bitcast.112, bf16[256,2048]{1,0:T(8,128)(2,1)S(1)} %copy-done.3, bf16[256,2,256]{2,1,0:T(2,128)(2,1)S(1)} %copy-done.5, bf16[256,2688]{1,0:T(8,128)(2,1)S(1)} %collective-permute-done.refs_0_), custom_call_target="tpu_custom_call" | custom-call | flops 352321536 | bytes 2752512 | tf_op jit(solution)/shard_map/pallas_call | solution.py:167
  10.2 7.9 %all-to-all-start = ((bf16[16,16,2688]{2,1,0:T(8,128)(2,1)}), bf16[16,16,2688]{2,1,0:T(8,128)(2,1)}, u32[]{:S(2)}, u32[]{:S(2)}) async-start(bf16[16,16,2688]{2,1,0:T(8,128)(2,1)} %bitcast.40), calls=%async_computation | async-start | bytes 2752512 | tf_op jit(solution)/shard_map/all_to_all | solution.py:392
  18.3 19.1 %all-to-all-done = bf16[16,16,2688]{2,1,0:T(8,128)(2,1)} async-done(((bf16[16,16,2688]{2,1,0:T(8,128)(2,1)}), bf16[16,16,2688]{2,1,0:T(8,128)(2,1)}, u32[]{:S(2)}, u32[]{:S(2)}) %all-to-all-start) | async-done | bytes 1376288 | tf_op jit(solution)/shard_map/all_to_all | solution.py:392
  37.5 1.5 convert_reduce_fusion
  39.7 0.2 fusion.11
  40.0 1.0 fusion.26
  41.0 0.2 fusion.2
  41.3 0.6 fusion.1
  41.9 1.1 shard_map.120
  43.0 8.2 %all-to-all-start.1 = ((bf16[64,4,2048]{2,1,0:T(4,128)(2,1)}), bf16[64,4,2048]{2,1,0:T(4,128)(2,1)S(1)}, u32[]{:S(2)}, u32[]{:S(2)}) async-start(bf16[64,4,2048]{2,1,0:T(4,128)(2,1)} %bitcast.48), calls=%async_computation.1 | async-start | bytes 2097152 | tf_op jit(solution)/shard_map/all_to_all | solution.py:411
  51.4 2.2 %shard_map.121 = bf16[8192,256]{1,0:T(8,128)(2,1)S(1)} custom-call(bf16[8192,256]{1,0:T(8,128)(2,1)} %w_ref.1, bf16[16,2048]{1,0:T(8,128)(2,1)S(1)} %bitcast.108), custom_call_target="tpu_custom_call" | custom-call | bytes 8388608 | tf_op jit(solution)/shard_map/pallas_call | solution.py:99
  53.6 2.0 %copy-done.1 = bf16[8192,256]{1,0:T(8,128)(2,1)} copy-done((bf16[8192,256]{1,0:T(8,128)(2,1)}, bf16[8192,256]{1,0:T(8,128)(2,1)S(1)}, u32[]{:S(2)}) %copy-start.1) | copy-done | bytes 4194328
  55.5 12.1 %all-to-all-done.1 = bf16[64,4,2048]{2,1,0:T(4,128)(2,1)S(1)} async-done(((bf16[64,4,2048]{2,1,0:T(4,128)(2,1)}), bf16[64,4,2048]{2,1,0:T(4,128)(2,1)S(1)}, u32[]{:S(2)}, u32[]{:S(2)}) %all-to-all-start.1) | async-done | bytes 1048608 | tf_op jit(solution)/shard_map/all_to_all | solution.py:411
  67.6 0.9 copy.57
  68.5 0.6 copy.70
  69.1 3.2 %collective-permute-start.1 = (bf16[64,8192]{1,0:T(8,128)(2,1)S(1)}, bf16[64,8192]{1,0:T(8,128)(2,1)}, u32[]{:S(2)}, u32[]{:S(2)}) collective-permute-start(bf16[64,8192]{1,0:T(8,128)(2,1)S(1)} %bitcast.117), channel_id=1, source_target_pairs={{0,4},{4,0},{1,5},{5,1},{2,6},{6,2},{3,7},{7,3},{8,12},{12,8},{9,1... | collective-permute-start | bytes 3145736 | tf_op jit(solution)/shard_map/ppermute | solution.py:32
  73.0 3.1 %fusion.27 = f32[64,256]{1,0:T(8,128)S(1)} fusion(bf16[64,8192]{1,0:T(8,128)(2,1)S(1)} %bitcast.118, bf16[8192,256]{1,0:T(8,128)(2,1)} %copy-done.1), kind=kOutput, calls=%fused_computation.76 | convolution fusion | flops 268435456 | bytes 5308416 | tf_op jit(solution)/shard_map/dot_general | solution.py:416
  76.2 0.3 copy-done.2
  76.5 2.0 %broadcast_select_fusion.1 = (f32[64,256]{1,0:T(8,128)S(1)}, f32[64,256]{1,0:T(8,128)S(1)}) fusion(f32[64,256]{1,0:T(8,128)S(1)} %fusion.27, pred[]{:T(512)S(6)} %eq.65, bf16[64,8192]{1,0:T(8,128)(2,1)} %collective-permute-done.1, bf16[8192,256]{1,0:T(8,128)(2,1)S(1)} %copy-done.2), kind=kOutput, calls=%fused_computation.36 | convolution fusion | flops 268468224 | bytes 5439489 | tf_op jit(solution)/shard_map/dot_general | solution.py:417
  78.5 0.6 collective-permute-start.2
  79.2 1.2 collective-permute-start.3
  80.4 1.4 collective-permute-start.4
  82.1 2.8 %collective-permute-done.2.refs_1_ = bf16[128,256]{1,0:T(8,128)(2,1)S(1)} collective-permute-done((bf16[128,256]{1,0:T(8,128)(2,1)S(1)}, bf16[128,256]{1,0:T(8,128)(2,1)S(1)}, u32[]{:S(2)}, u32[]{:S(2)}) %collective-permute-start.2) | collective-permute-done | bytes 65568 | tf_op jit(solution)/shard_map/ppermute | solution.py:32
  84.9 0.3 collective-permute-done.4.refs_3_
  85.2 0.4 shard_map.122
  85.6 0.2 collective-permute-start.5
  85.8 0.9 collective-permute-start.6
  86.7 0.4 collective-permute-start.7
  87.2 0.6 collective-permute-start.8
  88.0 0.7 broadcast_in_dim.73
  88.7 9.6 %all-to-all-start.2 = ((f32[128,1,128]{2,1,0:T(1,128)}), f32[128,1,128]{2,1,0:T(1,128)S(1)}, u32[]{:S(2)}, u32[]{:S(2)}) async-start(f32[128,1,128]{2,1,0:T(1,128)} %broadcast_in_dim.73), calls=%async_computation.2 | async-start | bytes 131072 | tf_op jit(solution)/shard_map/all_to_all | solution.py:445
  98.4 2.7 %collective-permute-start.9 = (bf16[2,128,256]{2,1,0:T(8,128)(2,1)S(1)}, bf16[2,128,256]{2,1,0:T(8,128)(2,1)S(1)}, u32[]{:S(2)}, u32[]{:S(2)}) collective-permute-start(bf16[2,128,256]{2,1,0:T(8,128)(2,1)S(1)} %get-tuple-element.34.refs_0_), channel_id=1, source_target_pairs={{0,96},{32,64},{64,32},{96,0},{1,97},{33,65},{65,33},{97,1},{2,98}... | collective-permute-start | bytes 393224 | tf_op jit(solution)/shard_map/ppermute | solution.py:37
  101.1 1.4 collective-permute-start.10
  102.4 2.1 %collective-permute-start.11 = (bf16[2,128,256]{2,1,0:T(8,128)(2,1)S(1)}, bf16[2,128,256]{2,1,0:T(8,128)(2,1)S(1)}, u32[]{:S(2)}, u32[]{:S(2)}) collective-permute-start(bf16[2,128,256]{2,1,0:T(8,128)(2,1)S(1)} %get-tuple-element.38.refs_4_), channel_id=1, source_target_pairs={{0,24},{8,16},{16,8},{24,0},{1,25},{9,17},{17,9},{25,1},{2,26},{10... | collective-permute-start | bytes 393224 | tf_op jit(solution)/shard_map/ppermute | solution.py:37
  104.5 0.2 select_reduce_fusion
  104.9 3.2 %all-to-all-done.2 = f32[128,1,128]{2,1,0:T(1,128)S(1)} async-done(((f32[128,1,128]{2,1,0:T(1,128)}), f32[128,1,128]{2,1,0:T(1,128)S(1)}, u32[]{:S(2)}, u32[]{:S(2)}) %all-to-all-start.2) | async-done | bytes 65568 | tf_op jit(solution)/shard_map/all_to_all | solution.py:445
  108.1 0.5 collective-permute-done.12.refs_7_
  108.6 0.4 shard_map.124
  109.0 0.6 collective-permute-start.13
  109.6 0.6 collective-permute-start.14
  110.4 0.9 collective-permute-start.16
  111.3 1.6 collective-permute-done.13.refs_1_
  112.9 1.8 %collective-permute-done.14.refs_3_ = bf16[4,64,256]{2,1,0:T(8,128)(2,1)S(1)} collective-permute-done((bf16[4,64,256]{2,1,0:T(8,128)(2,1)S(1)}, bf16[4,64,256]{2,1,0:T(8,128)(2,1)S(1)}, u32[]{:S(2)}, u32[]{:S(2)}) %collective-permute-start.14) | collective-permute-done | bytes 131104 | tf_op jit(solution)/shard_map/ppermute | solution.py:37
  114.7 0.8 collective-permute-done.16.refs_7_
  115.4 1.1 shard_map.125
  116.5 3.6 %collective-permute-start.17 = (bf16[4,8,64,256]{3,2,1,0:T(8,128)(2,1)}, bf16[4,8,64,256]{3,2,1,0:T(8,128)(2,1)S(1)}, u32[]{:S(2)}, u32[]{:S(2)}) collective-permute-start(bf16[4,8,64,256]{3,2,1,0:T(8,128)(2,1)} %get-tuple-element.48), channel_id=1, source_target_pairs={{0,4},{4,0},{1,5},{5,1},{2,6},{6,2},{3,7},{7,3},{8,12},{12,8},{9,1... | collective-permute-start | bytes 3145736 | tf_op jit(solution)/shard_map/ppermute | solution.py:32
  120.2 2.3 %collective-permute-start.18 = (bf16[8,64,256]{2,1,0:T(8,128)(2,1)S(1)}, bf16[8,64,256]{2,1,0:T(8,128)(2,1)}, u32[]{:S(2)}, u32[]{:S(2)}) collective-permute-start(bf16[8,64,256]{2,1,0:T(8,128)(2,1)S(1)} %get-tuple-element.44.refs_0_), channel_id=1, source_target_pairs={{0,24},{8,16},{16,8},{24,0},{1,25},{9,17},{17,9},{25,1},{2,26},{10... | collective-permute-start | bytes 786440 | tf_op jit(solution)/shard_map/ppermute | solution.py:37
  122.5 0.3 collective-permute-start.19
  122.8 0.6 collective-permute-start.20
  123.3 0.7 copy-done.7
  124.0 5.4 %collective-permute-done.18.refs_5_ = bf16[8,64,256]{2,1,0:T(8,128)(2,1)} collective-permute-done((bf16[8,64,256]{2,1,0:T(8,128)(2,1)S(1)}, bf16[8,64,256]{2,1,0:T(8,128)(2,1)}, u32[]{:S(2)}, u32[]{:S(2)}) %collective-permute-start.18) | collective-permute-done | bytes 262176 | tf_op jit(solution)/shard_map/ppermute | solution.py:37
  129.4 0.8 collective-permute-start.22
  130.2 1.1 collective-permute-start.23
  131.4 1.4 collective-permute-start.24
  132.9 1.4 collective-permute-done.24.refs_11_
  134.3 0.4 collective-permute-done.25.refs_12_
  134.7 0.9 copy-done.8
  135.6 10.2 %shard_map.126 = (f32[1002,256]{1,0:T(8,128)S(1)}, f32[1,256]{1,0:T(1,128)S(1)}) custom-call(s32[33]{0:T(128)S(1)} %stack.135.places, bf16[1002,8192]{1,0:T(8,128)(2,1)} %bitcast.114, bf16[8,64,256]{2,1,0:T(8,128)(2,1)S(1)} %get-tuple-element.44.refs_0_, bf16[8,64,256]{2,1,0:T(8,128)(2,1)S(1)} %get-tuple-element.45.refs_1_, ...), custom_call_target="tpu_custom_call" | custom-call | flops 4202692608 | bytes 16416768 | tf_op jit(solution)/shard_map/pallas_call | solution.py:342
  145.9 1.0 copy-done.6
  146.9 15.6 %all_to_all.28 = f32[128,1,256]{2,1,0:T(1,128)S(1)} all-to-all(f32[128,1,256]{2,1,0:T(1,128)S(1)} %broadcast_in_dim.77), channel_id=1, replica_groups=mesh['x'=4,'z'=4,'c'=2,'y'=4] {'x','z','c','y'}, dimensions={0} | all-to-all | bytes 262144 | tf_op jit(solution)/shard_map/all_to_all | solution.py:477
  162.7 2.3 %select_bitcast_fusion = f32[256,1002]{0,1:T(8,128)} fusion(f32[1002,256]{1,0:T(8,128)} %copy-done.6, f32[256]{0:T(256)S(1)} %log_add_fusion), kind=kLoop, calls=%fused_computation.7 | loop fusion | flops 769536 | bytes 2053120 | tf_op jit(solution)/shard_map/transpose | solution.py:482
  (91 shorter events, 3.1 us)
Async XLA Ops:
  0.0 40.0 %copy-start = (bf16[16,2,192,128]{3,2,1,0:T(8,128)(2,1)S(1)}, bf16[16,2,192,128]{3,2,1,0:T(8,128)(2,1)}, u32[]{:S(2)}) copy-start(bf16[16,2,192,128]{3,2,1,0:T(8,128)(2,1)} %param.17) | copy-start | bytes 4718596
  0.0 8.0 %copy-start.4 = (bf16[512,256]{1,0:T(8,128)(2,1)S(1)}, bf16[512,256]{1,0:T(8,128)(2,1)}, u32[]{:S(2)}) copy-start(bf16[512,256]{1,0:T(8,128)(2,1)} %param.12) | copy-start | bytes 786436
  0.0 8.0 %copy-start.10 = (f32[256]{0:T(256)S(1)}, f32[256]{0:T(256)}, u32[]{:S(2)}) copy-start(f32[256]{0:T(256)} %param.13) | copy-start | bytes 3076
  0.0 8.0 %copy-start.3 = (bf16[256,2048]{1,0:T(8,128)(2,1)S(1)}, bf16[256,2048]{1,0:T(8,128)(2,1)}, u32[]{:S(2)}) copy-start(bf16[256,2048]{1,0:T(8,128)(2,1)} %query_ref.3) | copy-start | bytes 3145732
  0.0 8.0 %copy-start.5 = (bf16[256,2,256]{2,1,0:T(2,128)(2,1)S(1)}, bf16[256,2,256]{2,1,0:T(2,128)(2,1)}, u32[]{:S(2)}) copy-start(bf16[256,2,256]{2,1,0:T(2,128)(2,1)} %keyval_ref.3) | copy-start | bytes 786436
  3.6 4.4 %collective-permute-start = (bf16[256,2688]{1,0:T(8,128)(2,1)}, bf16[256,2688]{1,0:T(8,128)(2,1)S(1)}, u32[]{:S(2)}, u32[]{:S(2)}) collective-permute-start(bf16[256,2688]{1,0:T(8,128)(2,1)} %shard_map.118), channel_id=1, source_target_pairs={{0,4},{4,0},{1,5},{5,1},{2,6},{6,2},{3,7},{7,3},{8,12},{12,8},{9,1... | collective-permute-start | bytes 4128776 | tf_op jit(solution)/shard_map/ppermute | solution.py:32
  10.2 7.9 %copy-start.13 = (s32[16]{0:T(128)S(1)}, s32[16]{0:T(128)}, u32[]{:S(2)}) copy-start(s32[16]{0:T(128)} %param.19) | copy-start | bytes 196
  10.2 27.3 %all-to-all-start = ((bf16[16,16,2688]{2,1,0:T(8,128)(2,1)}), bf16[16,16,2688]{2,1,0:T(8,128)(2,1)}, u32[]{:S(2)}, u32[]{:S(2)}) async-start(bf16[16,16,2688]{2,1,0:T(8,128)(2,1)} %bitcast.40), calls=%async_computation | async-start | bytes 2752512 | tf_op jit(solution)/shard_map/all_to_all | solution.py:392
  39.4 1.8 %copy-start.14 = (bf16[16,2,192,128]{3,2,1,0:T(8,128)(2,1)S(1)}, bf16[16,2,192,128]{3,2,1,0:T(8,128)(2,1)}, u32[]{:S(2)}) copy-start(bf16[16,2,192,128]{3,2,1,0:T(8,128)(2,1)} %param.18) | copy-start | bytes 4718596
  43.0 24.6 %all-to-all-start.1 = ((bf16[64,4,2048]{2,1,0:T(4,128)(2,1)}), bf16[64,4,2048]{2,1,0:T(4,128)(2,1)S(1)}, u32[]{:S(2)}, u32[]{:S(2)}) async-start(bf16[64,4,2048]{2,1,0:T(4,128)(2,1)} %bitcast.48), calls=%async_computation.1 | async-start | bytes 2097152 | tf_op jit(solution)/shard_map/all_to_all | solution.py:411
  53.6 2.0 %copy-start.1 = (bf16[8192,256]{1,0:T(8,128)(2,1)}, bf16[8192,256]{1,0:T(8,128)(2,1)S(1)}, u32[]{:S(2)}) copy-start(bf16[8192,256]{1,0:T(8,128)(2,1)S(1)} %shard_map.121) | copy-start | bytes 12582916
  68.5 4.2 %copy-start.11 = (s32[512]{0:T(512)S(1)}, s32[512]{0:T(512)}, u32[]{:S(2)}) copy-start(s32[512]{0:T(512)} %param.22) | copy-start | bytes 6148
  69.1 7.0 %collective-permute-start.1 = (bf16[64,8192]{1,0:T(8,128)(2,1)S(1)}, bf16[64,8192]{1,0:T(8,128)(2,1)}, u32[]{:S(2)}, u32[]{:S(2)}) collective-permute-start(bf16[64,8192]{1,0:T(8,128)(2,1)S(1)} %bitcast.117), channel_id=1, source_target_pairs={{0,4},{4,0},{1,5},{5,1},{2,6},{6,2},{3,7},{7,3},{8,12},{12,8},{9,1... | collective-permute-start | bytes 3145736 | tf_op jit(solution)/shard_map/ppermute | solution.py:32
  73.0 3.5 %copy-start.2 = (bf16[8192,256]{1,0:T(8,128)(2,1)S(1)}, bf16[8192,256]{1,0:T(8,128)(2,1)}, u32[]{:S(2)}) copy-start(bf16[8192,256]{1,0:T(8,128)(2,1)} %copy-done.1) | copy-start | bytes 12582916
  76.1 2.4 %copy-start.12 = (f32[256]{0:T(256)S(1)}, f32[256]{0:T(256)}, u32[]{:S(2)}) copy-start(f32[256]{0:T(256)} %param.20) | copy-start | bytes 3076
  78.5 6.4 %collective-permute-start.2 = (bf16[128,256]{1,0:T(8,128)(2,1)S(1)}, bf16[128,256]{1,0:T(8,128)(2,1)S(1)}, u32[]{:S(2)}, u32[]{:S(2)}) collective-permute-start(bf16[128,256]{1,0:T(8,128)(2,1)S(1)} %get-tuple-element.53.refs_0_), channel_id=1, source_target_pairs={{0,1},{1,2},{2,3},{3,0},{4,5},{5,6},{6,7},{7,4},{8,9},{9,10},{10,1... | collective-permute-start | bytes 196616 | tf_op jit(solution)/shard_map/ppermute | solution.py:32
  79.2 5.8 %collective-permute-start.3 = (bf16[128,256]{1,0:T(8,128)(2,1)S(1)}, bf16[128,256]{1,0:T(8,128)(2,1)S(1)}, u32[]{:S(2)}, u32[]{:S(2)}) collective-permute-start(bf16[128,256]{1,0:T(8,128)(2,1)S(1)} %get-tuple-element.53.refs_0_), channel_id=1, source_target_pairs={{0,2},{1,3},{2,0},{3,1},{4,6},{5,7},{6,4},{7,5},{8,10},{9,11},{10,... | collective-permute-start | bytes 196616 | tf_op jit(solution)/shard_map/ppermute | solution.py:32
  80.4 4.8 %collective-permute-start.4 = (bf16[128,256]{1,0:T(8,128)(2,1)S(1)}, bf16[128,256]{1,0:T(8,128)(2,1)S(1)}, u32[]{:S(2)}, u32[]{:S(2)}) collective-permute-start(bf16[128,256]{1,0:T(8,128)(2,1)S(1)} %get-tuple-element.53.refs_0_), channel_id=1, source_target_pairs={{0,3},{1,0},{2,1},{3,2},{4,7},{5,4},{6,5},{7,6},{8,11},{9,8},{10,9... | collective-permute-start | bytes 196616 | tf_op jit(solution)/shard_map/ppermute | solution.py:32
  85.6 12.7 %collective-permute-start.5 = (bf16[1,128,256]{2,1,0:T(8,128)(2,1)S(1)}, bf16[1,128,256]{2,1,0:T(8,128)(2,1)S(1)}, u32[]{:S(2)}, u32[]{:S(2)}) collective-permute-start(bf16[1,128,256]{2,1,0:T(8,128)(2,1)S(1)} %get-tuple-element.30.refs_0_), channel_id=1, source_target_pairs={{0,32},{32,0},{64,96},{96,64},{1,33},{33,1},{65,97},{97,65},{2,34}... | collective-permute-start | bytes 196616 | tf_op jit(solution)/shard_map/ppermute | solution.py:37
  85.8 12.5 %collective-permute-start.6 = (bf16[1,128,256]{2,1,0:T(8,128)(2,1)S(1)}, bf16[1,128,256]{2,1,0:T(8,128)(2,1)S(1)}, u32[]{:S(2)}, u32[]{:S(2)}) collective-permute-start(bf16[1,128,256]{2,1,0:T(8,128)(2,1)S(1)} %get-tuple-element.31.refs_2_), channel_id=1, source_target_pairs={{0,96},{32,64},{64,32},{96,0},{1,97},{33,65},{65,33},{97,1},{2,98}... | collective-permute-start | bytes 196616 | tf_op jit(solution)/shard_map/ppermute | solution.py:37
  86.7 11.6 %collective-permute-start.7 = (bf16[1,128,256]{2,1,0:T(8,128)(2,1)S(1)}, bf16[1,128,256]{2,1,0:T(8,128)(2,1)S(1)}, u32[]{:S(2)}, u32[]{:S(2)}) collective-permute-start(bf16[1,128,256]{2,1,0:T(8,128)(2,1)S(1)} %get-tuple-element.32.refs_4_), channel_id=1, source_target_pairs={{0,8},{8,0},{16,24},{24,16},{1,9},{9,1},{17,25},{25,17},{2,10},{10... | collective-permute-start | bytes 196616 | tf_op jit(solution)/shard_map/ppermute | solution.py:37
  87.2 11.2 %collective-permute-start.8 = (bf16[1,128,256]{2,1,0:T(8,128)(2,1)S(1)}, bf16[1,128,256]{2,1,0:T(8,128)(2,1)S(1)}, u32[]{:S(2)}, u32[]{:S(2)}) collective-permute-start(bf16[1,128,256]{2,1,0:T(8,128)(2,1)S(1)} %get-tuple-element.33.refs_6_), channel_id=1, source_target_pairs={{0,24},{8,16},{16,8},{24,0},{1,25},{9,17},{17,9},{25,1},{2,26},{10... | collective-permute-start | bytes 196616 | tf_op jit(solution)/shard_map/ppermute | solution.py:37
  88.7 19.4 %all-to-all-start.2 = ((f32[128,1,128]{2,1,0:T(1,128)}), f32[128,1,128]{2,1,0:T(1,128)S(1)}, u32[]{:S(2)}, u32[]{:S(2)}) async-start(f32[128,1,128]{2,1,0:T(1,128)} %broadcast_in_dim.73), calls=%async_computation.2 | async-start | bytes 131072 | tf_op jit(solution)/shard_map/all_to_all | solution.py:445
  98.4 36.3 %copy-start.9 = (s32[256,63]{0,1:T(8,128)S(1)}, s32[256,63]{0,1:T(8,128)}, u32[]{:S(2)}) copy-start(s32[256,63]{0,1:T(8,128)} %param.23) | copy-start | bytes 193540
  98.4 9.7 %collective-permute-start.9 = (bf16[2,128,256]{2,1,0:T(8,128)(2,1)S(1)}, bf16[2,128,256]{2,1,0:T(8,128)(2,1)S(1)}, u32[]{:S(2)}, u32[]{:S(2)}) collective-permute-start(bf16[2,128,256]{2,1,0:T(8,128)(2,1)S(1)} %get-tuple-element.34.refs_0_), channel_id=1, source_target_pairs={{0,96},{32,64},{64,32},{96,0},{1,97},{33,65},{65,33},{97,1},{2,98}... | collective-permute-start | bytes 393224 | tf_op jit(solution)/shard_map/ppermute | solution.py:37
  101.1 7.1 %collective-permute-start.10 = (bf16[2,128,256]{2,1,0:T(8,128)(2,1)S(1)}, bf16[2,128,256]{2,1,0:T(8,128)(2,1)S(1)}, u32[]{:S(2)}, u32[]{:S(2)}) collective-permute-start(bf16[2,128,256]{2,1,0:T(8,128)(2,1)S(1)} %get-tuple-element.37.refs_2_), channel_id=1, source_target_pairs={{0,8},{8,0},{16,24},{24,16},{1,9},{9,1},{17,25},{25,17},{2,10},{10... | collective-permute-start | bytes 393224 | tf_op jit(solution)/shard_map/ppermute | solution.py:37
  102.4 5.7 %collective-permute-start.11 = (bf16[2,128,256]{2,1,0:T(8,128)(2,1)S(1)}, bf16[2,128,256]{2,1,0:T(8,128)(2,1)S(1)}, u32[]{:S(2)}, u32[]{:S(2)}) collective-permute-start(bf16[2,128,256]{2,1,0:T(8,128)(2,1)S(1)} %get-tuple-element.38.refs_4_), channel_id=1, source_target_pairs={{0,24},{8,16},{16,8},{24,0},{1,25},{9,17},{17,9},{25,1},{2,26},{10... | collective-permute-start | bytes 393224 | tf_op jit(solution)/shard_map/ppermute | solution.py:37
  104.5 4.1 %collective-permute-start.12 = (bf16[2,128,256]{2,1,0:T(8,128)(2,1)S(1)}, bf16[2,128,256]{2,1,0:T(8,128)(2,1)S(1)}, u32[]{:S(2)}, u32[]{:S(2)}) collective-permute-start(bf16[2,128,256]{2,1,0:T(8,128)(2,1)S(1)} %get-tuple-element.39.refs_6_), channel_id=1, source_target_pairs={{0,32},{32,0},{64,96},{96,64},{1,33},{33,1},{65,97},{97,65},{2,34}... | collective-permute-start | bytes 393224 | tf_op jit(solution)/shard_map/ppermute | solution.py:37
  109.0 3.9 %collective-permute-start.13 = (bf16[4,64,256]{2,1,0:T(8,128)(2,1)S(1)}, bf16[4,64,256]{2,1,0:T(8,128)(2,1)S(1)}, u32[]{:S(2)}, u32[]{:S(2)}) collective-permute-start(bf16[4,64,256]{2,1,0:T(8,128)(2,1)S(1)} %get-tuple-element.40.refs_0_), channel_id=1, source_target_pairs={{0,8},{8,0},{16,24},{24,16},{1,9},{9,1},{17,25},{25,17},{2,10},{10... | collective-permute-start | bytes 393224 | tf_op jit(solution)/shard_map/ppermute | solution.py:37
  109.6 5.0 %collective-permute-start.14 = (bf16[4,64,256]{2,1,0:T(8,128)(2,1)S(1)}, bf16[4,64,256]{2,1,0:T(8,128)(2,1)S(1)}, u32[]{:S(2)}, u32[]{:S(2)}) collective-permute-start(bf16[4,64,256]{2,1,0:T(8,128)(2,1)S(1)} %get-tuple-element.41.refs_2_), channel_id=1, source_target_pairs={{0,24},{8,16},{16,8},{24,0},{1,25},{9,17},{17,9},{25,1},{2,26},{10... | collective-permute-start | bytes 393224 | tf_op jit(solution)/shard_map/ppermute | solution.py:37
  110.2 4.4 %collective-permute-start.15 = (bf16[4,64,256]{2,1,0:T(8,128)(2,1)S(1)}, bf16[4,64,256]{2,1,0:T(8,128)(2,1)S(1)}, u32[]{:S(2)}, u32[]{:S(2)}) collective-permute-start(bf16[4,64,256]{2,1,0:T(8,128)(2,1)S(1)} %get-tuple-element.42.refs_4_), channel_id=1, source_target_pairs={{0,32},{32,0},{64,96},{96,64},{1,33},{33,1},{65,97},{97,65},{2,34}... | collective-permute-start | bytes 393224 | tf_op jit(solution)/shard_map/ppermute | solution.py:37
  110.4 5.0 %collective-permute-start.16 = (bf16[4,64,256]{2,1,0:T(8,128)(2,1)S(1)}, bf16[4,64,256]{2,1,0:T(8,128)(2,1)S(1)}, u32[]{:S(2)}, u32[]{:S(2)}) collective-permute-start(bf16[4,64,256]{2,1,0:T(8,128)(2,1)S(1)} %get-tuple-element.43.refs_6_), channel_id=1, source_target_pairs={{0,96},{32,64},{64,32},{96,0},{1,97},{33,65},{65,33},{97,1},{2,98}... | collective-permute-start | bytes 393224 | tf_op jit(solution)/shard_map/ppermute | solution.py:37
  116.5 18.1 %collective-permute-start.17 = (bf16[4,8,64,256]{3,2,1,0:T(8,128)(2,1)}, bf16[4,8,64,256]{3,2,1,0:T(8,128)(2,1)S(1)}, u32[]{:S(2)}, u32[]{:S(2)}) collective-permute-start(bf16[4,8,64,256]{3,2,1,0:T(8,128)(2,1)} %get-tuple-element.48), channel_id=1, source_target_pairs={{0,4},{4,0},{1,5},{5,1},{2,6},{6,2},{3,7},{7,3},{8,12},{12,8},{9,1... | collective-permute-start | bytes 3145736 | tf_op jit(solution)/shard_map/ppermute | solution.py:32
  120.2 9.3 %collective-permute-start.18 = (bf16[8,64,256]{2,1,0:T(8,128)(2,1)S(1)}, bf16[8,64,256]{2,1,0:T(8,128)(2,1)}, u32[]{:S(2)}, u32[]{:S(2)}) collective-permute-start(bf16[8,64,256]{2,1,0:T(8,128)(2,1)S(1)} %get-tuple-element.44.refs_0_), channel_id=1, source_target_pairs={{0,24},{8,16},{16,8},{24,0},{1,25},{9,17},{17,9},{25,1},{2,26},{10... | collective-permute-start | bytes 786440 | tf_op jit(solution)/shard_map/ppermute | solution.py:37
  122.5 7.8 %collective-permute-start.19 = (bf16[8,64,256]{2,1,0:T(8,128)(2,1)S(1)}, bf16[8,64,256]{2,1,0:T(8,128)(2,1)}, u32[]{:S(2)}, u32[]{:S(2)}) collective-permute-start(bf16[8,64,256]{2,1,0:T(8,128)(2,1)S(1)} %get-tuple-element.45.refs_1_), channel_id=1, source_target_pairs={{0,32},{32,0},{64,96},{96,64},{1,33},{33,1},{65,97},{97,65},{2,34}... | collective-permute-start | bytes 786440 | tf_op jit(solution)/shard_map/ppermute | solution.py:37
  122.8 8.6 %collective-permute-start.20 = (bf16[8,64,256]{2,1,0:T(8,128)(2,1)S(1)}, bf16[8,64,256]{2,1,0:T(8,128)(2,1)}, u32[]{:S(2)}, u32[]{:S(2)}) collective-permute-start(bf16[8,64,256]{2,1,0:T(8,128)(2,1)S(1)} %get-tuple-element.46.refs_2_), channel_id=1, source_target_pairs={{0,96},{32,64},{64,32},{96,0},{1,97},{33,65},{65,33},{97,1},{2,98}... | collective-permute-start | bytes 786440 | tf_op jit(solution)/shard_map/ppermute | solution.py:37
  123.3 9.5 %collective-permute-start.21 = (bf16[8,64,256]{2,1,0:T(8,128)(2,1)S(1)}, bf16[8,64,256]{2,1,0:T(8,128)(2,1)}, u32[]{:S(2)}, u32[]{:S(2)}) collective-permute-start(bf16[8,64,256]{2,1,0:T(8,128)(2,1)S(1)} %get-tuple-element.47.refs_3_), channel_id=1, source_target_pairs={{0,8},{8,0},{16,24},{24,16},{1,9},{9,1},{17,25},{25,17},{2,10},{10... | collective-permute-start | bytes 786440 | tf_op jit(solution)/shard_map/ppermute | solution.py:37
  123.3 0.7 copy-start.7
  129.4 3.5 %collective-permute-start.22 = (bf16[8,64,256]{2,1,0:T(8,128)(2,1)}, bf16[8,64,256]{2,1,0:T(8,128)(2,1)}, u32[]{:S(2)}, u32[]{:S(2)}) collective-permute-start(bf16[8,64,256]{2,1,0:T(8,128)(2,1)} %collective-permute-done.18.refs_5_), channel_id=1, source_target_pairs={{0,4},{4,0},{1,5},{5,1},{2,6},{6,2},{3,7},{7,3},{8,12},{12,8},{9,1... | collective-permute-start | bytes 786440 | tf_op jit(solution)/shard_map/ppermute | solution.py:32
  130.2 2.7 %collective-permute-start.23 = (bf16[8,64,256]{2,1,0:T(8,128)(2,1)}, bf16[8,64,256]{2,1,0:T(8,128)(2,1)}, u32[]{:S(2)}, u32[]{:S(2)}) collective-permute-start(bf16[8,64,256]{2,1,0:T(8,128)(2,1)} %collective-permute-done.19.refs_6_), channel_id=1, source_target_pairs={{0,4},{4,0},{1,5},{5,1},{2,6},{6,2},{3,7},{7,3},{8,12},{12,8},{9,1... | collective-permute-start | bytes 786440 | tf_op jit(solution)/shard_map/ppermute | solution.py:32
  131.4 2.9 %collective-permute-start.24 = (bf16[8,64,256]{2,1,0:T(8,128)(2,1)}, bf16[8,64,256]{2,1,0:T(8,128)(2,1)}, u32[]{:S(2)}, u32[]{:S(2)}) collective-permute-start(bf16[8,64,256]{2,1,0:T(8,128)(2,1)} %collective-permute-done.20.refs_7_), channel_id=1, source_target_pairs={{0,4},{4,0},{1,5},{5,1},{2,6},{6,2},{3,7},{7,3},{8,12},{12,8},{9,1... | collective-permute-start | bytes 786440 | tf_op jit(solution)/shard_map/ppermute | solution.py:32
  132.8 1.9 %collective-permute-start.25 = (bf16[8,64,256]{2,1,0:T(8,128)(2,1)}, bf16[8,64,256]{2,1,0:T(8,128)(2,1)}, u32[]{:S(2)}, u32[]{:S(2)}) collective-permute-start(bf16[8,64,256]{2,1,0:T(8,128)(2,1)} %collective-permute-done.21.refs_8_), channel_id=1, source_target_pairs={{0,4},{4,0},{1,5},{5,1},{2,6},{6,2},{3,7},{7,3},{8,12},{12,8},{9,1... | collective-permute-start | bytes 786440 | tf_op jit(solution)/shard_map/ppermute | solution.py:32
  134.7 1.0 copy-start.8
  145.9 1.0 copy-start.6

commit v3 on v2

--- a/solution.py
+++ b/solution.py
@@ -23,6 +23,7 @@
 SHIFTS = (1, 3, 2)
 SWAPS = (("x", 1), ("x", 3), ("z", 1), ("z", 3))
 PARTS = len(SWAPS)
+SQUARES_COPIES = 4
 bf16 = jnp.bfloat16
 f32 = jnp.float32
 
@@ -442,9 +443,10 @@
     place = jnp.sum(jnp.where(grid == rows_of(quarters)[None, :], order[None, :], 0), 1)
 
     parts = pick_rows(pick, [scaled, got[1], got[2], got[3]])
+    squares_out = jnp.sum(rounded * rounded, 1)
     shares = lax.all_to_all(
-        jnp.broadcast_to(jnp.sum(rounded * rounded, 1), (NX * NZ * NC * NY, held)), ALL, 0, 0
-    )
+        jnp.broadcast_to(squares_out, (NX * NZ * NC * NY, SQUARES_COPIES, held)), ALL, 0, 0
+    )[:, 0]
     parts = join([(part, swap(part, i, 0)) for i, part in enumerate(parts)], False)
     parts = [(part, swap(part, i, 1)) for i, part in enumerate(parts)]
     shares, first = lax.optimization_barrier((shares, parts[0][1]))

time: 166 us -> 164 us (0.988)
  waiting for transfers between devices: 52.3 us -> 49.6 us
    all_to_all x1, starting transfers between devices: 9.61 us -> 4.94 us  [local(): lax.all_to_all(jnp.broadcast_to(squares_out, (NX * NZ * NC * NY, SQUARES_...]
    ppermute x16, starting transfers between devices: 13.7 us -> 17.7 us  [swap(): lax.ppermute(value, axis, [(i, i ^ by) for i in range(lax.axis_size(axis))])]
    ppermute x16, waiting for transfers between devices: 10.1 us -> 14.1 us  [swap(): lax.ppermute(value, axis, [(i, i ^ by) for i in range(lax.axis_size(axis))])]
    ppermute x10, waiting for transfers between devices: 7.73 us -> 4.36 us  [shift(): lax.ppermute(value, axis, [(i, (i + by) % size) for i in range(size)])]
    all_to_all x1, waiting for transfers between devices: 3.22 us -> 0.01 us  [local(): lax.all_to_all(jnp.broadcast_to(squares_out, (NX * NZ * NC * NY, SQUARES_...]
  transfers between devices with their start and end apart: 29 -> 29, of which waited for: 14 -> 16; matrix products, arithmetic and copies ran while one was open for 4% -> 4% of each run, Pallas kernels for 1% -> 2%
where the time goes in v3:
time: 164 us
  starting transfers between devices  55.2 us (34%)
  waiting for transfers between devices  49.6 us (30%)
  Pallas kernels  21.2 us (13%)
  blocking collectives  16 us (10%)
  local copies, waits for them, and re-layouts  8.42 us (5%)
  matrix products  6.99 us (4%)
  other arithmetic  5.84 us (4%)
    all_to_all x1, waiting for transfers between devices, local(): lax.all_to_all(mine.reshape(NX * NZ, local_rows, -1), ('x', 'z'), 0, 0)  19.1 us
    ppermute x16, starting transfers between devices, swap(): lax.ppermute(value, axis, [(i, i ^ by) for i in range(lax.axis_size(axis))])  17.7 us
    ppermute x10, starting transfers between devices, shift(): lax.ppermute(value, axis, [(i, (i + by) % size) for i in range(size)])  16.4 us
    all_to_all x1, blocking collectives, local(): lax.all_to_all(jnp.broadcast_to(shares[0], (NX * NZ * NC * NY, pair_count...  16 us
    ppermute x16, waiting for transfers between devices, swap(): lax.ppermute(value, axis, [(i, i ^ by) for i in range(lax.axis_size(axis))])  14.1 us
    all_to_all x1, waiting for transfers between devices, local(): lax.all_to_all(blocks.reshape(-1, share, query_cols), ('x', 'z', 'y'), 0, 0)  12.1 us
    pallas_call x1, Pallas kernels, vocab_logits(): pl.pallas_call(functools.partial(vocab_kernel, count), out_shape=(jax.Sha...  10.2 us
    all_to_all x1, starting transfers between devices, local(): lax.all_to_all(blocks.reshape(-1, share, query_cols), ('x', 'z', 'y'), 0, 0)  8.24 us
  transfers between devices with their start and end apart: 29, of which 16 were waited for; matrix products, arithmetic and copies ran while one was open for 4% of the time, Pallas kernels for 2%

profile of v3, /device:TPU:1, one launch (start us, length us, event | category | flops | bytes accessed | tf_op | source)
XLA Modules:
  0.0 163.8 jit_solution(13929115835598059409)
XLA Ops:
  0.0 3.6 %shard_map.118 = bf16[256,2688]{1,0:T(8,128)(2,1)} custom-call(s32[1]{0:T(128)} %bitcast.39.core_ref, bf16[16,2,16,256]{3,2,1,0:T(8,128)(2,1)} %bitcast.108, f32[1,256]{1,0:T(1,128)} %bitcast.113, bf16[256,2048]{1,0:T(8,128)(2,1)} %query_ref.3, bf16[256,2,256]{2,1,0:T(2,128)(2,1)} %keyval_ref.3), custom_call_target="tpu_custom_call" | custom-call | flops 352321536 | bytes 2752512 | tf_op jit(solution)/shard_map/pallas_call | solution.py:168
  3.6 1.4 collective-permute-start
  5.1 3.0 %collective-permute-done.refs_0_ = bf16[256,2688]{1,0:T(8,128)(2,1)S(1)} collective-permute-done((bf16[256,2688]{1,0:T(8,128)(2,1)}, bf16[256,2688]{1,0:T(8,128)(2,1)S(1)}, u32[]{:S(2)}, u32[]{:S(2)}) %collective-permute-start) | collective-permute-done | bytes 1376288 | tf_op jit(solution)/shard_map/ppermute | solution.py:33
  8.0 2.2 %shard_map.119 = bf16[256,2688]{1,0:T(8,128)(2,1)} custom-call(s32[1]{0:T(128)} %bitcast.36.core_ref, bf16[16,2,16,256]{3,2,1,0:T(8,128)(2,1)S(1)} %bitcast.109, f32[1,256]{1,0:T(1,128)S(1)} %bitcast.114, bf16[256,2048]{1,0:T(8,128)(2,1)S(1)} %copy-done.3, bf16[256,2,256]{2,1,0:T(2,128)(2,1)S(1)} %copy-done.5, bf16[256,2688]{1,0:T(8,128)(2,1)S(1)} %collective-permute-done.refs_0_), custom_call_target="tpu_custom_call" | custom-call | flops 352321536 | bytes 2752512 | tf_op jit(solution)/shard_map/pallas_call | solution.py:168
  10.2 7.9 %all-to-all-start = ((bf16[16,16,2688]{2,1,0:T(8,128)(2,1)}), bf16[16,16,2688]{2,1,0:T(8,128)(2,1)}, u32[]{:S(2)}, u32[]{:S(2)}) async-start(bf16[16,16,2688]{2,1,0:T(8,128)(2,1)} %bitcast.40), calls=%async_computation | async-start | bytes 2752512 | tf_op jit(solution)/shard_map/all_to_all | solution.py:393
  18.3 19.1 %all-to-all-done = bf16[16,16,2688]{2,1,0:T(8,128)(2,1)} async-done(((bf16[16,16,2688]{2,1,0:T(8,128)(2,1)}), bf16[16,16,2688]{2,1,0:T(8,128)(2,1)}, u32[]{:S(2)}, u32[]{:S(2)}) %all-to-all-start) | async-done | bytes 1376288 | tf_op jit(solution)/shard_map/all_to_all | solution.py:393
  37.4 1.5 convert_reduce_fusion
  39.9 1.0 fusion.26
  41.2 0.6 fusion.1
  41.8 1.1 shard_map.120
  42.9 8.2 %all-to-all-start.1 = ((bf16[64,4,2048]{2,1,0:T(4,128)(2,1)}), bf16[64,4,2048]{2,1,0:T(4,128)(2,1)S(1)}, u32[]{:S(2)}, u32[]{:S(2)}) async-start(bf16[64,4,2048]{2,1,0:T(4,128)(2,1)} %bitcast.48), calls=%async_computation.1 | async-start | bytes 2097152 | tf_op jit(solution)/shard_map/all_to_all | solution.py:412
  51.3 2.2 %shard_map.121 = bf16[8192,256]{1,0:T(8,128)(2,1)S(1)} custom-call(bf16[8192,256]{1,0:T(8,128)(2,1)} %w_ref.1, bf16[16,2048]{1,0:T(8,128)(2,1)S(1)} %bitcast.110), custom_call_target="tpu_custom_call" | custom-call | bytes 8388608 | tf_op jit(solution)/shard_map/pallas_call | solution.py:100
  53.6 2.0 %copy-done.1 = bf16[8192,256]{1,0:T(8,128)(2,1)} copy-done((bf16[8192,256]{1,0:T(8,128)(2,1)}, bf16[8192,256]{1,0:T(8,128)(2,1)S(1)}, u32[]{:S(2)}) %copy-start.1) | copy-done | bytes 4194328
  55.5 12.1 %all-to-all-done.1 = bf16[64,4,2048]{2,1,0:T(4,128)(2,1)S(1)} async-done(((bf16[64,4,2048]{2,1,0:T(4,128)(2,1)}), bf16[64,4,2048]{2,1,0:T(4,128)(2,1)S(1)}, u32[]{:S(2)}, u32[]{:S(2)}) %all-to-all-start.1) | async-done | bytes 1048608 | tf_op jit(solution)/shard_map/all_to_all | solution.py:412
  67.6 0.9 copy.60
  68.5 0.6 copy.75
  69.1 3.2 %collective-permute-start.1 = (bf16[64,8192]{1,0:T(8,128)(2,1)S(1)}, bf16[64,8192]{1,0:T(8,128)(2,1)}, u32[]{:S(2)}, u32[]{:S(2)}) collective-permute-start(bf16[64,8192]{1,0:T(8,128)(2,1)S(1)} %bitcast.119), channel_id=1, source_target_pairs={{0,4},{4,0},{1,5},{5,1},{2,6},{6,2},{3,7},{7,3},{8,12},{12,8},{9,1... | collective-permute-start | bytes 3145736 | tf_op jit(solution)/shard_map/ppermute | solution.py:33
  73.0 3.1 %fusion.27 = f32[64,256]{1,0:T(8,128)S(1)} fusion(bf16[64,8192]{1,0:T(8,128)(2,1)S(1)} %bitcast.120, bf16[8192,256]{1,0:T(8,128)(2,1)} %copy-done.1), kind=kOutput, calls=%fused_computation.76 | convolution fusion | flops 268435456 | bytes 5308416 | tf_op jit(solution)/shard_map/dot_general | solution.py:417
  76.1 0.3 copy-done.2
  76.4 2.0 %broadcast_select_fusion.1 = (f32[64,256]{1,0:T(8,128)S(1)}, f32[64,256]{1,0:T(8,128)S(1)}) fusion(f32[64,256]{1,0:T(8,128)S(1)} %fusion.27, pred[]{:T(512)S(6)} %eq.65, bf16[64,8192]{1,0:T(8,128)(2,1)} %collective-permute-done.1, bf16[8192,256]{1,0:T(8,128)(2,1)S(1)} %copy-done.2), kind=kOutput, calls=%fused_computation.36 | convolution fusion | flops 268468224 | bytes 5439489 | tf_op jit(solution)/shard_map/dot_general | solution.py:418
  78.5 0.6 collective-permute-start.2
  79.1 1.2 collective-permute-start.3
  80.4 1.4 collective-permute-start.4
  82.1 0.7 broadcast_in_dim.42
  82.8 4.9 %all-to-all-start.2 = ((f32[128,4,128]{2,1,0:T(4,128)}), f32[128,4,128]{2,1,0:T(4,128)S(1)}, u32[]{:S(2)}, u32[]{:S(2)}) async-start(f32[128,4,128]{2,1,0:T(4,128)} %broadcast_in_dim.42), calls=%async_computation.2 | async-start | bytes 524288 | tf_op jit(solution)/shard_map/all_to_all | solution.py:447
  88.0 0.4 shard_map.122
  88.4 1.5 collective-permute-start.5
  89.9 1.8 %collective-permute-start.6 = (bf16[1,128,256]{2,1,0:T(8,128)(2,1)S(1)}, bf16[1,128,256]{2,1,0:T(8,128)(2,1)S(1)}, u32[]{:S(2)}, u32[]{:S(2)}) collective-permute-start(bf16[1,128,256]{2,1,0:T(8,128)(2,1)S(1)} %get-tuple-element.31.refs_2_), channel_id=1, source_target_pairs={{0,96},{32,64},{64,32},{96,0},{1,97},{33,65},{65,33},{97,1},{2,98}... | collective-permute-start | bytes 196616 | tf_op jit(solution)/shard_map/ppermute | solution.py:38
  91.7 1.3 collective-permute-start.7
  93.0 2.1 %collective-permute-start.8 = (bf16[1,128,256]{2,1,0:T(8,128)(2,1)S(1)}, bf16[1,128,256]{2,1,0:T(8,128)(2,1)S(1)}, u32[]{:S(2)}, u32[]{:S(2)}) collective-permute-start(bf16[1,128,256]{2,1,0:T(8,128)(2,1)S(1)} %get-tuple-element.33.refs_6_), channel_id=1, source_target_pairs={{0,24},{8,16},{16,8},{24,0},{1,25},{9,17},{17,9},{25,1},{2,26},{10... | collective-permute-start | bytes 196616 | tf_op jit(solution)/shard_map/ppermute | solution.py:38
  95.2 0.6 collective-permute-done.7.refs_5_
  95.8 2.3 %collective-permute-done.8.refs_7_ = bf16[1,128,256]{2,1,0:T(8,128)(2,1)S(1)} collective-permute-done((bf16[1,128,256]{2,1,0:T(8,128)(2,1)S(1)}, bf16[1,128,256]{2,1,0:T(8,128)(2,1)S(1)}, u32[]{:S(2)}, u32[]{:S(2)}) %collective-permute-start.8) | collective-permute-done | bytes 65568 | tf_op jit(solution)/shard_map/ppermute | solution.py:38
  98.1 1.1 collective-permute-start.9
  99.2 0.3 collective-permute-start.10
  99.5 1.3 collective-permute-start.11
  100.8 0.4 collective-permute-start.12
  101.2 0.2 select_reduce_fusion
  101.6 1.6 collective-permute-done.9.refs_1_
  103.2 1.6 collective-permute-done.11.refs_5_
  104.9 0.4 shard_map.124
  105.3 0.7 collective-permute-start.13
  105.9 1.4 collective-permute-start.14
  107.3 1.7 %collective-permute-start.16 = (bf16[4,64,256]{2,1,0:T(8,128)(2,1)S(1)}, bf16[4,64,256]{2,1,0:T(8,128)(2,1)S(1)}, u32[]{:S(2)}, u32[]{:S(2)}) collective-permute-start(bf16[4,64,256]{2,1,0:T(8,128)(2,1)S(1)} %get-tuple-element.43.refs_6_), channel_id=1, source_target_pairs={{0,96},{32,64},{64,32},{96,0},{1,97},{33,65},{65,33},{97,1},{2,98}... | collective-permute-start | bytes 393224 | tf_op jit(solution)/shard_map/ppermute | solution.py:38
  109.2 1.8 %collective-permute-done.14.refs_3_ = bf16[4,64,256]{2,1,0:T(8,128)(2,1)S(1)} collective-permute-done((bf16[4,64,256]{2,1,0:T(8,128)(2,1)S(1)}, bf16[4,64,256]{2,1,0:T(8,128)(2,1)S(1)}, u32[]{:S(2)}, u32[]{:S(2)}) %collective-permute-start.14) | collective-permute-done | bytes 131104 | tf_op jit(solution)/shard_map/ppermute | solution.py:38
  111.1 1.2 collective-permute-done.16.refs_7_
  112.3 1.1 shard_map.125
  113.4 5.0 %collective-permute-start.17 = (bf16[4,8,64,256]{3,2,1,0:T(8,128)(2,1)}, bf16[4,8,64,256]{3,2,1,0:T(8,128)(2,1)S(1)}, u32[]{:S(2)}, u32[]{:S(2)}) collective-permute-start(bf16[4,8,64,256]{3,2,1,0:T(8,128)(2,1)} %get-tuple-element.48), channel_id=1, source_target_pairs={{0,4},{4,0},{1,5},{5,1},{2,6},{6,2},{3,7},{7,3},{8,12},{12,8},{9,1... | collective-permute-start | bytes 3145736 | tf_op jit(solution)/shard_map/ppermute | solution.py:33
  118.4 2.0 %collective-permute-start.18 = (bf16[8,64,256]{2,1,0:T(8,128)(2,1)S(1)}, bf16[8,64,256]{2,1,0:T(8,128)(2,1)}, u32[]{:S(2)}, u32[]{:S(2)}) collective-permute-start(bf16[8,64,256]{2,1,0:T(8,128)(2,1)S(1)} %get-tuple-element.44.refs_0_), channel_id=1, source_target_pairs={{0,24},{8,16},{16,8},{24,0},{1,25},{9,17},{17,9},{25,1},{2,26},{10... | collective-permute-start | bytes 786440 | tf_op jit(solution)/shard_map/ppermute | solution.py:38
  120.4 0.5 collective-permute-start.19
  120.9 1.8 %collective-permute-start.20 = (bf16[8,64,256]{2,1,0:T(8,128)(2,1)S(1)}, bf16[8,64,256]{2,1,0:T(8,128)(2,1)}, u32[]{:S(2)}, u32[]{:S(2)}) collective-permute-start(bf16[8,64,256]{2,1,0:T(8,128)(2,1)S(1)} %get-tuple-element.46.refs_2_), channel_id=1, source_target_pairs={{0,96},{32,64},{64,32},{96,0},{1,97},{33,65},{65,33},{97,1},{2,98}... | collective-permute-start | bytes 786440 | tf_op jit(solution)/shard_map/ppermute | solution.py:38
  122.7 0.7 copy-done.7
  123.4 4.2 %collective-permute-done.18.refs_5_ = bf16[8,64,256]{2,1,0:T(8,128)(2,1)} collective-permute-done((bf16[8,64,256]{2,1,0:T(8,128)(2,1)S(1)}, bf16[8,64,256]{2,1,0:T(8,128)(2,1)}, u32[]{:S(2)}, u32[]{:S(2)}) %collective-permute-start.18) | collective-permute-done | bytes 262176 | tf_op jit(solution)/shard_map/ppermute | solution.py:38
  127.7 0.8 collective-permute-start.22
  128.4 0.8 collective-permute-start.23
  129.2 0.3 collective-permute-done.20.refs_7_
  129.5 1.4 collective-permute-start.24
  131.0 0.6 collective-permute-start.25
  131.7 0.8 collective-permute-done.24.refs_11_
  132.5 0.6 collective-permute-done.25.refs_12_
  133.1 0.9 copy-done.8
  134.0 10.2 %shard_map.126 = (f32[1002,256]{1,0:T(8,128)S(1)}, f32[1,256]{1,0:T(1,128)S(1)}) custom-call(s32[33]{0:T(128)S(1)} %stack.135.places, bf16[1002,8192]{1,0:T(8,128)(2,1)} %bitcast.116, bf16[8,64,256]{2,1,0:T(8,128)(2,1)S(1)} %get-tuple-element.44.refs_0_, bf16[8,64,256]{2,1,0:T(8,128)(2,1)S(1)} %get-tuple-element.45.refs_1_, ...), custom_call_target="tpu_custom_call" | custom-call | flops 4202692608 | bytes 16416768 | tf_op jit(solution)/shard_map/pallas_call | solution.py:343
  144.3 1.0 copy-done.6
  145.3 16.0 %all_to_all.24 = f32[128,1,256]{2,1,0:T(1,128)S(1)} all-to-all(f32[128,1,256]{2,1,0:T(1,128)S(1)} %broadcast_in_dim.74), channel_id=1, replica_groups=mesh['x'=4,'z'=4,'c'=2,'y'=4] {'x','z','c','y'}, dimensions={0} | all-to-all | bytes 262144 | tf_op jit(solution)/shard_map/all_to_all | solution.py:479
  161.5 2.3 %select_bitcast_fusion = f32[256,1002]{0,1:T(8,128)} fusion(f32[1002,256]{1,0:T(8,128)} %copy-done.6, f32[256]{0:T(256)S(1)} %log_add_fusion), kind=kLoop, calls=%fused_computation.7 | loop fusion | flops 769536 | bytes 2053120 | tf_op jit(solution)/shard_map/transpose | solution.py:484
  (92 shorter events, 3.8 us)
Async XLA Ops:
  0.0 39.9 %copy-start = (bf16[16,2,192,128]{3,2,1,0:T(8,128)(2,1)S(1)}, bf16[16,2,192,128]{3,2,1,0:T(8,128)(2,1)}, u32[]{:S(2)}) copy-start(bf16[16,2,192,128]{3,2,1,0:T(8,128)(2,1)} %param.17) | copy-start | bytes 4718596
  0.0 8.0 %copy-start.4 = (bf16[512,256]{1,0:T(8,128)(2,1)S(1)}, bf16[512,256]{1,0:T(8,128)(2,1)}, u32[]{:S(2)}) copy-start(bf16[512,256]{1,0:T(8,128)(2,1)} %param.12) | copy-start | bytes 786436
  0.0 8.0 %copy-start.10 = (f32[256]{0:T(256)S(1)}, f32[256]{0:T(256)}, u32[]{:S(2)}) copy-start(f32[256]{0:T(256)} %param.13) | copy-start | bytes 3076
  0.0 8.0 %copy-start.3 = (bf16[256,2048]{1,0:T(8,128)(2,1)S(1)}, bf16[256,2048]{1,0:T(8,128)(2,1)}, u32[]{:S(2)}) copy-start(bf16[256,2048]{1,0:T(8,128)(2,1)} %query_ref.3) | copy-start | bytes 3145732
  0.0 8.0 %copy-start.5 = (bf16[256,2,256]{2,1,0:T(2,128)(2,1)S(1)}, bf16[256,2,256]{2,1,0:T(2,128)(2,1)}, u32[]{:S(2)}) copy-start(bf16[256,2,256]{2,1,0:T(2,128)(2,1)} %keyval_ref.3) | copy-start | bytes 786436
  3.6 4.4 %collective-permute-start = (bf16[256,2688]{1,0:T(8,128)(2,1)}, bf16[256,2688]{1,0:T(8,128)(2,1)S(1)}, u32[]{:S(2)}, u32[]{:S(2)}) collective-permute-start(bf16[256,2688]{1,0:T(8,128)(2,1)} %shard_map.118), channel_id=1, source_target_pairs={{0,4},{4,0},{1,5},{5,1},{2,6},{6,2},{3,7},{7,3},{8,12},{12,8},{9,1... | collective-permute-start | bytes 4128776 | tf_op jit(solution)/shard_map/ppermute | solution.py:33
  10.2 7.9 %copy-start.13 = (s32[16]{0:T(128)S(1)}, s32[16]{0:T(128)}, u32[]{:S(2)}) copy-start(s32[16]{0:T(128)} %param.19) | copy-start | bytes 196
  10.2 27.2 %all-to-all-start = ((bf16[16,16,2688]{2,1,0:T(8,128)(2,1)}), bf16[16,16,2688]{2,1,0:T(8,128)(2,1)}, u32[]{:S(2)}, u32[]{:S(2)}) async-start(bf16[16,16,2688]{2,1,0:T(8,128)(2,1)} %bitcast.40), calls=%async_computation | async-start | bytes 2752512 | tf_op jit(solution)/shard_map/all_to_all | solution.py:393
  39.4 1.8 %copy-start.14 = (bf16[16,2,192,128]{3,2,1,0:T(8,128)(2,1)S(1)}, bf16[16,2,192,128]{3,2,1,0:T(8,128)(2,1)}, u32[]{:S(2)}) copy-start(bf16[16,2,192,128]{3,2,1,0:T(8,128)(2,1)} %param.18) | copy-start | bytes 4718596
  42.9 24.7 %all-to-all-start.1 = ((bf16[64,4,2048]{2,1,0:T(4,128)(2,1)}), bf16[64,4,2048]{2,1,0:T(4,128)(2,1)S(1)}, u32[]{:S(2)}, u32[]{:S(2)}) async-start(bf16[64,4,2048]{2,1,0:T(4,128)(2,1)} %bitcast.48), calls=%async_computation.1 | async-start | bytes 2097152 | tf_op jit(solution)/shard_map/all_to_all | solution.py:412
  53.5 2.0 %copy-start.1 = (bf16[8192,256]{1,0:T(8,128)(2,1)}, bf16[8192,256]{1,0:T(8,128)(2,1)S(1)}, u32[]{:S(2)}) copy-start(bf16[8192,256]{1,0:T(8,128)(2,1)S(1)} %shard_map.121) | copy-start | bytes 12582916
  68.5 4.2 %copy-start.11 = (s32[512]{0:T(512)S(1)}, s32[512]{0:T(512)}, u32[]{:S(2)}) copy-start(s32[512]{0:T(512)} %param.22) | copy-start | bytes 6148
  69.1 7.0 %collective-permute-start.1 = (bf16[64,8192]{1,0:T(8,128)(2,1)S(1)}, bf16[64,8192]{1,0:T(8,128)(2,1)}, u32[]{:S(2)}, u32[]{:S(2)}) collective-permute-start(bf16[64,8192]{1,0:T(8,128)(2,1)S(1)} %bitcast.119), channel_id=1, source_target_pairs={{0,4},{4,0},{1,5},{5,1},{2,6},{6,2},{3,7},{7,3},{8,12},{12,8},{9,1... | collective-permute-start | bytes 3145736 | tf_op jit(solution)/shard_map/ppermute | solution.py:33
  73.0 3.5 %copy-start.2 = (bf16[8192,256]{1,0:T(8,128)(2,1)S(1)}, bf16[8192,256]{1,0:T(8,128)(2,1)}, u32[]{:S(2)}) copy-start(bf16[8192,256]{1,0:T(8,128)(2,1)} %copy-done.1) | copy-start | bytes 12582916
  76.1 2.4 %copy-start.12 = (f32[256]{0:T(256)S(1)}, f32[256]{0:T(256)}, u32[]{:S(2)}) copy-start(f32[256]{0:T(256)} %param.20) | copy-start | bytes 3076
  78.5 9.4 %collective-permute-start.2 = (bf16[128,256]{1,0:T(8,128)(2,1)S(1)}, bf16[128,256]{1,0:T(8,128)(2,1)S(1)}, u32[]{:S(2)}, u32[]{:S(2)}) collective-permute-start(bf16[128,256]{1,0:T(8,128)(2,1)S(1)} %get-tuple-element.53.refs_0_), channel_id=1, source_target_pairs={{0,1},{1,2},{2,3},{3,0},{4,5},{5,6},{6,7},{7,4},{8,9},{9,10},{10,1... | collective-permute-start | bytes 196616 | tf_op jit(solution)/shard_map/ppermute | solution.py:33
  79.1 8.8 %collective-permute-start.3 = (bf16[128,256]{1,0:T(8,128)(2,1)S(1)}, bf16[128,256]{1,0:T(8,128)(2,1)S(1)}, u32[]{:S(2)}, u32[]{:S(2)}) collective-permute-start(bf16[128,256]{1,0:T(8,128)(2,1)S(1)} %get-tuple-element.53.refs_0_), channel_id=1, source_target_pairs={{0,2},{1,3},{2,0},{3,1},{4,6},{5,7},{6,4},{7,5},{8,10},{9,11},{10,... | collective-permute-start | bytes 196616 | tf_op jit(solution)/shard_map/ppermute | solution.py:33
  80.4 7.6 %collective-permute-start.4 = (bf16[128,256]{1,0:T(8,128)(2,1)S(1)}, bf16[128,256]{1,0:T(8,128)(2,1)S(1)}, u32[]{:S(2)}, u32[]{:S(2)}) collective-permute-start(bf16[128,256]{1,0:T(8,128)(2,1)S(1)} %get-tuple-element.53.refs_0_), channel_id=1, source_target_pairs={{0,3},{1,0},{2,1},{3,2},{4,7},{5,4},{6,5},{7,6},{8,11},{9,8},{10,9... | collective-permute-start | bytes 196616 | tf_op jit(solution)/shard_map/ppermute | solution.py:33
  82.8 18.7 %all-to-all-start.2 = ((f32[128,4,128]{2,1,0:T(4,128)}), f32[128,4,128]{2,1,0:T(4,128)S(1)}, u32[]{:S(2)}, u32[]{:S(2)}) async-start(f32[128,4,128]{2,1,0:T(4,128)} %broadcast_in_dim.42), calls=%async_computation.2 | async-start | bytes 524288 | tf_op jit(solution)/shard_map/all_to_all | solution.py:447
  88.4 6.8 %collective-permute-start.5 = (bf16[1,128,256]{2,1,0:T(8,128)(2,1)S(1)}, bf16[1,128,256]{2,1,0:T(8,128)(2,1)S(1)}, u32[]{:S(2)}, u32[]{:S(2)}) collective-permute-start(bf16[1,128,256]{2,1,0:T(8,128)(2,1)S(1)} %get-tuple-element.30.refs_0_), channel_id=1, source_target_pairs={{0,32},{32,0},{64,96},{96,64},{1,33},{33,1},{65,97},{97,65},{2,34}... | collective-permute-start | bytes 196616 | tf_op jit(solution)/shard_map/ppermute | solution.py:38
  89.9 5.3 %collective-permute-start.6 = (bf16[1,128,256]{2,1,0:T(8,128)(2,1)S(1)}, bf16[1,128,256]{2,1,0:T(8,128)(2,1)S(1)}, u32[]{:S(2)}, u32[]{:S(2)}) collective-permute-start(bf16[1,128,256]{2,1,0:T(8,128)(2,1)S(1)} %get-tuple-element.31.refs_2_), channel_id=1, source_target_pairs={{0,96},{32,64},{64,32},{96,0},{1,97},{33,65},{65,33},{97,1},{2,98}... | collective-permute-start | bytes 196616 | tf_op jit(solution)/shard_map/ppermute | solution.py:38
  91.7 4.1 %collective-permute-start.7 = (bf16[1,128,256]{2,1,0:T(8,128)(2,1)S(1)}, bf16[1,128,256]{2,1,0:T(8,128)(2,1)S(1)}, u32[]{:S(2)}, u32[]{:S(2)}) collective-permute-start(bf16[1,128,256]{2,1,0:T(8,128)(2,1)S(1)} %get-tuple-element.32.refs_4_), channel_id=1, source_target_pairs={{0,8},{8,0},{16,24},{24,16},{1,9},{9,1},{17,25},{25,17},{2,10},{10... | collective-permute-start | bytes 196616 | tf_op jit(solution)/shard_map/ppermute | solution.py:38
  93.0 5.1 %collective-permute-start.8 = (bf16[1,128,256]{2,1,0:T(8,128)(2,1)S(1)}, bf16[1,128,256]{2,1,0:T(8,128)(2,1)S(1)}, u32[]{:S(2)}, u32[]{:S(2)}) collective-permute-start(bf16[1,128,256]{2,1,0:T(8,128)(2,1)S(1)} %get-tuple-element.33.refs_6_), channel_id=1, source_target_pairs={{0,24},{8,16},{16,8},{24,0},{1,25},{9,17},{17,9},{25,1},{2,26},{10... | collective-permute-start | bytes 196616 | tf_op jit(solution)/shard_map/ppermute | solution.py:38
  98.1 5.1 %collective-permute-start.9 = (bf16[2,128,256]{2,1,0:T(8,128)(2,1)S(1)}, bf16[2,128,256]{2,1,0:T(8,128)(2,1)S(1)}, u32[]{:S(2)}, u32[]{:S(2)}) collective-permute-start(bf16[2,128,256]{2,1,0:T(8,128)(2,1)S(1)} %get-tuple-element.34.refs_0_), channel_id=1, source_target_pairs={{0,96},{32,64},{64,32},{96,0},{1,97},{33,65},{65,33},{97,1},{2,98}... | collective-permute-start | bytes 393224 | tf_op jit(solution)/shard_map/ppermute | solution.py:38
  99.2 4.0 %collective-permute-start.10 = (bf16[2,128,256]{2,1,0:T(8,128)(2,1)S(1)}, bf16[2,128,256]{2,1,0:T(8,128)(2,1)S(1)}, u32[]{:S(2)}, u32[]{:S(2)}) collective-permute-start(bf16[2,128,256]{2,1,0:T(8,128)(2,1)S(1)} %get-tuple-element.37.refs_2_), channel_id=1, source_target_pairs={{0,8},{8,0},{16,24},{24,16},{1,9},{9,1},{17,25},{25,17},{2,10},{10... | collective-permute-start | bytes 393224 | tf_op jit(solution)/shard_map/ppermute | solution.py:38
  99.5 5.3 %collective-permute-start.11 = (bf16[2,128,256]{2,1,0:T(8,128)(2,1)S(1)}, bf16[2,128,256]{2,1,0:T(8,128)(2,1)S(1)}, u32[]{:S(2)}, u32[]{:S(2)}) collective-permute-start(bf16[2,128,256]{2,1,0:T(8,128)(2,1)S(1)} %get-tuple-element.38.refs_4_), channel_id=1, source_target_pairs={{0,24},{8,16},{16,8},{24,0},{1,25},{9,17},{17,9},{25,1},{2,26},{10... | collective-permute-start | bytes 393224 | tf_op jit(solution)/shard_map/ppermute | solution.py:38
  100.8 4.1 %collective-permute-start.12 = (bf16[2,128,256]{2,1,0:T(8,128)(2,1)S(1)}, bf16[2,128,256]{2,1,0:T(8,128)(2,1)S(1)}, u32[]{:S(2)}, u32[]{:S(2)}) collective-permute-start(bf16[2,128,256]{2,1,0:T(8,128)(2,1)S(1)} %get-tuple-element.39.refs_6_), channel_id=1, source_target_pairs={{0,32},{32,0},{64,96},{96,64},{1,33},{33,1},{65,97},{97,65},{2,34}... | collective-permute-start | bytes 393224 | tf_op jit(solution)/shard_map/ppermute | solution.py:38
  101.4 31.6 %copy-start.9 = (s32[256,63]{0,1:T(8,128)S(1)}, s32[256,63]{0,1:T(8,128)}, u32[]{:S(2)}) copy-start(s32[256,63]{0,1:T(8,128)} %param.23) | copy-start | bytes 193540
  105.3 3.9 %collective-permute-start.13 = (bf16[4,64,256]{2,1,0:T(8,128)(2,1)S(1)}, bf16[4,64,256]{2,1,0:T(8,128)(2,1)S(1)}, u32[]{:S(2)}, u32[]{:S(2)}) collective-permute-start(bf16[4,64,256]{2,1,0:T(8,128)(2,1)S(1)} %get-tuple-element.40.refs_0_), channel_id=1, source_target_pairs={{0,8},{8,0},{16,24},{24,16},{1,9},{9,1},{17,25},{25,17},{2,10},{10... | collective-permute-start | bytes 393224 | tf_op jit(solution)/shard_map/ppermute | solution.py:38
  105.9 5.0 %collective-permute-start.14 = (bf16[4,64,256]{2,1,0:T(8,128)(2,1)S(1)}, bf16[4,64,256]{2,1,0:T(8,128)(2,1)S(1)}, u32[]{:S(2)}, u32[]{:S(2)}) collective-permute-start(bf16[4,64,256]{2,1,0:T(8,128)(2,1)S(1)} %get-tuple-element.41.refs_2_), channel_id=1, source_target_pairs={{0,24},{8,16},{16,8},{24,0},{1,25},{9,17},{17,9},{25,1},{2,26},{10... | collective-permute-start | bytes 393224 | tf_op jit(solution)/shard_map/ppermute | solution.py:38
  107.3 3.8 %collective-permute-start.15 = (bf16[4,64,256]{2,1,0:T(8,128)(2,1)S(1)}, bf16[4,64,256]{2,1,0:T(8,128)(2,1)S(1)}, u32[]{:S(2)}, u32[]{:S(2)}) collective-permute-start(bf16[4,64,256]{2,1,0:T(8,128)(2,1)S(1)} %get-tuple-element.42.refs_4_), channel_id=1, source_target_pairs={{0,32},{32,0},{64,96},{96,64},{1,33},{33,1},{65,97},{97,65},{2,34}... | collective-permute-start | bytes 393224 | tf_op jit(solution)/shard_map/ppermute | solution.py:38
  107.3 5.0 %collective-permute-start.16 = (bf16[4,64,256]{2,1,0:T(8,128)(2,1)S(1)}, bf16[4,64,256]{2,1,0:T(8,128)(2,1)S(1)}, u32[]{:S(2)}, u32[]{:S(2)}) collective-permute-start(bf16[4,64,256]{2,1,0:T(8,128)(2,1)S(1)} %get-tuple-element.43.refs_6_), channel_id=1, source_target_pairs={{0,96},{32,64},{64,32},{96,0},{1,97},{33,65},{65,33},{97,1},{2,98}... | collective-permute-start | bytes 393224 | tf_op jit(solution)/shard_map/ppermute | solution.py:38
  113.4 19.6 %collective-permute-start.17 = (bf16[4,8,64,256]{3,2,1,0:T(8,128)(2,1)}, bf16[4,8,64,256]{3,2,1,0:T(8,128)(2,1)S(1)}, u32[]{:S(2)}, u32[]{:S(2)}) collective-permute-start(bf16[4,8,64,256]{3,2,1,0:T(8,128)(2,1)} %get-tuple-element.48), channel_id=1, source_target_pairs={{0,4},{4,0},{1,5},{5,1},{2,6},{6,2},{3,7},{7,3},{8,12},{12,8},{9,1... | collective-permute-start | bytes 3145736 | tf_op jit(solution)/shard_map/ppermute | solution.py:33
  118.4 9.3 %collective-permute-start.18 = (bf16[8,64,256]{2,1,0:T(8,128)(2,1)S(1)}, bf16[8,64,256]{2,1,0:T(8,128)(2,1)}, u32[]{:S(2)}, u32[]{:S(2)}) collective-permute-start(bf16[8,64,256]{2,1,0:T(8,128)(2,1)S(1)} %get-tuple-element.44.refs_0_), channel_id=1, source_target_pairs={{0,24},{8,16},{16,8},{24,0},{1,25},{9,17},{17,9},{25,1},{2,26},{10... | collective-permute-start | bytes 786440 | tf_op jit(solution)/shard_map/ppermute | solution.py:38
  120.4 8.1 %collective-permute-start.19 = (bf16[8,64,256]{2,1,0:T(8,128)(2,1)S(1)}, bf16[8,64,256]{2,1,0:T(8,128)(2,1)}, u32[]{:S(2)}, u32[]{:S(2)}) collective-permute-start(bf16[8,64,256]{2,1,0:T(8,128)(2,1)S(1)} %get-tuple-element.45.refs_1_), channel_id=1, source_target_pairs={{0,32},{32,0},{64,96},{96,64},{1,33},{33,1},{65,97},{97,65},{2,34}... | collective-permute-start | bytes 786440 | tf_op jit(solution)/shard_map/ppermute | solution.py:38
  120.9 8.6 %collective-permute-start.20 = (bf16[8,64,256]{2,1,0:T(8,128)(2,1)S(1)}, bf16[8,64,256]{2,1,0:T(8,128)(2,1)}, u32[]{:S(2)}, u32[]{:S(2)}) collective-permute-start(bf16[8,64,256]{2,1,0:T(8,128)(2,1)S(1)} %get-tuple-element.46.refs_2_), channel_id=1, source_target_pairs={{0,96},{32,64},{64,32},{96,0},{1,97},{33,65},{65,33},{97,1},{2,98}... | collective-permute-start | bytes 786440 | tf_op jit(solution)/shard_map/ppermute | solution.py:38
  122.7 8.2 %collective-permute-start.21 = (bf16[8,64,256]{2,1,0:T(8,128)(2,1)S(1)}, bf16[8,64,256]{2,1,0:T(8,128)(2,1)}, u32[]{:S(2)}, u32[]{:S(2)}) collective-permute-start(bf16[8,64,256]{2,1,0:T(8,128)(2,1)S(1)} %get-tuple-element.47.refs_3_), channel_id=1, source_target_pairs={{0,8},{8,0},{16,24},{24,16},{1,9},{9,1},{17,25},{25,17},{2,10},{10... | collective-permute-start | bytes 786440 | tf_op jit(solution)/shard_map/ppermute | solution.py:38
  122.7 0.7 copy-start.7
  127.7 4.0 %collective-permute-start.22 = (bf16[8,64,256]{2,1,0:T(8,128)(2,1)}, bf16[8,64,256]{2,1,0:T(8,128)(2,1)}, u32[]{:S(2)}, u32[]{:S(2)}) collective-permute-start(bf16[8,64,256]{2,1,0:T(8,128)(2,1)} %collective-permute-done.18.refs_5_), channel_id=1, source_target_pairs={{0,4},{4,0},{1,5},{5,1},{2,6},{6,2},{3,7},{7,3},{8,12},{12,8},{9,1... | collective-permute-start | bytes 786440 | tf_op jit(solution)/shard_map/ppermute | solution.py:33
  128.4 3.2 %collective-permute-start.23 = (bf16[8,64,256]{2,1,0:T(8,128)(2,1)}, bf16[8,64,256]{2,1,0:T(8,128)(2,1)}, u32[]{:S(2)}, u32[]{:S(2)}) collective-permute-start(bf16[8,64,256]{2,1,0:T(8,128)(2,1)} %collective-permute-done.19.refs_6_), channel_id=1, source_target_pairs={{0,4},{4,0},{1,5},{5,1},{2,6},{6,2},{3,7},{7,3},{8,12},{12,8},{9,1... | collective-permute-start | bytes 786440 | tf_op jit(solution)/shard_map/ppermute | solution.py:33
  129.5 2.9 %collective-permute-start.24 = (bf16[8,64,256]{2,1,0:T(8,128)(2,1)}, bf16[8,64,256]{2,1,0:T(8,128)(2,1)}, u32[]{:S(2)}, u32[]{:S(2)}) collective-permute-start(bf16[8,64,256]{2,1,0:T(8,128)(2,1)} %collective-permute-done.20.refs_7_), channel_id=1, source_target_pairs={{0,4},{4,0},{1,5},{5,1},{2,6},{6,2},{3,7},{7,3},{8,12},{12,8},{9,1... | collective-permute-start | bytes 786440 | tf_op jit(solution)/shard_map/ppermute | solution.py:33
  131.0 2.1 %collective-permute-start.25 = (bf16[8,64,256]{2,1,0:T(8,128)(2,1)}, bf16[8,64,256]{2,1,0:T(8,128)(2,1)}, u32[]{:S(2)}, u32[]{:S(2)}) collective-permute-start(bf16[8,64,256]{2,1,0:T(8,128)(2,1)} %collective-permute-done.21.refs_8_), channel_id=1, source_target_pairs={{0,4},{4,0},{1,5},{5,1},{2,6},{6,2},{3,7},{7,3},{8,12},{12,8},{9,1... | collective-permute-start | bytes 786440 | tf_op jit(solution)/shard_map/ppermute | solution.py:33
  133.1 1.0 copy-start.8
  144.2 1.0 copy-start.6

commit v4 on v3

--- a/solution.py
+++ b/solution.py
@@ -22,7 +22,9 @@
 WORD_BITS = 16
 SHIFTS = (1, 3, 2)
 SWAPS = (("x", 1), ("x", 3), ("z", 1), ("z", 3))
-PARTS = len(SWAPS)
+PARTS = 4
+ORDERS = ((0, 1, 2, 3), (0, 1, 3, 2), (2, 3, 0, 1), (2, 3, 1, 0))
+GROUPS = 2
 SQUARES_COPIES = 4
 bf16 = jnp.bfloat16
 f32 = jnp.float32
@@ -34,12 +36,12 @@
 
 
 def swap(value, part, step):
-    axis, by = SWAPS[(part + step) % PARTS]
+    axis, by = SWAPS[ORDERS[part][step]]
     return lax.ppermute(value, axis, [(i, i ^ by) for i in range(lax.axis_size(axis))])
 
 
 def slot_of(part, distance):
-    return sum((distance >> (part + step) % PARTS & 1) << step for step in range(PARTS))
+    return sum((distance >> bit & 1) << step for step, bit in enumerate(ORDERS[part]))
 
 
 def rotate(values, cosine, sin_part):
@@ -193,39 +195,41 @@
 
 def pick_rows(pick, blocks):
     whole = pl.BlockSpec(memory_space=pltpu.VMEM)
-    shape = (1, pick.shape[0] // PARTS, blocks[0].shape[1])
+    shape = (1, pick.shape[0] // GROUPS, blocks[0].shape[1])
     return pl.pallas_call(
         pick_kernel,
-        out_shape=[jax.ShapeDtypeStruct(shape, bf16)] * PARTS,
+        out_shape=[jax.ShapeDtypeStruct(shape, bf16)] * GROUPS,
         in_specs=[whole] * (1 + len(blocks)),
-        out_specs=[whole] * PARTS,
+        out_specs=[whole] * GROUPS,
         compiler_params=pltpu.CompilerParams(vmem_limit_bytes=12 * 2**20),
         cost_estimate=small_cost(2 * pick.size * blocks[0].shape[1], pick.size * 4),
     )(pick, *blocks)
 
 
 def join_kernel(*refs):
-    ins, outs = refs[: 2 * PARTS], refs[2 * PARTS :]
+    parts = len(refs) // 3
+    ins, outs = refs[: 2 * parts], refs[2 * parts :]
     count = ins[0].shape[0]
-    for part in range(PARTS):
+    for part in range(parts):
         for half in range(2):
             value = ins[2 * part + half][...]
             lines = slice(half * count, (half + 1) * count)
             outs[part][lines] = value
-            if len(outs) > PARTS:
-                outs[PARTS][part, lines] = value
+            if len(outs) > parts:
+                outs[parts][part, lines] = value
 
 
 def join(pairs, together):
     whole = pl.BlockSpec(memory_space=pltpu.VMEM)
     count, *rest = pairs[0][0].shape
-    shapes = [jax.ShapeDtypeStruct((2 * count, *rest), bf16)] * PARTS
+    parts = len(pairs)
+    shapes = [jax.ShapeDtypeStruct((2 * count, *rest), bf16)] * parts
     if together:
-        shapes.append(jax.ShapeDtypeStruct((PARTS, 2 * count, *rest), bf16))
+        shapes.append(jax.ShapeDtypeStruct((parts, 2 * count, *rest), bf16))
     return pl.pallas_call(
         join_kernel,
         out_shape=shapes,
-        in_specs=[whole] * (2 * PARTS),
+        in_specs=[whole] * (2 * parts),
         out_specs=[whole] * len(shapes),
         compiler_params=pltpu.CompilerParams(vmem_limit_bytes=12 * 2**20),
         cost_estimate=small_cost(0, 16 * PARTS * pairs[0][0].size),
@@ -233,7 +237,7 @@
 
 
 def guide_kernel(shares_ref, place_ref, *refs):
-    ins, outs = refs[: 2 * PARTS], refs[2 * PARTS :]
+    ins, outs = refs[: 2 * GROUPS], refs[2 * GROUPS :]
     devices, held = shares_ref.shape
     total = jnp.sum(shares_ref[...].reshape(devices // NY, NY, held), 0)
     scale = lax.rsqrt(total / D + EPSILON)
@@ -244,15 +248,17 @@
         here = lane + quarter * held == place
         chosen = chosen + jnp.where(here, scale[quarter : quarter + 1, :], 0.0)
     chosen = jnp.sum(chosen, 1, keepdims=True)
-    rows = ins[0].shape[1]
+    parts_each = PARTS // GROUPS
+    rows = ins[0].shape[1] // parts_each
     half = rows // 2
     for part in range(PARTS):
         kept = GUIDANCE * chosen[part * rows : part * rows + half]
         taken = (GUIDANCE - 1.0) * chosen[part * rows + half : (part + 1) * rows]
+        first = part % parts_each * rows
         for slot in range(outs[part].shape[0]):
-            ref = ins[2 * part + slot // 2]
-            both = kept * ref[slot % 2, :half, :].astype(f32)
-            both = both - taken * ref[slot % 2, half:, :].astype(f32)
+            ref = ins[part // parts_each * 2 + slot // 2]
+            both = kept * ref[slot % 2, first : first + half, :].astype(f32)
+            both = both - taken * ref[slot % 2, first + half : first + rows, :].astype(f32)
             outs[part][slot] = both.astype(bf16)
 
 
@@ -261,8 +267,8 @@
     whole = pl.BlockSpec(memory_space=pltpu.VMEM)
     return pl.pallas_call(
         guide_kernel,
-        out_shape=[jax.ShapeDtypeStruct((4, rows // 2, features), bf16)] * PARTS,
-        in_specs=[whole] * (2 + 2 * PARTS),
+        out_shape=[jax.ShapeDtypeStruct((4, rows * GROUPS // PARTS // 2, features), bf16)] * PARTS,
+        in_specs=[whole] * (2 + 2 * GROUPS),
         out_specs=[whole] * PARTS,
         compiler_params=pltpu.CompilerParams(vmem_limit_bytes=12 * 2**20),
         cost_estimate=small_cost(0, 16 * PARTS * pairs[0][0].size),
@@ -442,16 +448,17 @@
     order = jnp.arange(row_count, dtype=jnp.int32)
     place = jnp.sum(jnp.where(grid == rows_of(quarters)[None, :], order[None, :], 0), 1)
 
-    parts = pick_rows(pick, [scaled, got[1], got[2], got[3]])
+    groups = pick_rows(pick, [scaled, got[1], got[2], got[3]])
     squares_out = jnp.sum(rounded * rounded, 1)
     shares = lax.all_to_all(
         jnp.broadcast_to(squares_out, (NX * NZ * NC * NY, SQUARES_COPIES, held)), ALL, 0, 0
     )[:, 0]
-    parts = join([(part, swap(part, i, 0)) for i, part in enumerate(parts)], False)
-    parts = [(part, swap(part, i, 1)) for i, part in enumerate(parts)]
-    shares, first = lax.optimization_barrier((shares, parts[0][1]))
-    parts[0] = (parts[0][0], first)
-    parts = guide_pairs(shares, place[:, None], parts)
+    first_parts = range(0, PARTS, PARTS // GROUPS)
+    groups = join([(group, swap(group, i, 0)) for i, group in zip(first_parts, groups)], False)
+    groups = [(group, swap(group, i, 1)) for i, group in zip(first_parts, groups)]
+    shares, first = lax.optimization_barrier((shares, groups[0][1]))
+    groups[0] = (groups[0][0], first)
+    parts = guide_pairs(shares, place[:, None], groups)
     *near, together = join([(part, swap(part, i, 2)) for i, part in enumerate(parts)], True)
     far = shift(together, "c", 1)
     near_later = [swap(part, i, 3) for i, part in enumerate(near)]

time: 164 us -> 169 us (1.030)
  waiting for transfers between devices: 49.6 us -> 62.4 us
  starting transfers between devices: 55.2 us -> 47 us
    all_to_all x1, waiting for transfers between devices: 0.01 us -> 10.8 us  [local(): lax.all_to_all(jnp.broadcast_to(squares_out, (NX * NZ * NC * NY, SQUARES_...]
    ppermute x16 -> x12, starting transfers between devices: 17.7 us -> 7.9 us  [swap(): lax.ppermute(value, axis, [(i, i ^ by) for i in range(lax.axis_size(axis))])]
    all_to_all x1, starting transfers between devices: 4.94 us -> 9.76 us  [local(): lax.all_to_all(jnp.broadcast_to(squares_out, (NX * NZ * NC * NY, SQUARES_...]
    ppermute x10, starting transfers between devices: 16.4 us -> 13.1 us  [shift(): lax.ppermute(value, axis, [(i, (i + by) % size) for i in range(size)])]
    ppermute x10, waiting for transfers between devices: 4.36 us -> 7.55 us  [shift(): lax.ppermute(value, axis, [(i, (i + by) % size) for i in range(size)])]
    ppermute x16 -> x12, waiting for transfers between devices: 14.1 us -> 13.1 us  [swap(): lax.ppermute(value, axis, [(i, i ^ by) for i in range(lax.axis_size(axis))])]
  transfers between devices with their start and end apart: 29 -> 25, of which waited for: 16 -> 13; matrix products, arithmetic and copies ran while one was open for 4% -> 4% of each run, Pallas kernels for 2% -> 1%
where the time goes in v4:
time: 169 us; the launch traced here: 168 us
  waiting for transfers between devices  62.4 us (37%)
  starting transfers between devices  47 us (28%)
  Pallas kernels  21.2 us (13%)
  blocking collectives  15.7 us (9%)
  local copies, waits for them, and re-layouts  8.4 us (5%)
  matrix products  6.99 us (4%)
  other arithmetic  5.84 us (3%)
    all_to_all x1, waiting for transfers between devices, local(): lax.all_to_all(mine.reshape(NX * NZ, local_rows, -1), ('x', 'z'), 0, 0)  18.9 us
    all_to_all x1, blocking collectives, local(): lax.all_to_all(jnp.broadcast_to(shares[0], (NX * NZ * NC * NY, pair_count...  15.7 us
    ppermute x12, waiting for transfers between devices, swap(): lax.ppermute(value, axis, [(i, i ^ by) for i in range(lax.axis_size(axis))])  13.1 us
    ppermute x10, starting transfers between devices, shift(): lax.ppermute(value, axis, [(i, (i + by) % size) for i in range(size)])  13.1 us
    all_to_all x1, waiting for transfers between devices, local(): lax.all_to_all(blocks.reshape(-1, share, query_cols), ('x', 'z', 'y'), 0, 0)  12.1 us
    all_to_all x1, waiting for transfers between devices, local(): lax.all_to_all(jnp.broadcast_to(squares_out, (NX * NZ * NC * NY, SQUARES_...  10.8 us
    pallas_call x1, Pallas kernels, vocab_logits(): pl.pallas_call(functools.partial(vocab_kernel, count), out_shape=(jax.Sha...  10.2 us
    all_to_all x1, starting transfers between devices, local(): lax.all_to_all(jnp.broadcast_to(squares_out, (NX * NZ * NC * NY, SQUARES_...  9.76 us
  transfers between devices with their start and end apart: 25, of which 13 were waited for; matrix products, arithmetic and copies ran while one was open for 4% of the time, Pallas kernels for 1%

profile of v4, /device:TPU:1, one launch (start us, length us, event | category | flops | bytes accessed | tf_op | source)
XLA Modules:
  0.0 168.0 jit_solution(14897348546286473900)
XLA Ops:
  0.0 3.6 %shard_map.118 = bf16[256,2688]{1,0:T(8,128)(2,1)} custom-call(s32[1]{0:T(128)} %bitcast.39.core_ref, bf16[16,2,16,256]{3,2,1,0:T(8,128)(2,1)} %bitcast.108, f32[1,256]{1,0:T(1,128)} %bitcast.113, bf16[256,2048]{1,0:T(8,128)(2,1)} %query_ref.3, bf16[256,2,256]{2,1,0:T(2,128)(2,1)} %keyval_ref.3), custom_call_target="tpu_custom_call" | custom-call | flops 352321536 | bytes 2752512 | tf_op jit(solution)/shard_map/pallas_call | solution.py:170
  3.6 1.4 collective-permute-start
  5.0 3.0 %collective-permute-done.refs_0_ = bf16[256,2688]{1,0:T(8,128)(2,1)S(1)} collective-permute-done((bf16[256,2688]{1,0:T(8,128)(2,1)}, bf16[256,2688]{1,0:T(8,128)(2,1)S(1)}, u32[]{:S(2)}, u32[]{:S(2)}) %collective-permute-start) | collective-permute-done | bytes 1376288 | tf_op jit(solution)/shard_map/ppermute | solution.py:35
  8.0 2.2 %shard_map.119 = bf16[256,2688]{1,0:T(8,128)(2,1)} custom-call(s32[1]{0:T(128)} %bitcast.36.core_ref, bf16[16,2,16,256]{3,2,1,0:T(8,128)(2,1)S(1)} %bitcast.109, f32[1,256]{1,0:T(1,128)S(1)} %bitcast.114, bf16[256,2048]{1,0:T(8,128)(2,1)S(1)} %copy-done.3, bf16[256,2,256]{2,1,0:T(2,128)(2,1)S(1)} %copy-done.5, bf16[256,2688]{1,0:T(8,128)(2,1)S(1)} %collective-permute-done.refs_0_), custom_call_target="tpu_custom_call" | custom-call | flops 352321536 | bytes 2752512 | tf_op jit(solution)/shard_map/pallas_call | solution.py:170
  10.2 7.9 %all-to-all-start = ((bf16[16,16,2688]{2,1,0:T(8,128)(2,1)}), bf16[16,16,2688]{2,1,0:T(8,128)(2,1)}, u32[]{:S(2)}, u32[]{:S(2)}) async-start(bf16[16,16,2688]{2,1,0:T(8,128)(2,1)} %bitcast.40), calls=%async_computation | async-start | bytes 2752512 | tf_op jit(solution)/shard_map/all_to_all | solution.py:399
  18.3 18.9 %all-to-all-done = bf16[16,16,2688]{2,1,0:T(8,128)(2,1)} async-done(((bf16[16,16,2688]{2,1,0:T(8,128)(2,1)}), bf16[16,16,2688]{2,1,0:T(8,128)(2,1)}, u32[]{:S(2)}, u32[]{:S(2)}) %all-to-all-start) | async-done | bytes 1376288 | tf_op jit(solution)/shard_map/all_to_all | solution.py:399
  37.2 1.5 convert_reduce_fusion
  38.7 0.2 fusion.18
  39.4 0.2 fusion.11
  39.6 1.0 fusion.26
  40.7 0.2 fusion.2
  41.0 0.6 fusion.1
  41.6 1.1 shard_map.120
  42.7 8.4 %all-to-all-start.1 = ((bf16[64,4,2048]{2,1,0:T(4,128)(2,1)}), bf16[64,4,2048]{2,1,0:T(4,128)(2,1)S(1)}, u32[]{:S(2)}, u32[]{:S(2)}) async-start(bf16[64,4,2048]{2,1,0:T(4,128)(2,1)} %bitcast.48), calls=%async_computation.1 | async-start | bytes 2097152 | tf_op jit(solution)/shard_map/all_to_all | solution.py:418
  51.3 2.2 %shard_map.121 = bf16[8192,256]{1,0:T(8,128)(2,1)S(1)} custom-call(bf16[8192,256]{1,0:T(8,128)(2,1)} %w_ref.1, bf16[16,2048]{1,0:T(8,128)(2,1)S(1)} %bitcast.110), custom_call_target="tpu_custom_call" | custom-call | bytes 8388608 | tf_op jit(solution)/shard_map/pallas_call | solution.py:102
  53.5 1.9 %copy-done.1 = bf16[8192,256]{1,0:T(8,128)(2,1)} copy-done((bf16[8192,256]{1,0:T(8,128)(2,1)}, bf16[8192,256]{1,0:T(8,128)(2,1)S(1)}, u32[]{:S(2)}) %copy-start.1) | copy-done | bytes 4194328
  55.5 12.1 %all-to-all-done.1 = bf16[64,4,2048]{2,1,0:T(4,128)(2,1)S(1)} async-done(((bf16[64,4,2048]{2,1,0:T(4,128)(2,1)}), bf16[64,4,2048]{2,1,0:T(4,128)(2,1)S(1)}, u32[]{:S(2)}, u32[]{:S(2)}) %all-to-all-start.1) | async-done | bytes 1048608 | tf_op jit(solution)/shard_map/all_to_all | solution.py:418
  67.5 0.9 copy.60
  68.4 0.6 copy.75
  69.0 3.2 %collective-permute-start.1 = (bf16[64,8192]{1,0:T(8,128)(2,1)S(1)}, bf16[64,8192]{1,0:T(8,128)(2,1)}, u32[]{:S(2)}, u32[]{:S(2)}) collective-permute-start(bf16[64,8192]{1,0:T(8,128)(2,1)S(1)} %bitcast.119), channel_id=1, source_target_pairs={{0,4},{4,0},{1,5},{5,1},{2,6},{6,2},{3,7},{7,3},{8,12},{12,8},{9,1... | collective-permute-start | bytes 3145736 | tf_op jit(solution)/shard_map/ppermute | solution.py:35
  72.9 3.1 %fusion.27 = f32[64,256]{1,0:T(8,128)S(1)} fusion(bf16[64,8192]{1,0:T(8,128)(2,1)S(1)} %bitcast.120, bf16[8192,256]{1,0:T(8,128)(2,1)} %copy-done.1), kind=kOutput, calls=%fused_computation.76 | convolution fusion | flops 268435456 | bytes 5308416 | tf_op jit(solution)/shard_map/dot_general | solution.py:423
  76.1 0.3 copy-done.2
  76.4 2.0 %broadcast_select_fusion.1 = (f32[64,256]{1,0:T(8,128)S(1)}, f32[64,256]{1,0:T(8,128)S(1)}) fusion(f32[64,256]{1,0:T(8,128)S(1)} %fusion.27, pred[]{:T(512)S(6)} %eq.65, bf16[64,8192]{1,0:T(8,128)(2,1)} %collective-permute-done.1, bf16[8192,256]{1,0:T(8,128)(2,1)S(1)} %copy-done.2), kind=kOutput, calls=%fused_computation.36 | convolution fusion | flops 268468224 | bytes 5439489 | tf_op jit(solution)/shard_map/dot_general | solution.py:424
  78.5 0.6 collective-permute-start.2
  79.1 1.2 collective-permute-start.3
  80.3 1.4 collective-permute-start.4
  81.8 0.1 compare_convert_fusion.pick_ref
  81.9 2.9 %collective-permute-done.2.refs_1_ = bf16[128,256]{1,0:T(8,128)(2,1)S(1)} collective-permute-done((bf16[128,256]{1,0:T(8,128)(2,1)S(1)}, bf16[128,256]{1,0:T(8,128)(2,1)S(1)}, u32[]{:S(2)}, u32[]{:S(2)}) %collective-permute-start.2) | collective-permute-done | bytes 65568 | tf_op jit(solution)/shard_map/ppermute | solution.py:35
  84.8 0.3 collective-permute-done.4.refs_3_
  85.1 0.4 shard_map.122
  85.5 0.2 collective-permute-start.5
  85.9 3.5 %collective-permute-done.5.refs_1_ = bf16[1,256,256]{2,1,0:T(8,128)(2,1)S(1)} collective-permute-done((bf16[1,256,256]{2,1,0:T(8,128)(2,1)S(1)}, bf16[1,256,256]{2,1,0:T(8,128)(2,1)S(1)}, u32[]{:S(2)}, u32[]{:S(2)}) %collective-permute-start.5) | collective-permute-done | bytes 131104 | tf_op jit(solution)/shard_map/ppermute | solution.py:40
  89.4 0.1 collective-permute-done.6.refs_3_
  89.6 1.2 collective-permute-start.7
  90.8 1.0 collective-permute-start.8
  92.0 0.7 broadcast_in_dim.42
  92.8 9.8 %all-to-all-start.2 = ((f32[128,4,128]{2,1,0:T(4,128)}), f32[128,4,128]{2,1,0:T(4,128)S(1)}, u32[]{:S(2)}, u32[]{:S(2)}) async-start(f32[128,4,128]{2,1,0:T(4,128)} %broadcast_in_dim.42), calls=%async_computation.2 | async-start | bytes 524288 | tf_op jit(solution)/shard_map/all_to_all | solution.py:453
  102.6 0.3 select_reduce_fusion
  102.9 0.1 copy.63.place_ref
  103.1 10.8 %all-to-all-done.2 = f32[128,4,128]{2,1,0:T(4,128)S(1)} async-done(((f32[128,4,128]{2,1,0:T(4,128)}), f32[128,4,128]{2,1,0:T(4,128)S(1)}, u32[]{:S(2)}, u32[]{:S(2)}) %all-to-all-start.2) | async-done | bytes 262176 | tf_op jit(solution)/shard_map/all_to_all | solution.py:453
  113.9 0.4 shard_map.124
  114.3 0.5 collective-permute-start.10
  114.8 0.3 collective-permute-start.11
  115.1 0.7 collective-permute-start.12
  115.8 0.3 collective-permute-start.9
  116.1 4.3 %collective-permute-done.10.refs_3_ = bf16[4,64,256]{2,1,0:T(8,128)(2,1)S(1)} collective-permute-done((bf16[4,64,256]{2,1,0:T(8,128)(2,1)S(1)}, bf16[4,64,256]{2,1,0:T(8,128)(2,1)S(1)}, u32[]{:S(2)}, u32[]{:S(2)}) %collective-permute-start.10) | collective-permute-done | bytes 131104 | tf_op jit(solution)/shard_map/ppermute | solution.py:40
  120.5 1.1 shard_map.125
  121.6 2.1 %collective-permute-start.13 = (bf16[4,8,64,256]{3,2,1,0:T(8,128)(2,1)}, bf16[4,8,64,256]{3,2,1,0:T(8,128)(2,1)S(1)}, u32[]{:S(2)}, u32[]{:S(2)}) collective-permute-start(bf16[4,8,64,256]{3,2,1,0:T(8,128)(2,1)} %get-tuple-element.40), channel_id=1, source_target_pairs={{0,4},{4,0},{1,5},{5,1},{2,6},{6,2},{3,7},{7,3},{8,12},{12,8},{9,1... | collective-permute-start | bytes 3145736 | tf_op jit(solution)/shard_map/ppermute | solution.py:35
  123.7 2.0 %collective-permute-start.14 = (bf16[8,64,256]{2,1,0:T(8,128)(2,1)S(1)}, bf16[8,64,256]{2,1,0:T(8,128)(2,1)}, u32[]{:S(2)}, u32[]{:S(2)}) collective-permute-start(bf16[8,64,256]{2,1,0:T(8,128)(2,1)S(1)} %get-tuple-element.36.refs_0_), channel_id=1, source_target_pairs={{0,24},{8,16},{16,8},{24,0},{1,25},{9,17},{17,9},{25,1},{2,26},{10... | collective-permute-start | bytes 786440 | tf_op jit(solution)/shard_map/ppermute | solution.py:40
  125.7 1.6 collective-permute-start.16
  127.2 0.7 copy-done.7
  127.9 5.0 %collective-permute-done.14.refs_5_ = bf16[8,64,256]{2,1,0:T(8,128)(2,1)} collective-permute-done((bf16[8,64,256]{2,1,0:T(8,128)(2,1)S(1)}, bf16[8,64,256]{2,1,0:T(8,128)(2,1)}, u32[]{:S(2)}, u32[]{:S(2)}) %collective-permute-start.14) | collective-permute-done | bytes 262176 | tf_op jit(solution)/shard_map/ppermute | solution.py:40
  132.9 0.8 collective-permute-start.18
  133.7 0.8 collective-permute-start.19
  134.6 1.1 collective-permute-start.20
  135.7 0.3 collective-permute-start.21
  136.2 1.0 collective-permute-done.20.refs_11_
  137.2 0.4 collective-permute-done.21.refs_12_
  137.6 0.9 copy-done.8
  138.6 10.2 %shard_map.126 = (f32[1002,256]{1,0:T(8,128)S(1)}, f32[1,256]{1,0:T(1,128)S(1)}) custom-call(s32[33]{0:T(128)S(1)} %stack.135.places, bf16[1002,8192]{1,0:T(8,128)(2,1)} %bitcast.116, bf16[8,64,256]{2,1,0:T(8,128)(2,1)S(1)} %get-tuple-element.36.refs_0_, bf16[8,64,256]{2,1,0:T(8,128)(2,1)S(1)} %get-tuple-element.37.refs_1_, ...), custom_call_target="tpu_custom_call" | custom-call | flops 4202692608 | bytes 16416768 | tf_op jit(solution)/shard_map/pallas_call | solution.py:349
  148.8 1.0 copy-done.6
  149.8 15.7 %all_to_all.24 = f32[128,1,256]{2,1,0:T(1,128)S(1)} all-to-all(f32[128,1,256]{2,1,0:T(1,128)S(1)} %broadcast_in_dim.74), channel_id=1, replica_groups=mesh['x'=4,'z'=4,'c'=2,'y'=4] {'x','z','c','y'}, dimensions={0} | all-to-all | bytes 262144 | tf_op jit(solution)/shard_map/all_to_all | solution.py:486
  165.5 0.2 reduce_max.19
  165.7 2.3 %select_bitcast_fusion = f32[256,1002]{0,1:T(8,128)} fusion(f32[1002,256]{1,0:T(8,128)} %copy-done.6, f32[256]{0:T(256)S(1)} %log_add_fusion), kind=kLoop, calls=%fused_computation.7 | loop fusion | flops 769536 | bytes 2053120 | tf_op jit(solution)/shard_map/transpose | solution.py:491
  (84 shorter events, 2.5 us)
Async XLA Ops:
  0.0 39.6 %copy-start = (bf16[16,2,192,128]{3,2,1,0:T(8,128)(2,1)S(1)}, bf16[16,2,192,128]{3,2,1,0:T(8,128)(2,1)}, u32[]{:S(2)}) copy-start(bf16[16,2,192,128]{3,2,1,0:T(8,128)(2,1)} %param.17) | copy-start | bytes 4718596
  0.0 8.0 %copy-start.4 = (bf16[512,256]{1,0:T(8,128)(2,1)S(1)}, bf16[512,256]{1,0:T(8,128)(2,1)}, u32[]{:S(2)}) copy-start(bf16[512,256]{1,0:T(8,128)(2,1)} %param.12) | copy-start | bytes 786436
  0.0 8.0 %copy-start.10 = (f32[256]{0:T(256)S(1)}, f32[256]{0:T(256)}, u32[]{:S(2)}) copy-start(f32[256]{0:T(256)} %param.13) | copy-start | bytes 3076
  0.0 8.0 %copy-start.3 = (bf16[256,2048]{1,0:T(8,128)(2,1)S(1)}, bf16[256,2048]{1,0:T(8,128)(2,1)}, u32[]{:S(2)}) copy-start(bf16[256,2048]{1,0:T(8,128)(2,1)} %query_ref.3) | copy-start | bytes 3145732
  0.0 8.0 %copy-start.5 = (bf16[256,2,256]{2,1,0:T(2,128)(2,1)S(1)}, bf16[256,2,256]{2,1,0:T(2,128)(2,1)}, u32[]{:S(2)}) copy-start(bf16[256,2,256]{2,1,0:T(2,128)(2,1)} %keyval_ref.3) | copy-start | bytes 786436
  3.6 4.4 %collective-permute-start = (bf16[256,2688]{1,0:T(8,128)(2,1)}, bf16[256,2688]{1,0:T(8,128)(2,1)S(1)}, u32[]{:S(2)}, u32[]{:S(2)}) collective-permute-start(bf16[256,2688]{1,0:T(8,128)(2,1)} %shard_map.118), channel_id=1, source_target_pairs={{0,4},{4,0},{1,5},{5,1},{2,6},{6,2},{3,7},{7,3},{8,12},{12,8},{9,1... | collective-permute-start | bytes 4128776 | tf_op jit(solution)/shard_map/ppermute | solution.py:35
  10.2 7.9 %copy-start.13 = (s32[16]{0:T(128)S(1)}, s32[16]{0:T(128)}, u32[]{:S(2)}) copy-start(s32[16]{0:T(128)} %param.19) | copy-start | bytes 196
  10.2 27.0 %all-to-all-start = ((bf16[16,16,2688]{2,1,0:T(8,128)(2,1)}), bf16[16,16,2688]{2,1,0:T(8,128)(2,1)}, u32[]{:S(2)}, u32[]{:S(2)}) async-start(bf16[16,16,2688]{2,1,0:T(8,128)(2,1)} %bitcast.40), calls=%async_computation | async-start | bytes 2752512 | tf_op jit(solution)/shard_map/all_to_all | solution.py:399
  39.1 1.8 %copy-start.14 = (bf16[16,2,192,128]{3,2,1,0:T(8,128)(2,1)S(1)}, bf16[16,2,192,128]{3,2,1,0:T(8,128)(2,1)}, u32[]{:S(2)}) copy-start(bf16[16,2,192,128]{3,2,1,0:T(8,128)(2,1)} %param.18) | copy-start | bytes 4718596
  42.7 24.8 %all-to-all-start.1 = ((bf16[64,4,2048]{2,1,0:T(4,128)(2,1)}), bf16[64,4,2048]{2,1,0:T(4,128)(2,1)S(1)}, u32[]{:S(2)}, u32[]{:S(2)}) async-start(bf16[64,4,2048]{2,1,0:T(4,128)(2,1)} %bitcast.48), calls=%async_computation.1 | async-start | bytes 2097152 | tf_op jit(solution)/shard_map/all_to_all | solution.py:418
  53.5 2.0 %copy-start.1 = (bf16[8192,256]{1,0:T(8,128)(2,1)}, bf16[8192,256]{1,0:T(8,128)(2,1)S(1)}, u32[]{:S(2)}) copy-start(bf16[8192,256]{1,0:T(8,128)(2,1)S(1)} %shard_map.121) | copy-start | bytes 12582916
  68.4 4.2 %copy-start.11 = (s32[512]{0:T(512)S(1)}, s32[512]{0:T(512)}, u32[]{:S(2)}) copy-start(s32[512]{0:T(512)} %param.22) | copy-start | bytes 6148
  69.0 7.1 %collective-permute-start.1 = (bf16[64,8192]{1,0:T(8,128)(2,1)S(1)}, bf16[64,8192]{1,0:T(8,128)(2,1)}, u32[]{:S(2)}, u32[]{:S(2)}) collective-permute-start(bf16[64,8192]{1,0:T(8,128)(2,1)S(1)} %bitcast.119), channel_id=1, source_target_pairs={{0,4},{4,0},{1,5},{5,1},{2,6},{6,2},{3,7},{7,3},{8,12},{12,8},{9,1... | collective-permute-start | bytes 3145736 | tf_op jit(solution)/shard_map/ppermute | solution.py:35
  72.9 3.5 %copy-start.2 = (bf16[8192,256]{1,0:T(8,128)(2,1)S(1)}, bf16[8192,256]{1,0:T(8,128)(2,1)}, u32[]{:S(2)}) copy-start(bf16[8192,256]{1,0:T(8,128)(2,1)} %copy-done.1) | copy-start | bytes 12582916
  76.1 2.4 %copy-start.12 = (f32[256]{0:T(256)S(1)}, f32[256]{0:T(256)}, u32[]{:S(2)}) copy-start(f32[256]{0:T(256)} %param.20) | copy-start | bytes 3076
  78.5 6.4 %collective-permute-start.2 = (bf16[128,256]{1,0:T(8,128)(2,1)S(1)}, bf16[128,256]{1,0:T(8,128)(2,1)S(1)}, u32[]{:S(2)}, u32[]{:S(2)}) collective-permute-start(bf16[128,256]{1,0:T(8,128)(2,1)S(1)} %get-tuple-element.45.refs_0_), channel_id=1, source_target_pairs={{0,1},{1,2},{2,3},{3,0},{4,5},{5,6},{6,7},{7,4},{8,9},{9,10},{10,1... | collective-permute-start | bytes 196616 | tf_op jit(solution)/shard_map/ppermute | solution.py:35
  79.1 5.8 %collective-permute-start.3 = (bf16[128,256]{1,0:T(8,128)(2,1)S(1)}, bf16[128,256]{1,0:T(8,128)(2,1)S(1)}, u32[]{:S(2)}, u32[]{:S(2)}) collective-permute-start(bf16[128,256]{1,0:T(8,128)(2,1)S(1)} %get-tuple-element.45.refs_0_), channel_id=1, source_target_pairs={{0,2},{1,3},{2,0},{3,1},{4,6},{5,7},{6,4},{7,5},{8,10},{9,11},{10,... | collective-permute-start | bytes 196616 | tf_op jit(solution)/shard_map/ppermute | solution.py:35
  80.3 4.8 %collective-permute-start.4 = (bf16[128,256]{1,0:T(8,128)(2,1)S(1)}, bf16[128,256]{1,0:T(8,128)(2,1)S(1)}, u32[]{:S(2)}, u32[]{:S(2)}) collective-permute-start(bf16[128,256]{1,0:T(8,128)(2,1)S(1)} %get-tuple-element.45.refs_0_), channel_id=1, source_target_pairs={{0,3},{1,0},{2,1},{3,2},{4,7},{5,4},{6,5},{7,6},{8,11},{9,8},{10,9... | collective-permute-start | bytes 196616 | tf_op jit(solution)/shard_map/ppermute | solution.py:35
  85.5 3.9 %collective-permute-start.5 = (bf16[1,256,256]{2,1,0:T(8,128)(2,1)S(1)}, bf16[1,256,256]{2,1,0:T(8,128)(2,1)S(1)}, u32[]{:S(2)}, u32[]{:S(2)}) collective-permute-start(bf16[1,256,256]{2,1,0:T(8,128)(2,1)S(1)} %get-tuple-element.26.refs_0_), channel_id=1, source_target_pairs={{0,32},{32,0},{64,96},{96,64},{1,33},{33,1},{65,97},{97,65},{2,34}... | collective-permute-start | bytes 393224 | tf_op jit(solution)/shard_map/ppermute | solution.py:40
  85.7 3.8 %collective-permute-start.6 = (bf16[1,256,256]{2,1,0:T(8,128)(2,1)S(1)}, bf16[1,256,256]{2,1,0:T(8,128)(2,1)S(1)}, u32[]{:S(2)}, u32[]{:S(2)}) collective-permute-start(bf16[1,256,256]{2,1,0:T(8,128)(2,1)S(1)} %get-tuple-element.27.refs_2_), channel_id=1, source_target_pairs={{0,8},{8,0},{16,24},{24,16},{1,9},{9,1},{17,25},{25,17},{2,10},{10... | collective-permute-start | bytes 393224 | tf_op jit(solution)/shard_map/ppermute | solution.py:40
  89.6 24.3 %collective-permute-start.7 = (bf16[2,256,256]{2,1,0:T(8,128)(2,1)S(1)}, bf16[2,256,256]{2,1,0:T(8,128)(2,1)S(1)}, u32[]{:S(2)}, u32[]{:S(2)}) collective-permute-start(bf16[2,256,256]{2,1,0:T(8,128)(2,1)S(1)} %get-tuple-element.28.refs_0_), channel_id=1, source_target_pairs={{0,96},{32,64},{64,32},{96,0},{1,97},{33,65},{65,33},{97,1},{2,98}... | collective-permute-start | bytes 786440 | tf_op jit(solution)/shard_map/ppermute | solution.py:40
  90.8 23.1 %collective-permute-start.8 = (bf16[2,256,256]{2,1,0:T(8,128)(2,1)S(1)}, bf16[2,256,256]{2,1,0:T(8,128)(2,1)S(1)}, u32[]{:S(2)}, u32[]{:S(2)}) collective-permute-start(bf16[2,256,256]{2,1,0:T(8,128)(2,1)S(1)} %get-tuple-element.31.refs_2_), channel_id=1, source_target_pairs={{0,24},{8,16},{16,8},{24,0},{1,25},{9,17},{17,9},{25,1},{2,26},{10... | collective-permute-start | bytes 786440 | tf_op jit(solution)/shard_map/ppermute | solution.py:40
  92.8 21.1 %all-to-all-start.2 = ((f32[128,4,128]{2,1,0:T(4,128)}), f32[128,4,128]{2,1,0:T(4,128)S(1)}, u32[]{:S(2)}, u32[]{:S(2)}) async-start(f32[128,4,128]{2,1,0:T(4,128)} %broadcast_in_dim.42), calls=%async_computation.2 | async-start | bytes 524288 | tf_op jit(solution)/shard_map/all_to_all | solution.py:453
  102.9 34.7 %copy-start.9 = (s32[256,63]{0,1:T(8,128)S(1)}, s32[256,63]{0,1:T(8,128)}, u32[]{:S(2)}) copy-start(s32[256,63]{0,1:T(8,128)} %param.23) | copy-start | bytes 193540
  114.3 6.1 %collective-permute-start.10 = (bf16[4,64,256]{2,1,0:T(8,128)(2,1)S(1)}, bf16[4,64,256]{2,1,0:T(8,128)(2,1)S(1)}, u32[]{:S(2)}, u32[]{:S(2)}) collective-permute-start(bf16[4,64,256]{2,1,0:T(8,128)(2,1)S(1)} %get-tuple-element.33.refs_2_), channel_id=1, source_target_pairs={{0,24},{8,16},{16,8},{24,0},{1,25},{9,17},{17,9},{25,1},{2,26},{10... | collective-permute-start | bytes 393224 | tf_op jit(solution)/shard_map/ppermute | solution.py:40
  114.8 5.6 %collective-permute-start.11 = (bf16[4,64,256]{2,1,0:T(8,128)(2,1)S(1)}, bf16[4,64,256]{2,1,0:T(8,128)(2,1)S(1)}, u32[]{:S(2)}, u32[]{:S(2)}) collective-permute-start(bf16[4,64,256]{2,1,0:T(8,128)(2,1)S(1)} %get-tuple-element.34.refs_4_), channel_id=1, source_target_pairs={{0,32},{32,0},{64,96},{96,64},{1,33},{33,1},{65,97},{97,65},{2,34}... | collective-permute-start | bytes 393224 | tf_op jit(solution)/shard_map/ppermute | solution.py:40
  115.1 5.3 %collective-permute-start.12 = (bf16[4,64,256]{2,1,0:T(8,128)(2,1)S(1)}, bf16[4,64,256]{2,1,0:T(8,128)(2,1)S(1)}, u32[]{:S(2)}, u32[]{:S(2)}) collective-permute-start(bf16[4,64,256]{2,1,0:T(8,128)(2,1)S(1)} %get-tuple-element.35.refs_6_), channel_id=1, source_target_pairs={{0,96},{32,64},{64,32},{96,0},{1,97},{33,65},{65,33},{97,1},{2,98}... | collective-permute-start | bytes 393224 | tf_op jit(solution)/shard_map/ppermute | solution.py:40
  115.8 4.6 %collective-permute-start.9 = (bf16[4,64,256]{2,1,0:T(8,128)(2,1)S(1)}, bf16[4,64,256]{2,1,0:T(8,128)(2,1)S(1)}, u32[]{:S(2)}, u32[]{:S(2)}) collective-permute-start(bf16[4,64,256]{2,1,0:T(8,128)(2,1)S(1)} %get-tuple-element.32.refs_0_), channel_id=1, source_target_pairs={{0,8},{8,0},{16,24},{24,16},{1,9},{9,1},{17,25},{25,17},{2,10},{10... | collective-permute-start | bytes 393224 | tf_op jit(solution)/shard_map/ppermute | solution.py:40
  121.6 16.0 %collective-permute-start.13 = (bf16[4,8,64,256]{3,2,1,0:T(8,128)(2,1)}, bf16[4,8,64,256]{3,2,1,0:T(8,128)(2,1)S(1)}, u32[]{:S(2)}, u32[]{:S(2)}) collective-permute-start(bf16[4,8,64,256]{3,2,1,0:T(8,128)(2,1)} %get-tuple-element.40), channel_id=1, source_target_pairs={{0,4},{4,0},{1,5},{5,1},{2,6},{6,2},{3,7},{7,3},{8,12},{12,8},{9,1... | collective-permute-start | bytes 3145736 | tf_op jit(solution)/shard_map/ppermute | solution.py:35
  123.7 9.3 %collective-permute-start.14 = (bf16[8,64,256]{2,1,0:T(8,128)(2,1)S(1)}, bf16[8,64,256]{2,1,0:T(8,128)(2,1)}, u32[]{:S(2)}, u32[]{:S(2)}) collective-permute-start(bf16[8,64,256]{2,1,0:T(8,128)(2,1)S(1)} %get-tuple-element.36.refs_0_), channel_id=1, source_target_pairs={{0,24},{8,16},{16,8},{24,0},{1,25},{9,17},{17,9},{25,1},{2,26},{10... | collective-permute-start | bytes 786440 | tf_op jit(solution)/shard_map/ppermute | solution.py:40
  125.7 8.0 %collective-permute-start.15 = (bf16[8,64,256]{2,1,0:T(8,128)(2,1)S(1)}, bf16[8,64,256]{2,1,0:T(8,128)(2,1)}, u32[]{:S(2)}, u32[]{:S(2)}) collective-permute-start(bf16[8,64,256]{2,1,0:T(8,128)(2,1)S(1)} %get-tuple-element.37.refs_1_), channel_id=1, source_target_pairs={{0,8},{8,0},{16,24},{24,16},{1,9},{9,1},{17,25},{25,17},{2,10},{10... | collective-permute-start | bytes 786440 | tf_op jit(solution)/shard_map/ppermute | solution.py:40
  125.7 8.9 %collective-permute-start.16 = (bf16[8,64,256]{2,1,0:T(8,128)(2,1)S(1)}, bf16[8,64,256]{2,1,0:T(8,128)(2,1)}, u32[]{:S(2)}, u32[]{:S(2)}) collective-permute-start(bf16[8,64,256]{2,1,0:T(8,128)(2,1)S(1)} %get-tuple-element.38.refs_2_), channel_id=1, source_target_pairs={{0,96},{32,64},{64,32},{96,0},{1,97},{33,65},{65,33},{97,1},{2,98}... | collective-permute-start | bytes 786440 | tf_op jit(solution)/shard_map/ppermute | solution.py:40
  127.2 8.5 %collective-permute-start.17 = (bf16[8,64,256]{2,1,0:T(8,128)(2,1)S(1)}, bf16[8,64,256]{2,1,0:T(8,128)(2,1)}, u32[]{:S(2)}, u32[]{:S(2)}) collective-permute-start(bf16[8,64,256]{2,1,0:T(8,128)(2,1)S(1)} %get-tuple-element.39.refs_3_), channel_id=1, source_target_pairs={{0,32},{32,0},{64,96},{96,64},{1,33},{33,1},{65,97},{97,65},{2,34}... | collective-permute-start | bytes 786440 | tf_op jit(solution)/shard_map/ppermute | solution.py:40
  127.2 0.7 copy-start.7
  132.9 3.3 %collective-permute-start.18 = (bf16[8,64,256]{2,1,0:T(8,128)(2,1)}, bf16[8,64,256]{2,1,0:T(8,128)(2,1)}, u32[]{:S(2)}, u32[]{:S(2)}) collective-permute-start(bf16[8,64,256]{2,1,0:T(8,128)(2,1)} %collective-permute-done.14.refs_5_), channel_id=1, source_target_pairs={{0,4},{4,0},{1,5},{5,1},{2,6},{6,2},{3,7},{7,3},{8,12},{12,8},{9,1... | collective-permute-start | bytes 786440 | tf_op jit(solution)/shard_map/ppermute | solution.py:35
  133.7 2.5 %collective-permute-start.19 = (bf16[8,64,256]{2,1,0:T(8,128)(2,1)}, bf16[8,64,256]{2,1,0:T(8,128)(2,1)}, u32[]{:S(2)}, u32[]{:S(2)}) collective-permute-start(bf16[8,64,256]{2,1,0:T(8,128)(2,1)} %collective-permute-done.15.refs_6_), channel_id=1, source_target_pairs={{0,4},{4,0},{1,5},{5,1},{2,6},{6,2},{3,7},{7,3},{8,12},{12,8},{9,1... | collective-permute-start | bytes 786440 | tf_op jit(solution)/shard_map/ppermute | solution.py:35
  134.6 2.6 %collective-permute-start.20 = (bf16[8,64,256]{2,1,0:T(8,128)(2,1)}, bf16[8,64,256]{2,1,0:T(8,128)(2,1)}, u32[]{:S(2)}, u32[]{:S(2)}) collective-permute-start(bf16[8,64,256]{2,1,0:T(8,128)(2,1)} %collective-permute-done.16.refs_7_), channel_id=1, source_target_pairs={{0,4},{4,0},{1,5},{5,1},{2,6},{6,2},{3,7},{7,3},{8,12},{12,8},{9,1... | collective-permute-start | bytes 786440 | tf_op jit(solution)/shard_map/ppermute | solution.py:35
  135.7 1.9 %collective-permute-start.21 = (bf16[8,64,256]{2,1,0:T(8,128)(2,1)}, bf16[8,64,256]{2,1,0:T(8,128)(2,1)}, u32[]{:S(2)}, u32[]{:S(2)}) collective-permute-start(bf16[8,64,256]{2,1,0:T(8,128)(2,1)} %collective-permute-done.17.refs_8_), channel_id=1, source_target_pairs={{0,4},{4,0},{1,5},{5,1},{2,6},{6,2},{3,7},{7,3},{8,12},{12,8},{9,1... | collective-permute-start | bytes 786440 | tf_op jit(solution)/shard_map/ppermute | solution.py:35
  137.6 1.0 copy-start.8
  148.8 1.0 copy-start.6

commit v5 on v4

--- a/solution.py
+++ b/solution.py
@@ -25,7 +25,7 @@
 PARTS = 4
 ORDERS = ((0, 1, 2, 3), (0, 1, 3, 2), (2, 3, 0, 1), (2, 3, 1, 0))
 GROUPS = 2
-SQUARES_COPIES = 4
+SQUARES_COPIES = 8
 bf16 = jnp.bfloat16
 f32 = jnp.float32
 

time: 169 us -> 168 us (level)
  waiting for transfers between devices: 62.4 us -> 58.7 us
    all_to_all x1, waiting for transfers between devices: 10.8 us -> 0.01 us  [local(): lax.all_to_all(jnp.broadcast_to(squares_out, (NX * NZ * NC * NY, SQUARES_...]
    ppermute x12, waiting for transfers between devices: 13.1 us -> 23.4 us  [swap(): lax.ppermute(value, axis, [(i, i ^ by) for i in range(lax.axis_size(axis))])]
    ppermute x12, starting transfers between devices: 7.9 us -> 12.7 us  [swap(): lax.ppermute(value, axis, [(i, i ^ by) for i in range(lax.axis_size(axis))])]
    all_to_all x1, starting transfers between devices: 9.76 us -> 5.4 us  [local(): lax.all_to_all(jnp.broadcast_to(squares_out, (NX * NZ * NC * NY, SQUARES_...]
    ppermute x10, waiting for transfers between devices: 7.55 us -> 4.39 us  [shift(): lax.ppermute(value, axis, [(i, (i + by) % size) for i in range(size)])]
  transfers between devices with their start and end apart: 25 -> 25, of which waited for: 13 -> 15; matrix products, arithmetic and copies ran while one was open for 4% -> 4% of each run, Pallas kernels for 1% -> 2%
where the time goes in v5:
time: 168 us
  waiting for transfers between devices  58.7 us (35%)
  starting transfers between devices  47.4 us (28%)
  Pallas kernels  21.2 us (13%)
  blocking collectives  17.3 us (10%)
  local copies, waits for them, and re-layouts  9.52 us (6%)
  matrix products  6.99 us (4%)
  other arithmetic  5.85 us (3%)
    ppermute x12, waiting for transfers between devices, swap(): lax.ppermute(value, axis, [(i, i ^ by) for i in range(lax.axis_size(axis))])  23.4 us
    all_to_all x1, waiting for transfers between devices, local(): lax.all_to_all(mine.reshape(NX * NZ, local_rows, -1), ('x', 'z'), 0, 0)  18.9 us
    all_to_all x1, blocking collectives, local(): lax.all_to_all(jnp.broadcast_to(shares[0], (NX * NZ * NC * NY, pair_count...  17.3 us
    ppermute x10, starting transfers between devices, shift(): lax.ppermute(value, axis, [(i, (i + by) % size) for i in range(size)])  13 us
    ppermute x12, starting transfers between devices, swap(): lax.ppermute(value, axis, [(i, i ^ by) for i in range(lax.axis_size(axis))])  12.7 us
    all_to_all x1, waiting for transfers between devices, local(): lax.all_to_all(blocks.reshape(-1, share, query_cols), ('x', 'z', 'y'), 0, 0)  12.1 us
    pallas_call x1, Pallas kernels, vocab_logits(): pl.pallas_call(functools.partial(vocab_kernel, count), out_shape=(jax.Sha...  10.2 us
    all_to_all x1, starting transfers between devices, local(): lax.all_to_all(blocks.reshape(-1, share, query_cols), ('x', 'z', 'y'), 0, 0)  8.44 us
  transfers between devices with their start and end apart: 25, of which 15 were waited for; matrix products, arithmetic and copies ran while one was open for 4% of the time, Pallas kernels for 2%

profile of v5, /device:TPU:1, one launch (start us, length us, event | category | flops | bytes accessed | tf_op | source)
XLA Modules:
  0.0 167.5 jit_solution(9403654053371047849)
XLA Ops:
  0.0 3.6 %shard_map.118 = bf16[256,2688]{1,0:T(8,128)(2,1)} custom-call(s32[1]{0:T(128)} %bitcast.39.core_ref, bf16[16,2,16,256]{3,2,1,0:T(8,128)(2,1)} %bitcast.108, f32[1,256]{1,0:T(1,128)} %bitcast.113, bf16[256,2048]{1,0:T(8,128)(2,1)} %query_ref.3, bf16[256,2,256]{2,1,0:T(2,128)(2,1)} %keyval_ref.3), custom_call_target="tpu_custom_call" | custom-call | flops 352321536 | bytes 2752512 | tf_op jit(solution)/shard_map/pallas_call | solution.py:170
  3.6 1.4 collective-permute-start
  5.0 3.0 %collective-permute-done.refs_0_ = bf16[256,2688]{1,0:T(8,128)(2,1)S(1)} collective-permute-done((bf16[256,2688]{1,0:T(8,128)(2,1)}, bf16[256,2688]{1,0:T(8,128)(2,1)S(1)}, u32[]{:S(2)}, u32[]{:S(2)}) %collective-permute-start) | collective-permute-done | bytes 1376288 | tf_op jit(solution)/shard_map/ppermute | solution.py:35
  8.0 2.2 %shard_map.119 = bf16[256,2688]{1,0:T(8,128)(2,1)} custom-call(s32[1]{0:T(128)} %bitcast.36.core_ref, bf16[16,2,16,256]{3,2,1,0:T(8,128)(2,1)S(1)} %bitcast.109, f32[1,256]{1,0:T(1,128)S(1)} %bitcast.114, bf16[256,2048]{1,0:T(8,128)(2,1)S(1)} %copy-done.3, bf16[256,2,256]{2,1,0:T(2,128)(2,1)S(1)} %copy-done.5, bf16[256,2688]{1,0:T(8,128)(2,1)S(1)} %collective-permute-done.refs_0_), custom_call_target="tpu_custom_call" | custom-call | flops 352321536 | bytes 2752512 | tf_op jit(solution)/shard_map/pallas_call | solution.py:170
  10.2 7.9 %all-to-all-start = ((bf16[16,16,2688]{2,1,0:T(8,128)(2,1)}), bf16[16,16,2688]{2,1,0:T(8,128)(2,1)}, u32[]{:S(2)}, u32[]{:S(2)}) async-start(bf16[16,16,2688]{2,1,0:T(8,128)(2,1)} %bitcast.40), calls=%async_computation | async-start | bytes 2752512 | tf_op jit(solution)/shard_map/all_to_all | solution.py:399
  18.3 18.9 %all-to-all-done = bf16[16,16,2688]{2,1,0:T(8,128)(2,1)} async-done(((bf16[16,16,2688]{2,1,0:T(8,128)(2,1)}), bf16[16,16,2688]{2,1,0:T(8,128)(2,1)}, u32[]{:S(2)}, u32[]{:S(2)}) %all-to-all-start) | async-done | bytes 1376288 | tf_op jit(solution)/shard_map/all_to_all | solution.py:399
  37.2 1.5 convert_reduce_fusion
  38.7 0.2 fusion.18
  39.4 0.2 fusion.11
  39.6 1.0 fusion.26
  40.7 0.2 fusion.2
  41.0 0.6 fusion.1
  41.6 1.1 shard_map.120
  42.7 8.4 %all-to-all-start.1 = ((bf16[64,4,2048]{2,1,0:T(4,128)(2,1)}), bf16[64,4,2048]{2,1,0:T(4,128)(2,1)S(1)}, u32[]{:S(2)}, u32[]{:S(2)}) async-start(bf16[64,4,2048]{2,1,0:T(4,128)(2,1)} %bitcast.48), calls=%async_computation.1 | async-start | bytes 2097152 | tf_op jit(solution)/shard_map/all_to_all | solution.py:418
  51.3 2.2 %shard_map.121 = bf16[8192,256]{1,0:T(8,128)(2,1)S(1)} custom-call(bf16[8192,256]{1,0:T(8,128)(2,1)} %w_ref.1, bf16[16,2048]{1,0:T(8,128)(2,1)S(1)} %bitcast.110), custom_call_target="tpu_custom_call" | custom-call | bytes 8388608 | tf_op jit(solution)/shard_map/pallas_call | solution.py:102
  53.5 1.9 %copy-done.1 = bf16[8192,256]{1,0:T(8,128)(2,1)} copy-done((bf16[8192,256]{1,0:T(8,128)(2,1)}, bf16[8192,256]{1,0:T(8,128)(2,1)S(1)}, u32[]{:S(2)}) %copy-start.1) | copy-done | bytes 4194328
  55.5 12.1 %all-to-all-done.1 = bf16[64,4,2048]{2,1,0:T(4,128)(2,1)S(1)} async-done(((bf16[64,4,2048]{2,1,0:T(4,128)(2,1)}), bf16[64,4,2048]{2,1,0:T(4,128)(2,1)S(1)}, u32[]{:S(2)}, u32[]{:S(2)}) %all-to-all-start.1) | async-done | bytes 1048608 | tf_op jit(solution)/shard_map/all_to_all | solution.py:418
  67.5 0.9 copy.60
  68.4 0.6 copy.75
  69.0 3.2 %collective-permute-start.1 = (bf16[64,8192]{1,0:T(8,128)(2,1)S(1)}, bf16[64,8192]{1,0:T(8,128)(2,1)}, u32[]{:S(2)}, u32[]{:S(2)}) collective-permute-start(bf16[64,8192]{1,0:T(8,128)(2,1)S(1)} %bitcast.119), channel_id=1, source_target_pairs={{0,4},{4,0},{1,5},{5,1},{2,6},{6,2},{3,7},{7,3},{8,12},{12,8},{9,1... | collective-permute-start | bytes 3145736 | tf_op jit(solution)/shard_map/ppermute | solution.py:35
  72.9 3.1 %fusion.27 = f32[64,256]{1,0:T(8,128)S(1)} fusion(bf16[64,8192]{1,0:T(8,128)(2,1)S(1)} %bitcast.120, bf16[8192,256]{1,0:T(8,128)(2,1)} %copy-done.1), kind=kOutput, calls=%fused_computation.76 | convolution fusion | flops 268435456 | bytes 5308416 | tf_op jit(solution)/shard_map/dot_general | solution.py:423
  76.1 0.3 copy-done.2
  76.4 2.0 %broadcast_select_fusion.1 = (f32[64,256]{1,0:T(8,128)S(1)}, f32[64,256]{1,0:T(8,128)S(1)}) fusion(f32[64,256]{1,0:T(8,128)S(1)} %fusion.27, pred[]{:T(512)S(6)} %eq.65, bf16[64,8192]{1,0:T(8,128)(2,1)} %collective-permute-done.1, bf16[8192,256]{1,0:T(8,128)(2,1)S(1)} %copy-done.2), kind=kOutput, calls=%fused_computation.36 | convolution fusion | flops 268468224 | bytes 5439489 | tf_op jit(solution)/shard_map/dot_general | solution.py:424
  78.5 0.6 collective-permute-start.2
  79.1 1.2 collective-permute-start.3
  80.3 1.4 collective-permute-start.4
  82.0 0.8 broadcast_in_dim.42
  82.9 5.4 %all-to-all-start.2 = ((f32[128,8,128]{2,1,0:T(8,128)}), f32[128,8,128]{2,1,0:T(8,128)}, u32[]{:S(2)}, u32[]{:S(2)}) async-start(f32[128,8,128]{2,1,0:T(8,128)} %broadcast_in_dim.42), calls=%async_computation.2 | async-start | bytes 1048576 | tf_op jit(solution)/shard_map/all_to_all | solution.py:453
  88.5 0.4 shard_map.122
  88.9 1.5 collective-permute-start.5
  90.4 1.4 collective-permute-start.6
  91.8 6.1 %collective-permute-done.5.refs_1_ = bf16[1,256,256]{2,1,0:T(8,128)(2,1)S(1)} collective-permute-done((bf16[1,256,256]{2,1,0:T(8,128)(2,1)S(1)}, bf16[1,256,256]{2,1,0:T(8,128)(2,1)S(1)}, u32[]{:S(2)}, u32[]{:S(2)}) %collective-permute-start.5) | collective-permute-done | bytes 131104 | tf_op jit(solution)/shard_map/ppermute | solution.py:40
  97.8 2.2 %collective-permute-done.6.refs_3_ = bf16[1,256,256]{2,1,0:T(8,128)(2,1)S(1)} collective-permute-done((bf16[1,256,256]{2,1,0:T(8,128)(2,1)S(1)}, bf16[1,256,256]{2,1,0:T(8,128)(2,1)S(1)}, u32[]{:S(2)}, u32[]{:S(2)}) %collective-permute-start.6) | collective-permute-done | bytes 131104 | tf_op jit(solution)/shard_map/ppermute | solution.py:40
  100.1 2.1 %collective-permute-start.7 = (bf16[2,256,256]{2,1,0:T(8,128)(2,1)S(1)}, bf16[2,256,256]{2,1,0:T(8,128)(2,1)S(1)}, u32[]{:S(2)}, u32[]{:S(2)}) collective-permute-start(bf16[2,256,256]{2,1,0:T(8,128)(2,1)S(1)} %get-tuple-element.28.refs_0_), channel_id=1, source_target_pairs={{0,96},{32,64},{64,32},{96,0},{1,97},{33,65},{65,33},{97,1},{2,98}... | collective-permute-start | bytes 786440 | tf_op jit(solution)/shard_map/ppermute | solution.py:40
  102.3 2.2 %collective-permute-start.8 = (bf16[2,256,256]{2,1,0:T(8,128)(2,1)S(1)}, bf16[2,256,256]{2,1,0:T(8,128)(2,1)S(1)}, u32[]{:S(2)}, u32[]{:S(2)}) collective-permute-start(bf16[2,256,256]{2,1,0:T(8,128)(2,1)S(1)} %get-tuple-element.31.refs_2_), channel_id=1, source_target_pairs={{0,24},{8,16},{16,8},{24,0},{1,25},{9,17},{17,9},{25,1},{2,26},{10... | collective-permute-start | bytes 786440 | tf_op jit(solution)/shard_map/ppermute | solution.py:40
  104.5 0.3 select_reduce_fusion
  105.0 1.1 slice.55
  106.1 2.7 %collective-permute-done.7.refs_1_ = bf16[2,256,256]{2,1,0:T(8,128)(2,1)S(1)} collective-permute-done((bf16[2,256,256]{2,1,0:T(8,128)(2,1)S(1)}, bf16[2,256,256]{2,1,0:T(8,128)(2,1)S(1)}, u32[]{:S(2)}, u32[]{:S(2)}) %collective-permute-start.7) | collective-permute-done | bytes 262176 | tf_op jit(solution)/shard_map/ppermute | solution.py:40
  108.7 1.9 %collective-permute-done.8.refs_3_ = bf16[2,256,256]{2,1,0:T(8,128)(2,1)S(1)} collective-permute-done((bf16[2,256,256]{2,1,0:T(8,128)(2,1)S(1)}, bf16[2,256,256]{2,1,0:T(8,128)(2,1)S(1)}, u32[]{:S(2)}, u32[]{:S(2)}) %collective-permute-start.8) | collective-permute-done | bytes 262176 | tf_op jit(solution)/shard_map/ppermute | solution.py:40
  110.7 0.4 shard_map.124
  111.0 2.2 %collective-permute-start.10 = (bf16[4,64,256]{2,1,0:T(8,128)(2,1)S(1)}, bf16[4,64,256]{2,1,0:T(8,128)(2,1)S(1)}, u32[]{:S(2)}, u32[]{:S(2)}) collective-permute-start(bf16[4,64,256]{2,1,0:T(8,128)(2,1)S(1)} %get-tuple-element.33.refs_2_), channel_id=1, source_target_pairs={{0,24},{8,16},{16,8},{24,0},{1,25},{9,17},{17,9},{25,1},{2,26},{10... | collective-permute-start | bytes 393224 | tf_op jit(solution)/shard_map/ppermute | solution.py:40
  113.3 0.8 collective-permute-start.12
  114.1 2.0 %collective-permute-done.10.refs_3_ = bf16[4,64,256]{2,1,0:T(8,128)(2,1)S(1)} collective-permute-done((bf16[4,64,256]{2,1,0:T(8,128)(2,1)S(1)}, bf16[4,64,256]{2,1,0:T(8,128)(2,1)S(1)}, u32[]{:S(2)}, u32[]{:S(2)}) %collective-permute-start.10) | collective-permute-done | bytes 131104 | tf_op jit(solution)/shard_map/ppermute | solution.py:40
  116.2 1.2 collective-permute-done.11.refs_5_
  117.4 1.1 collective-permute-done.12.refs_7_
  118.5 1.1 shard_map.125
  119.6 3.2 %collective-permute-start.13 = (bf16[4,8,64,256]{3,2,1,0:T(8,128)(2,1)}, bf16[4,8,64,256]{3,2,1,0:T(8,128)(2,1)S(1)}, u32[]{:S(2)}, u32[]{:S(2)}) collective-permute-start(bf16[4,8,64,256]{3,2,1,0:T(8,128)(2,1)} %get-tuple-element.40), channel_id=1, source_target_pairs={{0,4},{4,0},{1,5},{5,1},{2,6},{6,2},{3,7},{7,3},{8,12},{12,8},{9,1... | collective-permute-start | bytes 3145736 | tf_op jit(solution)/shard_map/ppermute | solution.py:35
  122.8 0.6 collective-permute-start.14
  123.3 1.7 %collective-permute-start.16 = (bf16[8,64,256]{2,1,0:T(8,128)(2,1)S(1)}, bf16[8,64,256]{2,1,0:T(8,128)(2,1)}, u32[]{:S(2)}, u32[]{:S(2)}) collective-permute-start(bf16[8,64,256]{2,1,0:T(8,128)(2,1)S(1)} %get-tuple-element.38.refs_2_), channel_id=1, source_target_pairs={{0,96},{32,64},{64,32},{96,0},{1,97},{33,65},{65,33},{97,1},{2,98}... | collective-permute-start | bytes 786440 | tf_op jit(solution)/shard_map/ppermute | solution.py:40
  125.2 0.7 copy-done.7
  125.9 6.1 %collective-permute-done.14.refs_5_ = bf16[8,64,256]{2,1,0:T(8,128)(2,1)} collective-permute-done((bf16[8,64,256]{2,1,0:T(8,128)(2,1)S(1)}, bf16[8,64,256]{2,1,0:T(8,128)(2,1)}, u32[]{:S(2)}, u32[]{:S(2)}) %collective-permute-start.14) | collective-permute-done | bytes 262176 | tf_op jit(solution)/shard_map/ppermute | solution.py:40
  132.0 0.8 collective-permute-start.18
  132.8 0.6 collective-permute-start.20
  133.4 0.5 collective-permute-start.21
  134.0 0.3 collective-permute-done.18.refs_9_
  134.3 0.4 collective-permute-done.19.refs_10_
  134.7 0.4 collective-permute-done.20.refs_11_
  135.0 0.4 collective-permute-done.21.refs_12_
  135.4 0.9 copy-done.8
  136.4 10.2 %shard_map.126 = (f32[1002,256]{1,0:T(8,128)S(1)}, f32[1,256]{1,0:T(1,128)S(1)}) custom-call(s32[33]{0:T(128)S(1)} %stack.135.places, bf16[1002,8192]{1,0:T(8,128)(2,1)} %bitcast.116, bf16[8,64,256]{2,1,0:T(8,128)(2,1)S(1)} %get-tuple-element.36.refs_0_, bf16[8,64,256]{2,1,0:T(8,128)(2,1)S(1)} %get-tuple-element.37.refs_1_, ...), custom_call_target="tpu_custom_call" | custom-call | flops 4202692608 | bytes 16416768 | tf_op jit(solution)/shard_map/pallas_call | solution.py:349
  146.6 1.0 copy-done.6
  147.7 17.3 %all_to_all.24 = f32[128,1,256]{2,1,0:T(1,128)S(1)} all-to-all(f32[128,1,256]{2,1,0:T(1,128)S(1)} %broadcast_in_dim.74), channel_id=1, replica_groups=mesh['x'=4,'z'=4,'c'=2,'y'=4] {'x','z','c','y'}, dimensions={0} | all-to-all | bytes 262144 | tf_op jit(solution)/shard_map/all_to_all | solution.py:486
  165.0 0.2 reduce_max.19
  165.2 2.3 %select_bitcast_fusion = f32[256,1002]{0,1:T(8,128)} fusion(f32[1002,256]{1,0:T(8,128)} %copy-done.6, f32[256]{0:T(256)S(1)} %log_add_fusion), kind=kLoop, calls=%fused_computation.7 | loop fusion | flops 769536 | bytes 2053120 | tf_op jit(solution)/shard_map/transpose | solution.py:491
  (84 shorter events, 2.7 us)
Async XLA Ops:
  0.0 39.6 %copy-start = (bf16[16,2,192,128]{3,2,1,0:T(8,128)(2,1)S(1)}, bf16[16,2,192,128]{3,2,1,0:T(8,128)(2,1)}, u32[]{:S(2)}) copy-start(bf16[16,2,192,128]{3,2,1,0:T(8,128)(2,1)} %param.17) | copy-start | bytes 4718596
  0.0 8.0 %copy-start.4 = (bf16[512,256]{1,0:T(8,128)(2,1)S(1)}, bf16[512,256]{1,0:T(8,128)(2,1)}, u32[]{:S(2)}) copy-start(bf16[512,256]{1,0:T(8,128)(2,1)} %param.12) | copy-start | bytes 786436
  0.0 8.0 %copy-start.10 = (f32[256]{0:T(256)S(1)}, f32[256]{0:T(256)}, u32[]{:S(2)}) copy-start(f32[256]{0:T(256)} %param.13) | copy-start | bytes 3076
  0.0 8.0 %copy-start.3 = (bf16[256,2048]{1,0:T(8,128)(2,1)S(1)}, bf16[256,2048]{1,0:T(8,128)(2,1)}, u32[]{:S(2)}) copy-start(bf16[256,2048]{1,0:T(8,128)(2,1)} %query_ref.3) | copy-start | bytes 3145732
  0.0 8.0 %copy-start.5 = (bf16[256,2,256]{2,1,0:T(2,128)(2,1)S(1)}, bf16[256,2,256]{2,1,0:T(2,128)(2,1)}, u32[]{:S(2)}) copy-start(bf16[256,2,256]{2,1,0:T(2,128)(2,1)} %keyval_ref.3) | copy-start | bytes 786436
  3.6 4.4 %collective-permute-start = (bf16[256,2688]{1,0:T(8,128)(2,1)}, bf16[256,2688]{1,0:T(8,128)(2,1)S(1)}, u32[]{:S(2)}, u32[]{:S(2)}) collective-permute-start(bf16[256,2688]{1,0:T(8,128)(2,1)} %shard_map.118), channel_id=1, source_target_pairs={{0,4},{4,0},{1,5},{5,1},{2,6},{6,2},{3,7},{7,3},{8,12},{12,8},{9,1... | collective-permute-start | bytes 4128776 | tf_op jit(solution)/shard_map/ppermute | solution.py:35
  10.2 7.9 %copy-start.13 = (s32[16]{0:T(128)S(1)}, s32[16]{0:T(128)}, u32[]{:S(2)}) copy-start(s32[16]{0:T(128)} %param.19) | copy-start | bytes 196
  10.2 27.0 %all-to-all-start = ((bf16[16,16,2688]{2,1,0:T(8,128)(2,1)}), bf16[16,16,2688]{2,1,0:T(8,128)(2,1)}, u32[]{:S(2)}, u32[]{:S(2)}) async-start(bf16[16,16,2688]{2,1,0:T(8,128)(2,1)} %bitcast.40), calls=%async_computation | async-start | bytes 2752512 | tf_op jit(solution)/shard_map/all_to_all | solution.py:399
  39.1 1.8 %copy-start.14 = (bf16[16,2,192,128]{3,2,1,0:T(8,128)(2,1)S(1)}, bf16[16,2,192,128]{3,2,1,0:T(8,128)(2,1)}, u32[]{:S(2)}) copy-start(bf16[16,2,192,128]{3,2,1,0:T(8,128)(2,1)} %param.18) | copy-start | bytes 4718596
  42.7 24.8 %all-to-all-start.1 = ((bf16[64,4,2048]{2,1,0:T(4,128)(2,1)}), bf16[64,4,2048]{2,1,0:T(4,128)(2,1)S(1)}, u32[]{:S(2)}, u32[]{:S(2)}) async-start(bf16[64,4,2048]{2,1,0:T(4,128)(2,1)} %bitcast.48), calls=%async_computation.1 | async-start | bytes 2097152 | tf_op jit(solution)/shard_map/all_to_all | solution.py:418
  53.5 2.0 %copy-start.1 = (bf16[8192,256]{1,0:T(8,128)(2,1)}, bf16[8192,256]{1,0:T(8,128)(2,1)S(1)}, u32[]{:S(2)}) copy-start(bf16[8192,256]{1,0:T(8,128)(2,1)S(1)} %shard_map.121) | copy-start | bytes 12582916
  68.4 4.2 %copy-start.11 = (s32[512]{0:T(512)S(1)}, s32[512]{0:T(512)}, u32[]{:S(2)}) copy-start(s32[512]{0:T(512)} %param.22) | copy-start | bytes 6148
  69.0 7.1 %collective-permute-start.1 = (bf16[64,8192]{1,0:T(8,128)(2,1)S(1)}, bf16[64,8192]{1,0:T(8,128)(2,1)}, u32[]{:S(2)}, u32[]{:S(2)}) collective-permute-start(bf16[64,8192]{1,0:T(8,128)(2,1)S(1)} %bitcast.119), channel_id=1, source_target_pairs={{0,4},{4,0},{1,5},{5,1},{2,6},{6,2},{3,7},{7,3},{8,12},{12,8},{9,1... | collective-permute-start | bytes 3145736 | tf_op jit(solution)/shard_map/ppermute | solution.py:35
  72.9 3.5 %copy-start.2 = (bf16[8192,256]{1,0:T(8,128)(2,1)S(1)}, bf16[8192,256]{1,0:T(8,128)(2,1)}, u32[]{:S(2)}) copy-start(bf16[8192,256]{1,0:T(8,128)(2,1)} %copy-done.1) | copy-start | bytes 12582916
  76.1 2.4 %copy-start.12 = (f32[256]{0:T(256)S(1)}, f32[256]{0:T(256)}, u32[]{:S(2)}) copy-start(f32[256]{0:T(256)} %param.20) | copy-start | bytes 3076
  78.5 10.0 %collective-permute-start.2 = (bf16[128,256]{1,0:T(8,128)(2,1)S(1)}, bf16[128,256]{1,0:T(8,128)(2,1)S(1)}, u32[]{:S(2)}, u32[]{:S(2)}) collective-permute-start(bf16[128,256]{1,0:T(8,128)(2,1)S(1)} %get-tuple-element.45.refs_0_), channel_id=1, source_target_pairs={{0,1},{1,2},{2,3},{3,0},{4,5},{5,6},{6,7},{7,4},{8,9},{9,10},{10,1... | collective-permute-start | bytes 196616 | tf_op jit(solution)/shard_map/ppermute | solution.py:35
  79.1 9.4 %collective-permute-start.3 = (bf16[128,256]{1,0:T(8,128)(2,1)S(1)}, bf16[128,256]{1,0:T(8,128)(2,1)S(1)}, u32[]{:S(2)}, u32[]{:S(2)}) collective-permute-start(bf16[128,256]{1,0:T(8,128)(2,1)S(1)} %get-tuple-element.45.refs_0_), channel_id=1, source_target_pairs={{0,2},{1,3},{2,0},{3,1},{4,6},{5,7},{6,4},{7,5},{8,10},{9,11},{10,... | collective-permute-start | bytes 196616 | tf_op jit(solution)/shard_map/ppermute | solution.py:35
  80.3 8.1 %collective-permute-start.4 = (bf16[128,256]{1,0:T(8,128)(2,1)S(1)}, bf16[128,256]{1,0:T(8,128)(2,1)S(1)}, u32[]{:S(2)}, u32[]{:S(2)}) collective-permute-start(bf16[128,256]{1,0:T(8,128)(2,1)S(1)} %get-tuple-element.45.refs_0_), channel_id=1, source_target_pairs={{0,3},{1,0},{2,1},{3,2},{4,7},{5,4},{6,5},{7,6},{8,11},{9,8},{10,9... | collective-permute-start | bytes 196616 | tf_op jit(solution)/shard_map/ppermute | solution.py:35
  82.9 22.1 %all-to-all-start.2 = ((f32[128,8,128]{2,1,0:T(8,128)}), f32[128,8,128]{2,1,0:T(8,128)}, u32[]{:S(2)}, u32[]{:S(2)}) async-start(f32[128,8,128]{2,1,0:T(8,128)} %broadcast_in_dim.42), calls=%async_computation.2 | async-start | bytes 1048576 | tf_op jit(solution)/shard_map/all_to_all | solution.py:453
  88.9 9.0 %collective-permute-start.5 = (bf16[1,256,256]{2,1,0:T(8,128)(2,1)S(1)}, bf16[1,256,256]{2,1,0:T(8,128)(2,1)S(1)}, u32[]{:S(2)}, u32[]{:S(2)}) collective-permute-start(bf16[1,256,256]{2,1,0:T(8,128)(2,1)S(1)} %get-tuple-element.26.refs_0_), channel_id=1, source_target_pairs={{0,32},{32,0},{64,96},{96,64},{1,33},{33,1},{65,97},{97,65},{2,34}... | collective-permute-start | bytes 393224 | tf_op jit(solution)/shard_map/ppermute | solution.py:40
  90.4 9.7 %collective-permute-start.6 = (bf16[1,256,256]{2,1,0:T(8,128)(2,1)S(1)}, bf16[1,256,256]{2,1,0:T(8,128)(2,1)S(1)}, u32[]{:S(2)}, u32[]{:S(2)}) collective-permute-start(bf16[1,256,256]{2,1,0:T(8,128)(2,1)S(1)} %get-tuple-element.27.refs_2_), channel_id=1, source_target_pairs={{0,8},{8,0},{16,24},{24,16},{1,9},{9,1},{17,25},{25,17},{2,10},{10... | collective-permute-start | bytes 393224 | tf_op jit(solution)/shard_map/ppermute | solution.py:40
  100.1 8.6 %collective-permute-start.7 = (bf16[2,256,256]{2,1,0:T(8,128)(2,1)S(1)}, bf16[2,256,256]{2,1,0:T(8,128)(2,1)S(1)}, u32[]{:S(2)}, u32[]{:S(2)}) collective-permute-start(bf16[2,256,256]{2,1,0:T(8,128)(2,1)S(1)} %get-tuple-element.28.refs_0_), channel_id=1, source_target_pairs={{0,96},{32,64},{64,32},{96,0},{1,97},{33,65},{65,33},{97,1},{2,98}... | collective-permute-start | bytes 786440 | tf_op jit(solution)/shard_map/ppermute | solution.py:40
  102.3 8.4 %collective-permute-start.8 = (bf16[2,256,256]{2,1,0:T(8,128)(2,1)S(1)}, bf16[2,256,256]{2,1,0:T(8,128)(2,1)S(1)}, u32[]{:S(2)}, u32[]{:S(2)}) collective-permute-start(bf16[2,256,256]{2,1,0:T(8,128)(2,1)S(1)} %get-tuple-element.31.refs_2_), channel_id=1, source_target_pairs={{0,24},{8,16},{16,8},{24,0},{1,25},{9,17},{17,9},{25,1},{2,26},{10... | collective-permute-start | bytes 786440 | tf_op jit(solution)/shard_map/ppermute | solution.py:40
  104.8 30.6 %copy-start.9 = (s32[256,63]{0,1:T(8,128)S(1)}, s32[256,63]{0,1:T(8,128)}, u32[]{:S(2)}) copy-start(s32[256,63]{0,1:T(8,128)} %param.23) | copy-start | bytes 193540
  111.0 5.1 %collective-permute-start.10 = (bf16[4,64,256]{2,1,0:T(8,128)(2,1)S(1)}, bf16[4,64,256]{2,1,0:T(8,128)(2,1)S(1)}, u32[]{:S(2)}, u32[]{:S(2)}) collective-permute-start(bf16[4,64,256]{2,1,0:T(8,128)(2,1)S(1)} %get-tuple-element.33.refs_2_), channel_id=1, source_target_pairs={{0,24},{8,16},{16,8},{24,0},{1,25},{9,17},{17,9},{25,1},{2,26},{10... | collective-permute-start | bytes 393224 | tf_op jit(solution)/shard_map/ppermute | solution.py:40
  113.3 4.1 %collective-permute-start.11 = (bf16[4,64,256]{2,1,0:T(8,128)(2,1)S(1)}, bf16[4,64,256]{2,1,0:T(8,128)(2,1)S(1)}, u32[]{:S(2)}, u32[]{:S(2)}) collective-permute-start(bf16[4,64,256]{2,1,0:T(8,128)(2,1)S(1)} %get-tuple-element.34.refs_4_), channel_id=1, source_target_pairs={{0,32},{32,0},{64,96},{96,64},{1,33},{33,1},{65,97},{97,65},{2,34}... | collective-permute-start | bytes 393224 | tf_op jit(solution)/shard_map/ppermute | solution.py:40
  113.3 5.1 %collective-permute-start.12 = (bf16[4,64,256]{2,1,0:T(8,128)(2,1)S(1)}, bf16[4,64,256]{2,1,0:T(8,128)(2,1)S(1)}, u32[]{:S(2)}, u32[]{:S(2)}) collective-permute-start(bf16[4,64,256]{2,1,0:T(8,128)(2,1)S(1)} %get-tuple-element.35.refs_6_), channel_id=1, source_target_pairs={{0,96},{32,64},{64,32},{96,0},{1,97},{33,65},{65,33},{97,1},{2,98}... | collective-permute-start | bytes 393224 | tf_op jit(solution)/shard_map/ppermute | solution.py:40
  114.1 4.3 %collective-permute-start.9 = (bf16[4,64,256]{2,1,0:T(8,128)(2,1)S(1)}, bf16[4,64,256]{2,1,0:T(8,128)(2,1)S(1)}, u32[]{:S(2)}, u32[]{:S(2)}) collective-permute-start(bf16[4,64,256]{2,1,0:T(8,128)(2,1)S(1)} %get-tuple-element.32.refs_0_), channel_id=1, source_target_pairs={{0,8},{8,0},{16,24},{24,16},{1,9},{9,1},{17,25},{25,17},{2,10},{10... | collective-permute-start | bytes 393224 | tf_op jit(solution)/shard_map/ppermute | solution.py:40
  119.6 15.9 %collective-permute-start.13 = (bf16[4,8,64,256]{3,2,1,0:T(8,128)(2,1)}, bf16[4,8,64,256]{3,2,1,0:T(8,128)(2,1)S(1)}, u32[]{:S(2)}, u32[]{:S(2)}) collective-permute-start(bf16[4,8,64,256]{3,2,1,0:T(8,128)(2,1)} %get-tuple-element.40), channel_id=1, source_target_pairs={{0,4},{4,0},{1,5},{5,1},{2,6},{6,2},{3,7},{7,3},{8,12},{12,8},{9,1... | collective-permute-start | bytes 3145736 | tf_op jit(solution)/shard_map/ppermute | solution.py:35
  122.8 9.3 %collective-permute-start.14 = (bf16[8,64,256]{2,1,0:T(8,128)(2,1)S(1)}, bf16[8,64,256]{2,1,0:T(8,128)(2,1)}, u32[]{:S(2)}, u32[]{:S(2)}) collective-permute-start(bf16[8,64,256]{2,1,0:T(8,128)(2,1)S(1)} %get-tuple-element.36.refs_0_), channel_id=1, source_target_pairs={{0,24},{8,16},{16,8},{24,0},{1,25},{9,17},{17,9},{25,1},{2,26},{10... | collective-permute-start | bytes 786440 | tf_op jit(solution)/shard_map/ppermute | solution.py:40
  123.3 9.5 %collective-permute-start.15 = (bf16[8,64,256]{2,1,0:T(8,128)(2,1)S(1)}, bf16[8,64,256]{2,1,0:T(8,128)(2,1)}, u32[]{:S(2)}, u32[]{:S(2)}) collective-permute-start(bf16[8,64,256]{2,1,0:T(8,128)(2,1)S(1)} %get-tuple-element.37.refs_1_), channel_id=1, source_target_pairs={{0,8},{8,0},{16,24},{24,16},{1,9},{9,1},{17,25},{25,17},{2,10},{10... | collective-permute-start | bytes 786440 | tf_op jit(solution)/shard_map/ppermute | solution.py:40
  123.3 9.5 %collective-permute-start.16 = (bf16[8,64,256]{2,1,0:T(8,128)(2,1)S(1)}, bf16[8,64,256]{2,1,0:T(8,128)(2,1)}, u32[]{:S(2)}, u32[]{:S(2)}) collective-permute-start(bf16[8,64,256]{2,1,0:T(8,128)(2,1)S(1)} %get-tuple-element.38.refs_2_), channel_id=1, source_target_pairs={{0,96},{32,64},{64,32},{96,0},{1,97},{33,65},{65,33},{97,1},{2,98}... | collective-permute-start | bytes 786440 | tf_op jit(solution)/shard_map/ppermute | solution.py:40
  125.1 8.3 %collective-permute-start.17 = (bf16[8,64,256]{2,1,0:T(8,128)(2,1)S(1)}, bf16[8,64,256]{2,1,0:T(8,128)(2,1)}, u32[]{:S(2)}, u32[]{:S(2)}) collective-permute-start(bf16[8,64,256]{2,1,0:T(8,128)(2,1)S(1)} %get-tuple-element.39.refs_3_), channel_id=1, source_target_pairs={{0,32},{32,0},{64,96},{96,64},{1,33},{33,1},{65,97},{97,65},{2,34}... | collective-permute-start | bytes 786440 | tf_op jit(solution)/shard_map/ppermute | solution.py:40
  125.2 0.7 copy-start.7
  132.0 2.3 %collective-permute-start.18 = (bf16[8,64,256]{2,1,0:T(8,128)(2,1)}, bf16[8,64,256]{2,1,0:T(8,128)(2,1)}, u32[]{:S(2)}, u32[]{:S(2)}) collective-permute-start(bf16[8,64,256]{2,1,0:T(8,128)(2,1)} %collective-permute-done.14.refs_5_), channel_id=1, source_target_pairs={{0,4},{4,0},{1,5},{5,1},{2,6},{6,2},{3,7},{7,3},{8,12},{12,8},{9,1... | collective-permute-start | bytes 786440 | tf_op jit(solution)/shard_map/ppermute | solution.py:35
  132.8 1.9 %collective-permute-start.19 = (bf16[8,64,256]{2,1,0:T(8,128)(2,1)}, bf16[8,64,256]{2,1,0:T(8,128)(2,1)}, u32[]{:S(2)}, u32[]{:S(2)}) collective-permute-start(bf16[8,64,256]{2,1,0:T(8,128)(2,1)} %collective-permute-done.15.refs_6_), channel_id=1, source_target_pairs={{0,4},{4,0},{1,5},{5,1},{2,6},{6,2},{3,7},{7,3},{8,12},{12,8},{9,1... | collective-permute-start | bytes 786440 | tf_op jit(solution)/shard_map/ppermute | solution.py:35
  132.8 2.2 %collective-permute-start.20 = (bf16[8,64,256]{2,1,0:T(8,128)(2,1)}, bf16[8,64,256]{2,1,0:T(8,128)(2,1)}, u32[]{:S(2)}, u32[]{:S(2)}) collective-permute-start(bf16[8,64,256]{2,1,0:T(8,128)(2,1)} %collective-permute-done.16.refs_7_), channel_id=1, source_target_pairs={{0,4},{4,0},{1,5},{5,1},{2,6},{6,2},{3,7},{7,3},{8,12},{12,8},{9,1... | collective-permute-start | bytes 786440 | tf_op jit(solution)/shard_map/ppermute | solution.py:35
  133.4 2.0 %collective-permute-start.21 = (bf16[8,64,256]{2,1,0:T(8,128)(2,1)}, bf16[8,64,256]{2,1,0:T(8,128)(2,1)}, u32[]{:S(2)}, u32[]{:S(2)}) collective-permute-start(bf16[8,64,256]{2,1,0:T(8,128)(2,1)} %collective-permute-done.17.refs_8_), channel_id=1, source_target_pairs={{0,4},{4,0},{1,5},{5,1},{2,6},{6,2},{3,7},{7,3},{8,12},{12,8},{9,1... | collective-permute-start | bytes 786440 | tf_op jit(solution)/shard_map/ppermute | solution.py:35
  135.4 1.0 copy-start.8
  146.6 1.0 copy-start.6
